TPU v7x, 256 devices: a whole 4x4x8 slice. The times are simulated.
256 devices in a mesh: dp: 8 (over z), seq: 32 (over x, y, core).
Axes of the slice: x: 4, y: 4, z: 8, core: 2. Of those that a mesh axis runs over, the one named last changes fastest.
Arguments:
- x_rows: bfloat16 [8, 4096, 1024], P('dp', 'seq'), may hold values from -6 to 6
- lengths: int32 [8, 8], P('dp'), may hold values from 1 to 2048, 4096 in all within a row
- targets: int32 [8, 8], P('dp'), may hold values from 1 to 64
- w_in: bfloat16 [1024, 2048], replicated, may hold values from -0.1875 to 0.1875
- w_out: bfloat16 [512, 1024], replicated, may hold values from -0.25 to 0.25
- w_score: bfloat16 [1024, 256], replicated, may hold values from -0.1875 to 0.1875
- head_score: float32 [256], replicated, may hold values from -0.375 to 0.375
- grad_out: bfloat16 [8, 4096, 1024], P('dp', 'seq'), may hold values from -6 to 6
- grad_score: float32 [8, 4096], P('dp', 'seq'), may hold values from -6 to 6
Outputs:
- d_x: bfloat16 [8, 4096, 1024], P('dp', 'seq')
- d_w_in: float32 [1024, 2048], P('seq', 'dp')
- d_w_out: float32 [512, 1024], P('seq', 'dp')
- d_w_score: float32 [1024, 256], P('seq', 'dp')
- d_head: float32 [256], replicated
Inputs may be any that keep to these rules, and one draw needn't show every extreme that they name: Each row lists the lengths of 8 histories packed end to end in the 4096 positions of a group; they sum to 4096 and the largest is 2048.
All inputs are finite; a program needn't handle non-finite values.
Results may differ from a plain program's by a relative error of at most 0.0084.
Values may be sent and summed in bfloat16 or wider, within the bound.
No kernel may reach another device: no remote copies, remote signals or barrier semaphores. Data moves between devices by JAX's collectives and lax.ppermute only.
A program may use at most 64 MiB of HBM per device.

v0:
```python
import functools

import jax
import jax.numpy as jnp
from jax import lax
from jax.experimental import pallas as pl
from jax.experimental.pallas import tpu as pltpu
from jax.sharding import Mesh
from jax.sharding import PartitionSpec as P

HEADS = 4
DH = 128
ROWS = 128
HIST = 8
TOKENS = 4096
DIVISOR = 2048.0
TILE = 256
PAIR = 4
NORM_EPS = 1e-05
SEQ = ("x", "y", "core")

f32 = jnp.float32
bf16 = jnp.bfloat16
VMEM = pl.BlockSpec(memory_space=pltpu.VMEM)
SMEM = pl.BlockSpec(memory_space=pltpu.SMEM)
HBM = pl.BlockSpec(memory_space=pltpu.HBM)
PARAMS = pltpu.CompilerParams(vmem_limit_bytes=16 * 1024 * 1024)


def cost(us):
    return pl.CostEstimate(flops=int(us * 1.15e9), bytes_accessed=0, transcendentals=0)


def shape(dims, kind):
    return jax.ShapeDtypeStruct(dims, kind)


def dot(a, b):
    return lax.dot_general(a, b, (((1,), (0,)), ((), ())), preferred_element_type=f32)


def dot_t(a, b):
    return lax.dot_general(a, b, (((1,), (1,)), ((), ())), preferred_element_type=f32)


def sigmoid(value):
    return 0.5 + 0.5 * jnp.tanh(0.5 * value)


def silu_slope(value):
    sigma = sigmoid(value)
    return sigma * (1.0 + value * (1.0 - sigma))


def norm_rows(value):
    centre = value - jnp.mean(value, axis=-1, keepdims=True)
    inverse = lax.rsqrt(jnp.mean(centre * centre, axis=-1, keepdims=True) + NORM_EPS)
    return centre * inverse, inverse


def norm_back(grad, normed, inverse):
    return inverse * (
        grad
        - jnp.mean(grad, axis=-1, keepdims=True)
        - normed * jnp.mean(grad * normed, axis=-1, keepdims=True)
    )


class Histories:
    def __init__(self, len_ref, tgt_ref):
        self.starts, self.ends, self.firsts = [], [], []
        total = jnp.int32(0)
        for h in range(HIST):
            length = len_ref[h]
            self.starts.append(total)
            total = total + length
            self.ends.append(total)
            self.firsts.append(total - jnp.minimum(tgt_ref[h], length - 1))

    def pick(self, values, pos):
        out = jnp.where(pos >= self.starts[1], values[1], values[0])
        for h in range(2, HIST):
            out = jnp.where(pos >= self.starts[h], values[h], out)
        return out

    def range_of(self, pos):
        return self.pick(self.starts, pos), jnp.minimum(self.pick(self.firsts, pos), pos + 1)


def copy_all(copies):
    for copy in copies:
        copy.start()
    return copies


def project_kernel(x_hbm, w_hbm, normed_ref, o0, o1, o2, o3, x_ref, w_ref, sems):
    width = HEADS * DH
    copies = copy_all(
        [pltpu.make_async_copy(x_hbm, x_ref, sems.at[3])]
        + [
            pltpu.make_async_copy(w_hbm.at[:, pl.ds(kind * width, width)], w_ref.at[i], sems.at[i])
            for i, kind in enumerate((3, 1, 2))
        ]
    )
    copies[0].wait()
    value, _ = norm_rows(x_ref[...].astype(f32))
    normed = value.astype(bf16)
    normed_ref[...] = normed
    for i in range(3):
        copies[i + 1].wait()
        pre = dot(normed, w_ref[i])
        hidden = (pre * sigmoid(pre)).astype(bf16)
        for h in range(HEADS):
            away = lax.rem(h - lax.axis_index("x") + HEADS, HEADS)
            for k, ref in enumerate((o0, o1, o2, o3)):

                @pl.when(away == k)
                def _(ref=ref, h=h):
                    ref[:, i * DH : (i + 1) * DH] = hidden[:, h * DH : (h + 1) * DH]


def project(x, w_in):
    out = pl.pallas_call(
        project_kernel,
        in_specs=[HBM, HBM],
        out_specs=[VMEM] * 5,
        out_shape=[shape((ROWS, 1024), bf16)] + [shape((ROWS, 3 * DH), bf16)] * 4,
        scratch_shapes=[
            pltpu.VMEM((ROWS, 1024), bf16),
            pltpu.VMEM((3, 1024, HEADS * DH), bf16),
            pltpu.SemaphoreType.DMA((4,)),
        ],
        compiler_params=pltpu.CompilerParams(vmem_limit_bytes=60 * 1024 * 1024),
        cost_estimate=cost(3),
        name="project",
    )(x, w_in)
    return out[0], out[1:5]


def gates_kernel(normed_ref, w_hbm, gate_ref, slope_ref, w_ref, sem):
    copy = pltpu.make_async_copy(w_hbm.at[:, pl.ds(0, HEADS * DH)], w_ref, sem)
    copy.start()
    copy.wait()
    pre = dot(normed_ref[...], w_ref[...])
    sigma = sigmoid(pre)
    gate_ref[...] = (pre * sigma).astype(bf16)
    slope_ref[...] = sigma * (1.0 + pre * (1.0 - sigma))


def gates(normed, w_in):
    width = HEADS * DH
    return pl.pallas_call(
        gates_kernel,
        in_specs=[VMEM, HBM],
        out_specs=[VMEM] * 2,
        out_shape=[shape((ROWS, width), bf16), shape((ROWS, width), f32)],
        scratch_shapes=[pltpu.VMEM((1024, width), bf16), pltpu.SemaphoreType.DMA],
        compiler_params=PARAMS,
        cost_estimate=cost(0.2),
        name="gates",
    )(normed, w_in)


def slopes_kernel(idx, n0, n1, n2, n3, w_hbm, out_ref, w_ref, sems):
    copies = []
    for i, kind in enumerate((2, 3, 1)):
        at = pl.ds(pl.multiple_of((kind * HEADS + idx[0]) * DH, DH), DH)
        copies.append(pltpu.make_async_copy(w_hbm.at[:, at], w_ref.at[i], sems.at[i]))
    copy_all(copies)
    for i in range(3):
        copies[i].wait()
        for k, ref in enumerate((n0, n1, n2, n3)):
            out_ref[k, :, i * DH : (i + 1) * DH] = silu_slope(dot(ref[...], w_ref[i]))


def slopes(idx, normed, w_in):
    return pl.pallas_call(
        slopes_kernel,
        in_specs=[SMEM] + [VMEM] * 4 + [HBM],
        out_specs=VMEM,
        out_shape=shape((4, ROWS, 3 * DH), f32),
        scratch_shapes=[pltpu.VMEM((3, 1024, DH), bf16), pltpu.SemaphoreType.DMA((3,))],
        compiler_params=PARAMS,
        cost_estimate=cost(0.5),
        name="slopes",
    )(idx, *normed, w_in)


def block_of(idx, k):
    return lax.rem(idx[0] - k + 4, 4) * 8 + idx[1] * 2 + idx[2]


WHOLE = [(j % 4, j // 4, 0, 4) for j in range(8)]
NEAR = [(0, 0, 0, 4), (1, 0, 0, 4), (3, 0, 0, 4), (0, 1, 0, 4), (1, 1, 0, 4), (3, 1, 0, 4)]


def assemble(idx, pieces, places, outs):
    for piece, (back, other, first, count) in zip(pieces, places, strict=True):
        at_y = lax.rem(idx[1] - back + 4, 4)
        at_core = 1 - idx[2] if other else idx[2]
        for i in range(count):
            block = lax.rem(idx[0] - first - i + 4, 4) * 8 + at_y * 2 + at_core
            where = pl.ds(pl.multiple_of(block * ROWS, ROWS), ROWS)
            for ref, column in outs:
                ref[where, :] = piece[i, :, column : column + DH]


def for_items(lows, highs, body):
    ends, total = [], jnp.int32(0)
    for low, high in zip(lows, highs, strict=True):
        total = total + (high - low + 1)
        ends.append(total)

    def step(i, carry):
        for j in range(PAIR):
            n = i * PAIR + j
            k, t = jnp.int32(0), n + lows[0]
            for q in range(1, 4):
                k = jnp.where(n >= ends[q - 1], q, k)
                t = jnp.where(n >= ends[q - 1], n - ends[q - 1] + lows[q], t)
            body(k, t, n < total)
        return carry

    lax.fori_loop(0, (total + PAIR - 1) // PAIR, step, 0)


def tile_at(t):
    return pl.ds(pl.multiple_of(jnp.minimum(t, TOKENS // TILE - 1) * TILE, TILE), TILE)


def set_marks(idx, hist, marks):
    row = lax.broadcasted_iota(jnp.int32, (ROWS, 128), 0)
    lows, highs = [], []
    for k in range(4):
        first = block_of(idx, k) * ROWS
        start, limit = hist.range_of(first + row)
        marks[0, k], marks[1, k] = start, limit
        lows.append(hist.pick(hist.starts, first) // TILE)
        highs.append(first // TILE)
    return lows, highs


def seen_by(idx, marks, k, t):
    row = lax.broadcasted_iota(jnp.int32, (ROWS, TILE), 0)
    lane = lax.broadcasted_iota(jnp.int32, (ROWS, TILE), 1)
    key = lane + t * TILE
    start, limit = [jnp.concatenate([marks[i, k]] * (TILE // 128), axis=1) for i in range(2)]
    return ((key >= start) & (key < limit)) | (key - row == block_of(idx, k) * ROWS)


def attend(idx, marks, q_own, total, k, t, keys, values):
    half = dot_t(q_own[k], keys) * (0.5 * DH**-0.5)
    weight = half * (1.0 + jnp.tanh(half))
    weight = jnp.where(seen_by(idx, marks, k, t), weight, 0.0).astype(bf16)
    total[k] += dot(weight, values)


def near_kernel(idx, len_ref, tgt_ref, *refs):
    pieces, out, all_hbm = refs[0:6], refs[6], refs[7:10]
    k_all, v_all, q_all, q_own, marks, sems = refs[10:16]
    hist = Histories(len_ref, tgt_ref)
    for x in range(4):
        at = pl.ds(pl.multiple_of((x * 4 + lax.rem(idx[1] + 2, 4)) * TILE, TILE), TILE)
        for ref in (k_all, v_all, q_all):
            ref[at, :] = jnp.zeros((TILE, DH), bf16)
    assemble(idx, pieces, NEAR, [(k_all, 0), (v_all, DH), (q_all, 2 * DH)])
    copies = copy_all(
        [
            pltpu.make_async_copy(ref, all_hbm[i], sems.at[i])
            for i, ref in enumerate((k_all, v_all, q_all))
        ]
    )
    for k in range(4):
        q_own[k] = pieces[0][k, :, 2 * DH : 3 * DH]
    out[...] = jnp.zeros_like(out)
    lows, highs = set_marks(idx, hist, marks)
    base = 3 - lax.rem(idx[1] + 2, 4)
    lows = [(low + base) // 4 * 3 + jnp.minimum((low + base) % 4, 3) for low in lows]
    highs = [(high + base) // 4 * 3 + jnp.minimum((high + base) % 4, 2) for high in highs]

    def body(k, u, valid):
        t = u + u // 3 - base
        at = tile_at(t)
        attend(idx, marks, q_own, out, k, t, k_all[at, :], v_all[at, :])

    for_items(lows, highs, body)
    for copy in copies:
        copy.wait()


def attend_near(idx, lengths, targets, pieces):
    return pl.pallas_call(
        near_kernel,
        in_specs=[SMEM] * 3 + [VMEM] * 6,
        out_specs=[VMEM] + [HBM] * 3,
        out_shape=[shape((4, ROWS, DH), f32)] + [shape((TOKENS, DH), bf16)] * 3,
        scratch_shapes=[pltpu.VMEM((TOKENS, DH), bf16)] * 3
        + [
            pltpu.VMEM((4, ROWS, DH), bf16),
            pltpu.VMEM((2, 4, ROWS, 128), jnp.int32),
            pltpu.SemaphoreType.DMA((3,)),
        ],
        compiler_params=PARAMS,
        cost_estimate=cost(0.5),
        name="attend_near",
    )(idx, lengths, targets, *pieces)


def far_kernel(idx, len_ref, tgt_ref, *refs):
    held, pieces, near, o_refs, all_hbm = refs[0], refs[1:5], refs[5], refs[9:13], refs[13:16]
    k_far, v_far, q_far, q_own, total, marks, sems = refs[16:23]
    hist = Histories(len_ref, tgt_ref)
    far = lax.rem(idx[1] + 2, 4)
    for j in range(4):
        other, first = j // 2, j % 2 * 2
        at_core = 1 - idx[2] if other else idx[2]
        for i in range(2):
            x = lax.rem(idx[0] - first - i + 4, 4)
            where = pl.ds(pl.multiple_of(x * TILE + at_core * ROWS, ROWS), ROWS)
            for n, ref in enumerate((k_far, v_far, q_far)):
                ref[where, :] = pieces[j][i, :, n * DH : (n + 1) * DH]
    copies = []
    for x in range(4):
        at = pl.ds(pl.multiple_of((x * 4 + far) * TILE, TILE), TILE)
        for n, ref in enumerate((k_far, v_far, q_far)):
            tile = ref.at[x * TILE : (x + 1) * TILE, :]
            copies.append(pltpu.make_async_copy(tile, all_hbm[n].at[at, :], sems.at[x * 3 + n]))
    copy_all(copies)
    for k in range(4):
        q_own[k] = held[k, :, 2 * DH : 3 * DH]
    total[...] = near[...]
    lows, highs = set_marks(idx, hist, marks)
    lows = [(low - far + 3) // 4 for low in lows]
    highs = [(high - far + 4) // 4 - 1 for high in highs]

    def body(k, u, valid):
        at = pl.ds(pl.multiple_of(jnp.minimum(u, 3) * TILE, TILE), TILE)
        attend(idx, marks, q_own, total, k, u * 4 + far, k_far[at, :], v_far[at, :])

    for_items(lows, highs, body)
    for k in range(4):
        o_refs[k][...] = total[k] * (1.0 / DIVISOR)
    for copy in copies:
        copy.wait()


def attend_far(idx, lengths, targets, held, pieces, near, everything):
    return pl.pallas_call(
        far_kernel,
        in_specs=[SMEM] * 3 + [VMEM] * 6 + [HBM] * 3,
        out_specs=[VMEM] * 4 + [HBM] * 3,
        out_shape=[shape((ROWS, DH), f32)] * 4 + [shape((TOKENS, DH), bf16)] * 3,
        input_output_aliases={9: 4, 10: 5, 11: 6},
        scratch_shapes=[pltpu.VMEM((4 * TILE, DH), bf16)] * 3
        + [
            pltpu.VMEM((4, ROWS, DH), bf16),
            pltpu.VMEM((4, ROWS, DH), f32),
            pltpu.VMEM((2, 4, ROWS, 128), jnp.int32),
            pltpu.SemaphoreType.DMA((12,)),
        ],
        compiler_params=PARAMS,
        cost_estimate=cost(0.5),
        name="attend_far",
    )(idx, lengths, targets, held, *pieces, near, *everything)


def two_of(head):
    high = head.astype(bf16).astype(f32)
    return high, (head - high).astype(bf16).astype(f32)


def with_head(rows, head, count):
    high, low = two_of(head)
    width = ACTS if rows is None else rows.shape[1]
    line = jnp.concatenate([high, low, jnp.zeros((1, width - 512), f32)], axis=1)
    line = jnp.concatenate([line, jnp.zeros((count - 1, width), f32)], axis=0)
    return (line if rows is None else jnp.concatenate([rows, line], axis=0)).astype(bf16)


def head_of(value, row):
    return value[row : row + 1, 0:256] + value[row : row + 1, 256:512]


ACTS = 512 + 1024 + 1024 + 256


def middle_kernel(idx, len_ref, tgt_ref, a0, a1, a2, a3, gate_ref, slope_ref, x_ref, w_out, w_score, head, grad, score, *refs):
    d_refs, g_full, acts, mid_ref = refs[0:4], refs[4], refs[5], refs[6]
    att, work = refs[7:9]
    for k, ref in enumerate((a0, a1, a2, a3)):
        at = pl.ds(pl.multiple_of(lax.rem(idx[0] + k, 4) * DH, DH), DH)
        att[:, at] = ref[...]
    onorm, inverse = norm_rows(att[...])
    gate = gate_ref[...].astype(f32)
    gated = (onorm * gate).astype(bf16)
    acts[0:ROWS, 0:512] = gated
    out_b = (x_ref[...].astype(f32) + dot(gated, w_out[...])).astype(bf16)
    acts[0:ROWS, 1536:2560] = out_b
    mid = dot(out_b, w_score[...])
    hist = Histories(len_ref, tgt_ref)
    own = ((idx[0] * 4 + idx[1]) * 2 + idx[2]) * ROWS
    pos = own + lax.broadcasted_iota(jnp.int32, (ROWS, 1), 0)
    diagonal = lax.broadcasted_iota(jnp.int32, (ROWS, ROWS), 0) == lax.broadcasted_iota(
        jnp.int32, (ROWS, ROWS), 1
    )
    column = jnp.sum(jnp.where(diagonal, score[...], 0.0), axis=1, keepdims=True)
    weight = jnp.where(pos >= hist.pick(hist.firsts, pos), column, 0.0)
    sigma = sigmoid(mid)
    head_part = jnp.sum(weight * (mid * sigma), axis=0, keepdims=True)
    acts[ROWS : ROWS + 16, :] = with_head(None, head_part, 16)
    d_mid = (weight * head[...] * (sigma * (1.0 + mid * (1.0 - sigma)))).astype(bf16)
    acts[0:ROWS, 2560:2816] = d_mid
    mid_ref[...] = d_mid
    total_b = (grad[...].astype(f32) + dot_t(d_mid, w_score[...])).astype(bf16)
    acts[0:ROWS, 512:1536] = total_b
    d_gated = dot_t(total_b, w_out[...])
    att[...] = norm_back(d_gated * gate, onorm, inverse)
    work[...] = d_gated * onorm * slope_ref[...]
    g_full[...] = work[...].astype(bf16)
    for k in range(4):
        at = pl.ds(pl.multiple_of(lax.rem(idx[0] + k, 4) * DH, DH), DH)
        d_refs[k][:, 0:DH] = att[:, at].astype(bf16)
        d_refs[k][:, DH : 2 * DH] = work[:, at].astype(bf16)


def middle(idx, lengths, targets, attended, gate, slope, x, w_out, w_score, head, grad, score):
    width = HEADS * DH
    return pl.pallas_call(
        middle_kernel,
        in_specs=[SMEM] * 3 + [VMEM] * 12,
        out_specs=[VMEM] * 7,
        out_shape=[shape((ROWS, 2 * DH), bf16)] * 4
        + [
            shape((ROWS, width), bf16),
            shape((ROWS + 16, ACTS), bf16),
            shape((ROWS, 256), bf16),
        ],
        scratch_shapes=[pltpu.VMEM((ROWS, width), f32)] * 2,
        compiler_params=PARAMS,
        cost_estimate=cost(0.5),
        name="middle",
    )(idx, lengths, targets, *attended, gate, slope, x, w_out, w_score, head, grad, score)


SLOPE_SCALE = 0.5 * 2**-0.5
SLOPE_REST = DH**-0.5 / DIVISOR / 2**-0.5


def query_kernel(idx, len_ref, tgt_ref, *refs):
    held, d_refs, (k_hbm, v_hbm), out_refs = refs[0], refs[1:5], refs[5:7], refs[7:11]
    k_all, v_all, q_own, d_own, total, marks, sems = refs[11:18]
    copies = copy_all(
        [
            pltpu.make_async_copy(k_hbm, k_all, sems.at[0]),
            pltpu.make_async_copy(v_hbm, v_all, sems.at[1]),
        ]
    )
    hist = Histories(len_ref, tgt_ref)
    for k in range(4):
        q_own[k] = held[k, :, 2 * DH : 3 * DH]
        d_own[k] = d_refs[k][:, 0:DH]
    total[...] = jnp.zeros_like(total)
    lows, highs = set_marks(idx, hist, marks)
    for copy in copies:
        copy.wait()

    def body(k, t, valid):
        at = tile_at(t)
        keys = k_all[at, :]
        half = dot_t(q_own[k], keys) * (0.5 * DH**-0.5)
        d_attn = dot_t(d_own[k], v_all[at, :])
        tanh = jnp.tanh(half)
        factor = (SLOPE_SCALE + SLOPE_SCALE * tanh) * (1.0 + half * (1.0 - tanh))
        d_raw = jnp.where(seen_by(idx, marks, k, t), d_attn * factor, 0.0).astype(bf16)
        total[k] += dot(d_raw, keys)

    for_items(lows, highs, body)
    for k in range(4):
        out_refs[k][...] = total[k] * SLOPE_REST


def query_grads(idx, lengths, targets, held, d_att, k_all, v_all):
    return pl.pallas_call(
        query_kernel,
        in_specs=[SMEM] * 3 + [VMEM] * 5 + [HBM] * 2,
        out_specs=[VMEM] * 4,
        out_shape=[shape((ROWS, DH), f32)] * 4,
        scratch_shapes=[pltpu.VMEM((TOKENS, DH), bf16)] * 2
        + [pltpu.VMEM((4, ROWS, DH), bf16)] * 2
        + [
            pltpu.VMEM((4, ROWS, DH), f32),
            pltpu.VMEM((2, 4, ROWS, 128), jnp.int32),
            pltpu.SemaphoreType.DMA((2,)),
        ],
        compiler_params=PARAMS,
        cost_estimate=cost(3),
        name="query_grads",
    )(idx, lengths, targets, held, *d_att, k_all, v_all)


def key_kernel(idx, len_ref, tgt_ref, *refs):
    d_pieces, (k_hbm, v_hbm, q_hbm, slope_ref) = refs[0:8], refs[8:12]
    dq_refs, d_refs, back_refs, all_ref = refs[12:16], refs[16:20], refs[20:24], refs[24]
    q_all, d_all, k_own, v_own, d_key, d_value, sems = refs[25:32]
    copies = [pltpu.make_async_copy(q_hbm, q_all, sems.at[8])]
    for k in range(4):
        at = pl.ds(pl.multiple_of(block_of(idx, k) * ROWS, ROWS), ROWS)
        copies.append(pltpu.make_async_copy(k_hbm.at[at, :], k_own.at[k], sems.at[k]))
        copies.append(pltpu.make_async_copy(v_hbm.at[at, :], v_own.at[k], sems.at[k + 4]))
    copy_all(copies)
    hist = Histories(len_ref, tgt_ref)
    assemble(idx, d_pieces, WHOLE, [(d_all, 0)])
    d_key[...] = jnp.zeros_like(d_key)
    d_value[...] = jnp.zeros_like(d_value)
    row = lax.broadcasted_iota(jnp.int32, (ROWS, TILE), 0)
    lane = lax.broadcasted_iota(jnp.int32, (1, TILE), 1)
    lows, highs = [], []
    for k in range(4):
        first = block_of(idx, k) * ROWS
        lows.append(first // TILE)
        highs.append((hist.pick(hist.ends, first + ROWS - 1) - 1) // TILE)
    for copy in copies:
        copy.wait()

    def body(k, t, valid):
        at = tile_at(t)
        queries, d_att = q_all[at, :], d_all[at, :]
        half = dot_t(k_own[k], queries) * (0.5 * DH**-0.5)
        d_attn = dot_t(v_own[k], d_att)
        key = block_of(idx, k) * ROWS + row
        pos = lane + t * TILE
        start, limit = hist.range_of(pos)
        start = start + jnp.where(valid, 0, TOKENS)
        seen = ((key >= start) & (key < limit)) | (key == pos)
        tanh = jnp.tanh(half)
        more = 1.0 + tanh
        weight = jnp.where(seen, half * more, 0.0).astype(bf16)
        factor = (SLOPE_SCALE * more) * (1.0 + half * (1.0 - tanh))
        d_raw = jnp.where(seen, d_attn * factor, 0.0).astype(bf16)
        d_key[k] += dot(d_raw, queries)
        d_value[k] += dot(weight, d_att)

    for_items(lows, highs, body)
    for k in range(4):
        d_q = (dq_refs[k][...] * slope_ref[k, :, 0:DH]).astype(bf16)
        d_k = (d_key[k] * SLOPE_REST * slope_ref[k, :, DH : 2 * DH]).astype(bf16)
        d_v = (d_value[k] * (1.0 / DIVISOR) * slope_ref[k, :, 2 * DH : 3 * DH]).astype(bf16)
        back_refs[k][:, 0:DH] = d_v
        back_refs[k][:, DH : 2 * DH] = d_q
        back_refs[k][:, 2 * DH : 3 * DH] = d_k
        at = pl.ds(k * ROWS, ROWS)
        all_ref[at, 0:DH] = d_refs[k][:, DH : 2 * DH]
        all_ref[at, DH : 2 * DH] = d_v
        all_ref[at, 2 * DH : 3 * DH] = d_q
        all_ref[at, 3 * DH : 4 * DH] = d_k


def key_grads(idx, lengths, targets, d_pieces, everything, slope, d_query, d_att):
    return pl.pallas_call(
        key_kernel,
        in_specs=[SMEM] * 3 + [VMEM] * 8 + [HBM] * 3 + [VMEM] * 9,
        out_specs=[VMEM] * 5,
        out_shape=[shape((ROWS, 3 * DH), bf16)] * 4 + [shape((4 * ROWS, 4 * DH), bf16)],
        scratch_shapes=[pltpu.VMEM((TOKENS, DH), bf16)] * 2
        + [pltpu.VMEM((4, ROWS, DH), bf16)] * 2
        + [pltpu.VMEM((4, ROWS, DH), f32)] * 2
        + [pltpu.SemaphoreType.DMA((9,))],
        compiler_params=PARAMS,
        cost_estimate=cost(0.02),
        name="key_grads",
    )(idx, lengths, targets, *d_pieces, *everything, slope, *d_query, *d_att)


def dot_first(a, b):
    return lax.dot_general(a, b, (((0,), (0,)), ((), ())), preferred_element_type=f32)


def parts_kernel(idx, own, got, out, rows):
    rows[0:ROWS, :] = own[0:ROWS, :]
    rows[ROWS : 2 * ROWS, :] = got[0:ROWS, :]
    total = rows[:, pl.ds(pl.multiple_of(512 + idx[2] * 512, 512), 512)]
    d_mid = rows[:, pl.ds(pl.multiple_of(2560 + idx[2] * 128, 128), 128)]
    head = [head_of(ref[ROWS : ROWS + 16, 0:512].astype(f32), 0) for ref in (own, got)]
    high, low = two_of(head[0] + head[1])
    line = jnp.concatenate([high, low], axis=1)
    line = jnp.concatenate([line, jnp.zeros((7, 512), f32)], axis=0)
    for x in range(4):
        part = dot_first(rows[:, x * 128 : (x + 1) * 128], total)
        score = dot_first(rows[:, 1536 + x * 256 : 1792 + x * 256], d_mid)
        for m in range(8):
            last = [score[m * 32 + j * 8 : m * 32 + (j + 1) * 8] for j in range(4)]
            block = [part[m * 16 : (m + 1) * 16], jnp.concatenate(last, axis=1), line]
            out[x * 8 + m] = jnp.concatenate(block, axis=0).astype(bf16)


def parts(idx, own, got):
    return pl.pallas_call(
        parts_kernel,
        in_specs=[SMEM] + [VMEM] * 2,
        out_specs=VMEM,
        out_shape=shape((32, 32, 512), bf16),
        scratch_shapes=[pltpu.VMEM((2 * ROWS, ACTS), bf16)],
        compiler_params=PARAMS,
        cost_estimate=cost(0.3),
        name="parts",
    )(idx, own, got)


def weights_kernel(idx, n0, n1, n2, n3, d_pre, keep, send, left):
    for k, ref in enumerate((n0, n1, n2, n3)):
        left[k * ROWS : (k + 1) * ROWS, :] = ref[...]
    for n in range(4):
        part = dot_first(left[:, n * 256 : (n + 1) * 256], d_pre[...])
        for c in range(2):

            @pl.when(idx[2] == c)
            def _(c=c, n=n, part=part):
                for i in range(8):
                    rows = [part[i * 32 : i * 32 + 16], part[i * 32 + 16 : (i + 1) * 32]]
                    halves_of = [
                        jnp.concatenate([v[:, d * 256 : (d + 1) * 256] for v in rows], axis=1)
                        for d in (c, 1 - c)
                    ]
                    keep[n * 8 + i] = halves_of[0]
                    send[n * 8 + i] = halves_of[1].astype(bf16)


def weights(idx, normed, d_pre):
    return pl.pallas_call(
        weights_kernel,
        in_specs=[SMEM] + [VMEM] * 5,
        out_specs=[VMEM] * 2,
        out_shape=[shape((32, 16, 512), f32), shape((32, 16, 512), bf16)],
        scratch_shapes=[pltpu.VMEM((512, 1024), bf16)],
        compiler_params=PARAMS,
        cost_estimate=cost(0.02),
        name="weights",
    )(idx, *normed, d_pre)


def merge_kernel(keep, got, early, out):
    for n in range(32):
        out[n, 0:16, :] = (keep[n] + got[n].astype(f32)).astype(bf16)
        out[n, 16:48, :] = early[n]


def merge(keep, got, early):
    return pl.pallas_call(
        merge_kernel,
        in_specs=[VMEM] * 3,
        out_specs=VMEM,
        out_shape=shape((32, 48, 512), bf16),
        compiler_params=PARAMS,
        cost_estimate=cost(0.3),
        name="merge",
    )(keep, got, early)


def pack_kernel(ref, out_ref):
    for c in range(2):
        for h in range(HEADS):
            total = ref[h * 8 + c, 0:16, :].astype(f32)
            for n in range(1, 4):
                total = total + ref[h * 8 + n * 2 + c, 0:16, :].astype(f32)
            for i in range(2):
                z, half = divmod((c * 2 + i) * HEADS + h, 2)
                rows = [total[:, r * 256 + i * 128 : r * 256 + (i + 1) * 128] for r in range(2)]
                rows = jnp.concatenate(rows, axis=0).astype(bf16)
                out_ref[z, half * 32 : (half + 1) * 32, :] = rows
    sums = []
    for c in range(2):
        total = ref[c, 16:48, :].astype(f32)
        head = head_of(total, 24)
        for n in range(c + 2, 32, 2):
            part = ref[n, 16:48, :].astype(f32)
            total, head = total + part, head + head_of(part, 24)
        sums.append(total)
    high, low = two_of(head)
    head = [high[:, 0:128], high[:, 128:256], low[:, 0:128], low[:, 128:256]]
    head = jnp.concatenate(head + [jnp.zeros((4, 128), f32)], axis=0)
    for z in range(8):
        total, at = sums[z // 4], z % 4 * 128
        score = [total[16:24, j * 128 + z % 4 * 32 : j * 128 + z % 4 * 32 + 32] for j in range(4)]
        rows = [total[0:16, at : at + 128], jnp.concatenate(score, axis=1), head]
        out_ref[z, 64:96, :] = jnp.concatenate(rows, axis=0).astype(bf16)


def pack(value):
    return pl.pallas_call(
        pack_kernel,
        in_specs=[VMEM],
        out_specs=VMEM,
        out_shape=shape((8, 96, 128), bf16),
        compiler_params=PARAMS,
        cost_estimate=cost(0.3),
        name="pack",
    )(value)


def last_kernel(ref, in_ref, out_ref, score_ref, head_ref):
    total = ref[0].astype(f32)
    for z in range(1, 8):
        total = total + ref[z].astype(f32)
    in_ref[:, 0:128] = total[0:32]
    in_ref[:, 128:256] = total[32:64]
    out_ref[...] = total[64:80]
    for j in range(4):
        score_ref[j * 8 : (j + 1) * 8, :] = total[80:88, j * 32 : (j + 1) * 32]
    head_ref[:, 0:128] = total[88:89] + total[90:91]
    head_ref[:, 128:256] = total[89:90] + total[91:92]


def last_sum(value):
    return pl.pallas_call(
        last_kernel,
        in_specs=[VMEM],
        out_specs=[VMEM] * 4,
        out_shape=[
            shape((32, 256), f32),
            shape((16, 128), f32),
            shape((32, 32), f32),
            shape((1, 256), f32),
        ],
        compiler_params=PARAMS,
        cost_estimate=cost(0.3),
        name="last_sum",
    )(value)


def input_kernel(idx, b0, b1, b2, b3, gate_ref, w_ref, x_ref, grad, d_mid, w_score, out_ref, d_pre, d_norm):
    step = pl.program_id(0)
    width = HEADS * DH

    @pl.when(step == 0)
    def _():
        d_pre[:, 0:width] = gate_ref[...]
        for k, ref in enumerate((b0, b1, b2, b3)):
            head = lax.rem(idx[0] + k, 4)
            for kind in range(3):
                at = pl.ds(pl.multiple_of((kind + 1) * width + head * DH, DH), DH)
                d_pre[:, at] = ref[:, kind * DH : (kind + 1) * DH]

    d_norm[:, pl.ds(pl.multiple_of(step * 256, 256), 256)] = dot_t(d_pre[...], w_ref[...])

    @pl.when(step == 3)
    def _():
        normed, inverse = norm_rows(x_ref[...].astype(f32))
        d_total = grad[...].astype(f32) + dot_t(d_mid[...], w_score[...])
        out_ref[...] = (d_total + norm_back(d_norm[...], normed, inverse)).astype(bf16)


def input_grads(idx, back, gate, w_in, x, grad, d_mid, w_score):
    whole = lambda dims: pl.BlockSpec(dims, lambda i: (0, 0))
    return pl.pallas_call(
        input_kernel,
        grid=(4,),
        in_specs=[SMEM]
        + [whole((ROWS, 3 * DH))] * 4
        + [
            whole((ROWS, HEADS * DH)),
            pl.BlockSpec((256, 2048), lambda i: (i, 0)),
            whole((ROWS, 1024)),
            whole((ROWS, 1024)),
            whole((ROWS, 256)),
            whole((1024, 256)),
        ],
        out_specs=whole((ROWS, 1024)),
        out_shape=shape((ROWS, 1024), bf16),
        scratch_shapes=[pltpu.VMEM((ROWS, 2048), bf16), pltpu.VMEM((ROWS, 1024), f32)],
        compiler_params=PARAMS,
        cost_estimate=cost(1),
        name="input_grads",
    )(idx, *back, gate, w_in, x, grad, d_mid, w_score)


def join_kernel(*refs):
    for k in range(4):
        refs[4][k] = refs[k][:, 0 : refs[4].shape[2]]


def join(arrays, width):
    return pl.pallas_call(
        join_kernel,
        in_specs=[VMEM] * 4,
        out_specs=VMEM,
        out_shape=shape((4, ROWS, width), bf16),
        compiler_params=PARAMS,
        cost_estimate=cost(0.1),
        name="join",
    )(*arrays)


def halves_kernel(back, ahead, low, high):
    low[...] = back[0:2]
    high[...] = ahead[2:4]


def halves(back, ahead):
    return pl.pallas_call(
        halves_kernel,
        in_specs=[VMEM] * 2,
        out_specs=[VMEM] * 2,
        out_shape=[shape((2,) + back.shape[1:], bf16)] * 2,
        compiler_params=PARAMS,
        cost_estimate=cost(0.1),
        name="halves",
    )(back, ahead)


def shifted(value, axis, by):
    size = lax.axis_size(axis)
    return lax.ppermute(value, axis, [(i, (i + by) % size) for i in range(size)])


def swapped(value, axis, bit):
    return lax.ppermute(value, axis, [(i, i ^ bit) for i in range(lax.axis_size(axis))])


def after(value, other):
    return lax.optimization_barrier((value, other))[0]


def exchange(values, sign):
    return [values[0]] + [shifted(values[k], "x", sign * k) for k in range(1, 4)]


def with_core(pieces):
    return pieces + [swapped(piece, "core", 1) for piece in pieces]


def gathered_ring(value):
    near = [value, shifted(value, "y", 1), shifted(value, "y", -1)]
    low, high = halves(near[1], near[2])
    far = [shifted(low, "y", 1), shifted(high, "y", -1)]
    return with_core(near), far


def on_device(x_rows, lengths, targets, w_in, w_out, w_score, head_score, grad_out, grad_score):
    x, lengths, targets = x_rows[0], lengths[0], targets[0]
    idx = jnp.stack([lax.axis_index(a) for a in SEQ]).astype(jnp.int32)
    normed, kvq = project(x, w_in)
    kvq = exchange(kvq, 1)
    held = join(kvq, 3 * DH)
    near_pieces, far_pieces = gathered_ring(held)
    normed = after(normed, kvq[3])
    near = [shifted(normed, "x", 1), shifted(normed, "x", -1)]
    normed_all = [normed, near[0], shifted(after(normed, near), "x", 2), near[1]]
    partly = attend_near(idx, lengths, targets, near_pieces)
    far_pieces, near, partly = lax.optimization_barrier((far_pieces, near, partly))
    far_pieces = with_core(far_pieces)
    forwarded = attend_far(idx, lengths, targets, held, far_pieces, partly[0], partly[1:4])
    k_all, v_all, q_all = forwarded[4:7]
    attended = exchange(forwarded[0:4], -1)
    gate, gate_slope = gates(after(normed, forwarded[0]), w_in)
    slope = slopes(idx, after(normed_all, forwarded[0]), w_in)
    attended = after(attended, slope)
    mid = middle(
        idx, lengths, targets, attended, gate, gate_slope, x, w_out, w_score,
        head_score.reshape(1, 256), grad_out[0], grad_score,
    )
    gate_full, acts, d_mid = mid[4:7]
    d_att = exchange(mid[0:4], 1)
    acts_other = swapped(after(acts, d_att), "core", 1)
    d_own = join(d_att, DH)
    late = [shifted(d_own, "y", k) for k in range(1, 4)]
    d_query = query_grads(idx, lengths, targets, held, d_att, k_all, v_all)
    early = parts(idx, after(acts, d_query[0]), acts_other)
    d_pieces = with_core([d_own] + after(late, early))
    keyed = key_grads(
        idx, lengths, targets, d_pieces, (k_all, v_all, q_all), slope, d_query, d_att
    )
    keep, send = weights(idx, normed_all, keyed[4])
    got = swapped(send, "core", 1)
    partial = merge(keep, got, early)
    back, partial = lax.optimization_barrier((keyed[0:4], partial))
    partial = lax.all_to_all(partial, SEQ, 0, 0, tiled=True)
    back = exchange(back, -1)
    partial = after(partial, back)
    d_x = input_grads(idx, back, gate_full, w_in, x, grad_out[0], d_mid, w_score)
    last = lax.all_to_all(pack(partial), "dp", 0, 0, tiled=True)
    d_w_in, d_w_out, d_w_score, d_head = last_sum(last)
    return d_x[None], d_w_in, d_w_out, d_w_score, d_head.reshape(256)


def solution(mesh):
    inner = Mesh(mesh.devices.reshape(8, 4, 4, 2), ("dp", "x", "y", "core"))
    placed = (
        P("dp", SEQ, None),
        P("dp", None),
        P("dp", None),
        P(),
        P(),
        P(),
        P(),
        P("dp", SEQ, None),
        P("dp", SEQ),
    )
    return jax.shard_map(
        on_device,
        mesh=inner,
        in_specs=placed,
        out_specs=(P("dp", SEQ, None), P(SEQ, "dp"), P(SEQ, "dp"), P(SEQ, "dp"), P()),
        check_vma=False,
    )
```

profile of v0, /device:TPU:1, one launch (start us, length us, event | category | flops | bytes accessed | tf_op | source)
XLA Modules:
  0.0 133.2 jit_solution(15079039100961967555)
XLA Ops:
  0.7 3.4 %project.1 = (bf16[128,1024]{1,0:T(8,128)(2,1)}, bf16[128,384]{1,0:T(8,128)(2,1)}, bf16[128,384]{1,0:T(8,128)(2,1)}, bf16[128,384]{1,0:T(8,128)(2,1)}, bf16[128,384]{1,0:T(8,128)(2,1)}) custom-call(bf16[128,1024]{1,0:T(8,128)(2,1)} %bitcast.10, bf16[1024,2048]{1,0:T(8,128)(2,1)} %w_ref.1), custom_call_target="tpu_custom_call" | custom-call | flops 3449999872 | tf_op jit(solution)/shard_map/project/pallas_call | solution.py:123
  4.1 3.4 %collective-permute-start.2 = (bf16[128,384]{1,0:T(8,128)(2,1)}, bf16[128,384]{1,0:T(8,128)(2,1)S(1)}, u32[]{:S(2)}, u32[]{:S(2)}) collective-permute-start(bf16[128,384]{1,0:T(8,128)(2,1)} %get-tuple-element.78), channel_id=1, source_target_pairs={{0,24},{8,0},{16,8},{24,16},{1,25},{9,1},{17,9},{25,17},{2,26},{10... | collective-permute-start | bytes 294920 | tf_op jit(solution)/shard_map/ppermute | solution.py:812
  7.4 1.7 %collective-permute-start.1 = (bf16[128,384]{1,0:T(8,128)(2,1)}, bf16[128,384]{1,0:T(8,128)(2,1)S(1)}, u32[]{:S(2)}, u32[]{:S(2)}) collective-permute-start(bf16[128,384]{1,0:T(8,128)(2,1)} %get-tuple-element.77), channel_id=1, source_target_pairs={{0,16},{8,24},{16,0},{24,8},{1,17},{9,25},{17,1},{25,9},{2,18},{10... | collective-permute-start | bytes 294920 | tf_op jit(solution)/shard_map/ppermute | solution.py:812
  9.2 0.2 collective-permute-done.2.refs_3_
  9.4 4.5 %collective-permute-done.refs_1_ = bf16[128,384]{1,0:T(8,128)(2,1)S(1)} collective-permute-done((bf16[128,384]{1,0:T(8,128)(2,1)}, bf16[128,384]{1,0:T(8,128)(2,1)S(1)}, u32[]{:S(2)}, u32[]{:S(2)}) %collective-permute-start) | collective-permute-done | bytes 98336 | tf_op jit(solution)/shard_map/ppermute | solution.py:812
  13.9 0.9 copy-done.7
  14.8 1.4 %collective-permute-start.3 = (bf16[4,128,384]{2,1,0:T(8,128)(2,1)S(1)}, bf16[4,128,384]{2,1,0:T(8,128)(2,1)S(1)}, u32[]{:S(2)}, u32[]{:S(2)}) collective-permute-start(bf16[4,128,384]{2,1,0:T(8,128)(2,1)S(1)} %join.2.refs_0_), channel_id=1, source_target_pairs={{0,2},{2,4},{4,6},{6,0},{1,3},{3,5},{5,7},{7,1},{8,10},{10,12},{12... | collective-permute-start | bytes 1179656 | tf_op jit(solution)/shard_map/ppermute | solution.py:812
  16.2 1.5 %collective-permute-start.4 = (bf16[4,128,384]{2,1,0:T(8,128)(2,1)S(1)}, bf16[4,128,384]{2,1,0:T(8,128)(2,1)S(1)}, u32[]{:S(2)}, u32[]{:S(2)}) collective-permute-start(bf16[4,128,384]{2,1,0:T(8,128)(2,1)S(1)} %join.2.refs_0_), channel_id=1, source_target_pairs={{0,6},{2,0},{4,2},{6,4},{1,7},{3,1},{5,3},{7,5},{8,14},{10,8},{12,... | collective-permute-start | bytes 1179656 | tf_op jit(solution)/shard_map/ppermute | solution.py:812
  17.7 2.7 %collective-permute-start.8 = (bf16[128,1024]{1,0:T(8,128)(2,1)}, bf16[128,1024]{1,0:T(8,128)(2,1)S(1)}, u32[]{:S(2)}, u32[]{:S(2)}) collective-permute-start(bf16[128,1024]{1,0:T(8,128)(2,1)} %get-tuple-element.106.n0.normed_ref), channel_id=1, source_target_pairs={{0,24},{8,0},{16,8},{24,16},{1,25},{9,1},{17,9},{25,17},{2,26},{10... | collective-permute-start | bytes 786440 | tf_op jit(solution)/shard_map/ppermute | solution.py:812
  20.4 3.3 %collective-permute-start.9 = (bf16[4,128,384]{2,1,0:T(8,128)(2,1)S(1)}, bf16[4,128,384]{2,1,0:T(8,128)(2,1)S(1)}, u32[]{:S(2)}, u32[]{:S(2)}) collective-permute-start(bf16[4,128,384]{2,1,0:T(8,128)(2,1)S(1)} %join.2.refs_0_), channel_id=1, source_target_pairs={{0,1},{1,0},{2,3},{3,2},{4,5},{5,4},{6,7},{7,6},{8,9},{9,8},{10,11... | collective-permute-start | bytes 1179656 | tf_op jit(solution)/shard_map/ppermute | solution.py:816
  23.7 0.9 collective-permute-done.3.back.refs_1_
  24.6 3.1 %collective-permute-start.10 = (bf16[4,128,384]{2,1,0:T(8,128)(2,1)S(1)}, bf16[4,128,384]{2,1,0:T(8,128)(2,1)S(1)}, u32[]{:S(2)}, u32[]{:S(2)}) collective-permute-start(bf16[4,128,384]{2,1,0:T(8,128)(2,1)S(1)} %collective-permute-done.3.back.refs_1_), channel_id=1, source_target_pairs={{0,1},{1,0},{2,3},{3,2},{4,5},{5,4},{6,7},{7,6},{8,9},{9,8},{10,11... | collective-permute-start | bytes 1179656 | tf_op jit(solution)/shard_map/ppermute | solution.py:816
  27.7 0.8 halves.1
  28.5 1.3 collective-permute-start.5
  29.8 1.5 %collective-permute-start.6 = (bf16[2,128,384]{2,1,0:T(8,128)(2,1)}, bf16[2,128,384]{2,1,0:T(8,128)(2,1)S(1)}, u32[]{:S(2)}, u32[]{:S(2)}) collective-permute-start(bf16[2,128,384]{2,1,0:T(8,128)(2,1)} %get-tuple-element.80), channel_id=1, source_target_pairs={{0,6},{2,0},{4,2},{6,4},{1,7},{3,1},{5,3},{7,5},{8,14},{10,8},{12,... | collective-permute-start | bytes 589832 | tf_op jit(solution)/shard_map/ppermute | solution.py:812
  31.4 1.1 collective-permute-start.17
  32.5 3.5 %attend_near.1 = (f32[4,128,128]{2,1,0:T(8,128)S(1)}, bf16[4096,128]{1,0:T(8,128)(2,1)S(1)}, bf16[4096,128]{1,0:T(8,128)(2,1)S(1)}, bf16[4096,128]{1,0:T(8,128)(2,1)S(1)}) custom-call(s32[3]{0:T(128)S(1)} %pad_add_fusion.idx, s32[8]{0:T(128)S(1)} %bitcast.15, s32[8]{0:T(128)S(1)} %bitcast.20, bf16[4,128,384]{2,1,0:T(8,128)(2,1)S(1)} %join.2.refs_0_, ...), custom_call_target="tpu_custom_call" | custom-call | flops 575000000 | tf_op jit(solution)/shard_map/attend_near/pallas_call | solution.py:292
  36.1 0.2 collective-permute-done.6.refs_2_
  36.2 1.3 %collective-permute-start.12 = (bf16[2,128,384]{2,1,0:T(8,128)(2,1)S(1)}, bf16[2,128,384]{2,1,0:T(8,128)(2,1)S(1)}, u32[]{:S(2)}, u32[]{:S(2)}) collective-permute-start(bf16[2,128,384]{2,1,0:T(8,128)(2,1)S(1)} %collective-permute-done.5.refs_1_), channel_id=1, source_target_pairs={{0,1},{1,0},{2,3},{3,2},{4,5},{5,4},{6,7},{7,6},{8,9},{9,8},{10,11... | collective-permute-start | bytes 589832 | tf_op jit(solution)/shard_map/ppermute | solution.py:816
  37.7 1.0 collective-permute-done.12.refs_3_
  38.7 0.4 collective-permute-done.13.refs_4_
  39.0 2.8 %attend_far.1 = (f32[128,128]{1,0:T(8,128)S(1)}, f32[128,128]{1,0:T(8,128)S(1)}, f32[128,128]{1,0:T(8,128)S(1)}, f32[128,128]{1,0:T(8,128)S(1)}, bf16[4096,128]{...) custom-call(s32[3]{0:T(128)S(1)} %pad_add_fusion.idx, ...), custom_call_target="tpu_custom_call", output_to_operand_aliasing={{4}: (9, {}), {5}: (10, {}), {6}: (11, {})} | custom-call | flops 575000000 | tf_op jit(solution)/shard_map/attend_far/pallas_call | solution.py:348
  41.8 1.2 collective-permute-start.14
  43.1 1.5 %collective-permute-start.15 = (f32[128,128]{1,0:T(8,128)S(1)}, f32[128,128]{1,0:T(8,128)S(1)}, u32[]{:S(2)}, u32[]{:S(2)}) collective-permute-start(f32[128,128]{1,0:T(8,128)S(1)} %get-tuple-element.95), channel_id=1, source_target_pairs={{0,16},{8,24},{16,0},{24,8},{1,17},{9,25},{17,1},{25,9},{2,18},{10... | collective-permute-start | bytes 196616 | tf_op jit(solution)/shard_map/ppermute | solution.py:812
  44.6 0.5 gates.1
  45.2 2.1 %slopes.1.refs_11_ = f32[4,128,384]{2,1,0:T(8,128)S(1)} custom-call(s32[3]{0:T(128)S(1)} %pad_add_fusion.idx, bf16[128,1024]{1,0:T(8,128)(2,1)S(1)} %copy-done.2, bf16[128,1024]{1,0:T(8,128)(2,1)S(1)} %collective-permute-done.7.n1, bf16[128,1024]{1,0:T(8,128)(2,1)S(1)} %collective-permute-done.17.n2, bf16[128,1024]{1,0:T(8,128)(2,1)S(1)} %collective-permute-done.8.n3, ...), custom_call_target="tpu_custom_call" | custom-call | flops 575000000 | tf_op jit(solution)/shard_map/slopes/pallas_call | solution.py:177
  47.4 0.3 collective-permute-done.15.a2
  47.7 1.9 %collective-permute-done.16.a3 = f32[128,128]{1,0:T(8,128)S(1)} collective-permute-done((f32[128,128]{1,0:T(8,128)S(1)}, f32[128,128]{1,0:T(8,128)S(1)}, u32[]{:S(2)}, u32[]{:S(2)}) %collective-permute-start.16) | collective-permute-done | bytes 65568 | tf_op jit(solution)/shard_map/ppermute | solution.py:812
  49.6 2.0 %middle.1 = (bf16[128,256]{1,0:T(8,128)(2,1)S(1)}, bf16[128,256]{1,0:T(8,128)(2,1)S(1)}, bf16[128,256]{1,0:T(8,128)(2,1)S(1)}, bf16[128,256]{1,0:T(8,128)(2,1)S(...) custom-call(s32[3]{0:T(128)S(1)} %pad_add_fusion.idx, ...), custom_call_target="tpu_custom_call" | custom-call | flops 575000000 | tf_op jit(solution)/shard_map/middle/pallas_call | solution.py:428
  51.7 1.6 %collective-permute-start.19 = (bf16[128,256]{1,0:T(8,128)(2,1)S(1)}, bf16[128,256]{1,0:T(8,128)(2,1)S(1)}, u32[]{:S(2)}, u32[]{:S(2)}) collective-permute-start(bf16[128,256]{1,0:T(8,128)(2,1)S(1)} %get-tuple-element.111), channel_id=1, source_target_pairs={{0,16},{8,24},{16,0},{24,8},{1,17},{9,25},{17,1},{25,9},{2,18},{10... | collective-permute-start | bytes 196616 | tf_op jit(solution)/shard_map/ppermute | solution.py:812
  53.3 1.9 %collective-permute-start.20 = (bf16[128,256]{1,0:T(8,128)(2,1)S(1)}, bf16[128,256]{1,0:T(8,128)(2,1)S(1)}, u32[]{:S(2)}, u32[]{:S(2)}) collective-permute-start(bf16[128,256]{1,0:T(8,128)(2,1)S(1)} %get-tuple-element.112), channel_id=1, source_target_pairs={{0,24},{8,0},{16,8},{24,16},{1,25},{9,1},{17,9},{25,17},{2,26},{10... | collective-permute-start | bytes 196616 | tf_op jit(solution)/shard_map/ppermute | solution.py:812
  55.2 1.3 collective-permute-done.18.refs_1_.refs_2_.refs_17_
  56.5 0.5 collective-permute-done.19.refs_2_.refs_3_.refs_18_
  57.0 0.6 collective-permute-done.20.refs_3_.refs_4_.refs_19_
  57.6 2.4 %collective-permute-start.24 = (bf16[144,2816]{1,0:T(8,128)(2,1)S(1)}, bf16[144,2816]{1,0:T(8,128)(2,1)S(1)}, u32[]{:S(2)}, u32[]{:S(2)}) collective-permute-start(bf16[144,2816]{1,0:T(8,128)(2,1)S(1)} %get-tuple-element.118.own), channel_id=1, source_target_pairs={{0,1},{1,0},{2,3},{3,2},{4,5},{5,4},{6,7},{7,6},{8,9},{9,8},{10,11... | collective-permute-start | bytes 2433032 | tf_op jit(solution)/shard_map/ppermute | solution.py:816
  60.1 0.5 collective-permute-start.21
  60.5 3.1 %collective-permute-start.22 = (bf16[4,128,128]{2,1,0:T(8,128)(2,1)S(1)}, bf16[4,128,128]{2,1,0:T(8,128)(2,1)S(1)}, u32[]{:S(2)}, u32[]{:S(2)}) collective-permute-start(bf16[4,128,128]{2,1,0:T(8,128)(2,1)S(1)} %join.3.refs_0_), channel_id=1, source_target_pairs={{0,4},{2,6},{4,0},{6,2},{1,5},{3,7},{5,1},{7,3},{8,12},{10,14},{12... | collective-permute-start | bytes 393224 | tf_op jit(solution)/shard_map/ppermute | solution.py:812
  63.6 0.8 collective-permute-start.23
  64.4 0.8 collective-permute-start.25
  65.3 3.5 %query_grads.1 = (f32[128,128]{1,0:T(8,128)S(1)}, f32[128,128]{1,0:T(8,128)S(1)}, f32[128,128]{1,0:T(8,128)S(1)}, f32[128,128]{1,0:T(8,128)S(1)}) custom-call(s32[3]{0:T(128)S(1)} %pad_add_fusion.idx, s32[8]{0:T(128)S(1)} %bitcast.18, s32[8]{0:T(128)S(1)} %bitcast.23, bf16[4,128,384]{2,1,0:T(8,128)(2,1)S(1)} %join.2.refs_0_, ...), custom_call_target="tpu_custom_call" | custom-call | flops 3449999872 | tf_op jit(solution)/shard_map/query_grads/pallas_call | solution.py:483
  68.8 1.1 parts.1.early
  69.9 0.2 collective-permute-done.22.refs_2_
  70.1 0.8 collective-permute-start.26
  70.9 0.5 collective-permute-start.28
  71.4 0.5 collective-permute-done.26.refs_5_
  71.9 0.4 collective-permute-done.27.refs_6_
  72.2 0.2 collective-permute-done.28.refs_7_
  72.4 6.3 %key_grads.1 = (bf16[128,384]{1,0:T(8,128)(2,1)S(1)}, bf16[128,384]{1,0:T(8,128)(2,1)S(1)}, bf16[128,384]{1,0:T(8,128)(2,1)S(1)}, bf16[128,384]{1,0:T(8,128)(2,1)S(1)}, bf16[512,512]{1,0:T(8,128)(2,1)S(1)}) custom-call(s32[3]{0:T(128)S(1)} %pad_add_fusion.idx, s32[8]{0:T(128)S(1)} %bitcast.19, s32[8]{0:T(128)S(1)} %bitcast.24, ...), custom_call_target="tpu_custom_call" | custom-call | flops 23000000 | tf_op jit(solution)/shard_map/key_grads/pallas_call | solution.py:559
  78.7 2.0 %weights.1 = (f32[32,16,512]{2,1,0:T(8,128)S(1)}, bf16[32,16,512]{2,1,0:T(8,128)(2,1)S(1)}) custom-call(s32[3]{0:T(128)S(1)} %pad_add_fusion.idx, bf16[128,1024]{1,0:T(8,128)(2,1)S(1)} %copy-done.2, bf16[128,1024]{1,0:T(8,128)(2,1)S(1)} %collective-permute-done.7.n1, bf16[128,1024]{1,0:T(8,128)(2,1)S(1)} %collective-permute-done.17.n2, ...), custom_call_target="tpu_custom_call" | custom-call | flops 23000000 | tf_op jit(solution)/shard_map/weights/pallas_call | solution.py:629
  80.9 1.9 %collective-permute-done.29.got = bf16[32,16,512]{2,1,0:T(8,128)(2,1)S(1)} collective-permute-done((bf16[32,16,512]{2,1,0:T(8,128)(2,1)S(1)}, bf16[32,16,512]{2,1,0:T(8,128)(2,1)S(1)}, u32[]{:S(2)}, u32[]{:S(2)}) %collective-permute-start.29) | collective-permute-done | bytes 524320 | tf_op jit(solution)/shard_map/ppermute | solution.py:816
  82.8 1.3 %merge.1 = bf16[32,48,512]{2,1,0:T(8,128)(2,1)} custom-call(f32[32,16,512]{2,1,0:T(8,128)S(1)} %get-tuple-element.131.keep, bf16[32,16,512]{2,1,0:T(8,128)(2,1)S(1)} %collective-permute-done.29.got, bf16[32,32,512]{2,1,0:T(8,128)(2,1)S(1)} %parts.1.early), custom_call_target="tpu_custom_call" | custom-call | flops 345000000 | tf_op jit(solution)/shard_map/merge/pallas_call | solution.py:648
  84.1 6.4 %all-to-all-start = ((bf16[32,48,512]{2,1,0:T(8,128)(2,1)}), bf16[32,48,512]{2,1,0:T(8,128)(2,1)S(1)}, u32[]{:S(2)}, u32[]{:S(2)}) async-start(bf16[32,48,512]{2,1,0:T(8,128)(2,1)} %merge.1), calls=%async_computation | async-start | bytes 3145728 | tf_op jit(solution)/shard_map/all_to_all | solution.py:876
  90.6 2.7 %collective-permute-start.30 = (bf16[128,384]{1,0:T(8,128)(2,1)S(1)}, bf16[128,384]{1,0:T(8,128)(2,1)S(1)}, u32[]{:S(2)}, u32[]{:S(2)}) collective-permute-start(bf16[128,384]{1,0:T(8,128)(2,1)S(1)} %copy-done.15), channel_id=1, source_target_pairs={{0,24},{8,0},{16,8},{24,16},{1,25},{9,1},{17,9},{25,17},{2,26},{10... | collective-permute-start | bytes 294920 | tf_op jit(solution)/shard_map/ppermute | solution.py:812
  93.3 0.5 collective-permute-start.31
  93.8 0.6 collective-permute-start.32
  94.4 17.5 %collective-permute-done.30.b1 = bf16[128,384]{1,0:T(8,128)(2,1)S(1)} collective-permute-done((bf16[128,384]{1,0:T(8,128)(2,1)S(1)}, bf16[128,384]{1,0:T(8,128)(2,1)S(1)}, u32[]{:S(2)}, u32[]{:S(2)}) %collective-permute-start.30) | collective-permute-done | bytes 98336 | tf_op jit(solution)/shard_map/ppermute | solution.py:812
  111.9 1.4 %collective-permute-done.31.b2 = bf16[128,384]{1,0:T(8,128)(2,1)S(1)} collective-permute-done((bf16[128,384]{1,0:T(8,128)(2,1)S(1)}, bf16[128,384]{1,0:T(8,128)(2,1)S(1)}, u32[]{:S(2)}, u32[]{:S(2)}) %collective-permute-start.31) | collective-permute-done | bytes 98336 | tf_op jit(solution)/shard_map/ppermute | solution.py:812
  113.4 1.7 %collective-permute-done.32.b3 = bf16[128,384]{1,0:T(8,128)(2,1)S(1)} collective-permute-done((bf16[128,384]{1,0:T(8,128)(2,1)S(1)}, bf16[128,384]{1,0:T(8,128)(2,1)S(1)}, u32[]{:S(2)}, u32[]{:S(2)}) %collective-permute-start.32) | collective-permute-done | bytes 98336 | tf_op jit(solution)/shard_map/ppermute | solution.py:812
  115.1 0.9 pack.1
  116.0 7.9 %all-to-all-start.1 = ((bf16[8,96,128]{2,1,0:T(8,128)(2,1)}), bf16[8,96,128]{2,1,0:T(8,128)(2,1)S(1)}, u32[]{:S(2)}, u32[]{:S(2)}) async-start(bf16[8,96,128]{2,1,0:T(8,128)(2,1)} %pack.1), calls=%async_computation.1 | async-start | bytes 393216 | tf_op jit(solution)/shard_map/all_to_all | solution.py:880
  123.9 2.2 %copy-done.1 = bf16[1024,2048]{1,0:T(8,128)(2,1)S(1)} copy-done((bf16[1024,2048]{1,0:T(8,128)(2,1)S(1)}, bf16[1024,2048]{1,0:T(8,128)(2,1)}, u32[]{:S(2)}) %copy-start.1) | copy-done | bytes 4194328
  126.1 3.8 %input_grads.1 = bf16[128,1024]{1,0:T(8,128)(2,1)} custom-call(s32[3]{0:T(128)S(1)} %pad_add_fusion.idx, bf16[128,384]{1,0:T(8,128)(2,1)S(1)} %get-tuple-element.133.b0, bf16[128,384]{1,0:T(8,128)(2,1)S(1)} %collective-permute-done.30.b1, bf16[128,384]{1,0:T(8,128)(2,1)S(1)} %collective-permute-done.31.b2, bf16[128,384]{1,0:T(8,128)(2,1)S(1)} %collective-permute-done.32.b3, ...), custom_call_target="tpu_custom_call" | custom-call | flops 1150000000 | tf_op jit(solution)/shard_map/input_grads/pallas_call | solution.py:754
  129.9 2.6 %all-to-all-done.1.ref = bf16[8,96,128]{2,1,0:T(8,128)(2,1)S(1)} async-done(((bf16[8,96,128]{2,1,0:T(8,128)(2,1)}), bf16[8,96,128]{2,1,0:T(8,128)(2,1)S(1)}, u32[]{:S(2)}, u32[]{:S(2)}) %all-to-all-start.1) | async-done | bytes 196640 | tf_op jit(solution)/shard_map/all_to_all | solution.py:880
  132.5 0.7 last_sum.1
  (56 shorter events, 0.7 us)
Async XLA Ops:
  0.6 31.9 %copy-start.8 = (s32[1,8]{1,0:T(1,128)S(1)}, s32[1,8]{1,0:T(1,128)}, u32[]{:S(2)}) copy-start(s32[1,8]{1,0:T(1,128)} %param.10) | copy-start | bytes 100
  0.6 31.9 %copy-start.9 = (s32[1,8]{1,0:T(1,128)S(1)}, s32[1,8]{1,0:T(1,128)}, u32[]{:S(2)}) copy-start(s32[1,8]{1,0:T(1,128)} %param.11) | copy-start | bytes 100
  4.0 27.4 %copy-start.2 = (bf16[128,1024]{1,0:T(8,128)(2,1)S(1)}, bf16[128,1024]{1,0:T(8,128)(2,1)}, u32[]{:S(2)}) copy-start(bf16[128,1024]{1,0:T(8,128)(2,1)} %get-tuple-element.106.n0.normed_ref) | copy-start | bytes 786436
  4.1 5.3 %collective-permute-start.2 = (bf16[128,384]{1,0:T(8,128)(2,1)}, bf16[128,384]{1,0:T(8,128)(2,1)S(1)}, u32[]{:S(2)}, u32[]{:S(2)}) collective-permute-start(bf16[128,384]{1,0:T(8,128)(2,1)} %get-tuple-element.78), channel_id=1, source_target_pairs={{0,24},{8,0},{16,8},{24,16},{1,25},{9,1},{17,9},{25,17},{2,26},{10... | collective-permute-start | bytes 294920 | tf_op jit(solution)/shard_map/ppermute | solution.py:812
  7.4 6.5 %collective-permute-start = (bf16[128,384]{1,0:T(8,128)(2,1)}, bf16[128,384]{1,0:T(8,128)(2,1)S(1)}, u32[]{:S(2)}, u32[]{:S(2)}) collective-permute-start(bf16[128,384]{1,0:T(8,128)(2,1)} %get-tuple-element.76), channel_id=1, source_target_pairs={{0,8},{8,16},{16,24},{24,0},{1,9},{9,17},{17,25},{25,1},{2,10},{10... | collective-permute-start | bytes 294920 | tf_op jit(solution)/shard_map/ppermute | solution.py:812
  7.4 6.5 %collective-permute-start.1 = (bf16[128,384]{1,0:T(8,128)(2,1)}, bf16[128,384]{1,0:T(8,128)(2,1)S(1)}, u32[]{:S(2)}, u32[]{:S(2)}) collective-permute-start(bf16[128,384]{1,0:T(8,128)(2,1)} %get-tuple-element.77), channel_id=1, source_target_pairs={{0,16},{8,24},{16,0},{24,8},{1,17},{9,25},{17,1},{25,9},{2,18},{10... | collective-permute-start | bytes 294920 | tf_op jit(solution)/shard_map/ppermute | solution.py:812
  13.9 0.9 copy-start.7
  14.8 9.7 %collective-permute-start.3 = (bf16[4,128,384]{2,1,0:T(8,128)(2,1)S(1)}, bf16[4,128,384]{2,1,0:T(8,128)(2,1)S(1)}, u32[]{:S(2)}, u32[]{:S(2)}) collective-permute-start(bf16[4,128,384]{2,1,0:T(8,128)(2,1)S(1)} %join.2.refs_0_), channel_id=1, source_target_pairs={{0,2},{2,4},{4,6},{6,0},{1,3},{3,5},{5,7},{7,1},{8,10},{10,12},{12... | collective-permute-start | bytes 1179656 | tf_op jit(solution)/shard_map/ppermute | solution.py:812
  16.2 11.5 %collective-permute-start.4 = (bf16[4,128,384]{2,1,0:T(8,128)(2,1)S(1)}, bf16[4,128,384]{2,1,0:T(8,128)(2,1)S(1)}, u32[]{:S(2)}, u32[]{:S(2)}) collective-permute-start(bf16[4,128,384]{2,1,0:T(8,128)(2,1)S(1)} %join.2.refs_0_), channel_id=1, source_target_pairs={{0,6},{2,0},{4,2},{6,4},{1,7},{3,1},{5,3},{7,5},{8,14},{10,8},{12,... | collective-permute-start | bytes 1179656 | tf_op jit(solution)/shard_map/ppermute | solution.py:812
  17.7 10.8 %collective-permute-start.7 = (bf16[128,1024]{1,0:T(8,128)(2,1)}, bf16[128,1024]{1,0:T(8,128)(2,1)S(1)}, u32[]{:S(2)}, u32[]{:S(2)}) collective-permute-start(bf16[128,1024]{1,0:T(8,128)(2,1)} %get-tuple-element.106.n0.normed_ref), channel_id=1, source_target_pairs={{0,8},{8,16},{16,24},{24,0},{1,9},{9,17},{17,25},{25,1},{2,10},{10... | collective-permute-start | bytes 786440 | tf_op jit(solution)/shard_map/ppermute | solution.py:812
  17.7 12.1 %collective-permute-start.8 = (bf16[128,1024]{1,0:T(8,128)(2,1)}, bf16[128,1024]{1,0:T(8,128)(2,1)S(1)}, u32[]{:S(2)}, u32[]{:S(2)}) collective-permute-start(bf16[128,1024]{1,0:T(8,128)(2,1)} %get-tuple-element.106.n0.normed_ref), channel_id=1, source_target_pairs={{0,24},{8,0},{16,8},{24,16},{1,25},{9,1},{17,9},{25,17},{2,26},{10... | collective-permute-start | bytes 786440 | tf_op jit(solution)/shard_map/ppermute | solution.py:812
  20.4 11.0 %collective-permute-start.9 = (bf16[4,128,384]{2,1,0:T(8,128)(2,1)S(1)}, bf16[4,128,384]{2,1,0:T(8,128)(2,1)S(1)}, u32[]{:S(2)}, u32[]{:S(2)}) collective-permute-start(bf16[4,128,384]{2,1,0:T(8,128)(2,1)S(1)} %join.2.refs_0_), channel_id=1, source_target_pairs={{0,1},{1,0},{2,3},{3,2},{4,5},{5,4},{6,7},{7,6},{8,9},{9,8},{10,11... | collective-permute-start | bytes 1179656 | tf_op jit(solution)/shard_map/ppermute | solution.py:816
  24.6 7.9 %collective-permute-start.10 = (bf16[4,128,384]{2,1,0:T(8,128)(2,1)S(1)}, bf16[4,128,384]{2,1,0:T(8,128)(2,1)S(1)}, u32[]{:S(2)}, u32[]{:S(2)}) collective-permute-start(bf16[4,128,384]{2,1,0:T(8,128)(2,1)S(1)} %collective-permute-done.3.back.refs_1_), channel_id=1, source_target_pairs={{0,1},{1,0},{2,3},{3,2},{4,5},{5,4},{6,7},{7,6},{8,9},{9,8},{10,11... | collective-permute-start | bytes 1179656 | tf_op jit(solution)/shard_map/ppermute | solution.py:816
  27.7 4.8 %collective-permute-start.11 = (bf16[4,128,384]{2,1,0:T(8,128)(2,1)S(1)}, bf16[4,128,384]{2,1,0:T(8,128)(2,1)S(1)}, u32[]{:S(2)}, u32[]{:S(2)}) collective-permute-start(bf16[4,128,384]{2,1,0:T(8,128)(2,1)S(1)} %collective-permute-done.4.ahead.refs_2_), channel_id=1, source_target_pairs={{0,1},{1,0},{2,3},{3,2},{4,5},{5,4},{6,7},{7,6},{8,9},{9,8},{10,11... | collective-permute-start | bytes 1179656 | tf_op jit(solution)/shard_map/ppermute | solution.py:816
  28.5 7.5 %collective-permute-start.5 = (bf16[2,128,384]{2,1,0:T(8,128)(2,1)}, bf16[2,128,384]{2,1,0:T(8,128)(2,1)S(1)}, u32[]{:S(2)}, u32[]{:S(2)}) collective-permute-start(bf16[2,128,384]{2,1,0:T(8,128)(2,1)} %get-tuple-element.79), channel_id=1, source_target_pairs={{0,2},{2,4},{4,6},{6,0},{1,3},{3,5},{5,7},{7,1},{8,10},{10,12},{12... | collective-permute-start | bytes 589832 | tf_op jit(solution)/shard_map/ppermute | solution.py:812
  29.8 6.4 %collective-permute-start.6 = (bf16[2,128,384]{2,1,0:T(8,128)(2,1)}, bf16[2,128,384]{2,1,0:T(8,128)(2,1)S(1)}, u32[]{:S(2)}, u32[]{:S(2)}) collective-permute-start(bf16[2,128,384]{2,1,0:T(8,128)(2,1)} %get-tuple-element.80), channel_id=1, source_target_pairs={{0,6},{2,0},{4,2},{6,4},{1,7},{3,1},{5,3},{7,5},{8,14},{10,8},{12,... | collective-permute-start | bytes 589832 | tf_op jit(solution)/shard_map/ppermute | solution.py:812
  31.4 10.4 %collective-permute-start.17 = (bf16[128,1024]{1,0:T(8,128)(2,1)S(1)}, bf16[128,1024]{1,0:T(8,128)(2,1)S(1)}, u32[]{:S(2)}, u32[]{:S(2)}) collective-permute-start(bf16[128,1024]{1,0:T(8,128)(2,1)S(1)} %copy-done.2), channel_id=1, source_target_pairs={{0,16},{8,24},{16,0},{24,8},{1,17},{9,25},{17,1},{25,9},{2,18},{10... | collective-permute-start | bytes 786440 | tf_op jit(solution)/shard_map/ppermute | solution.py:812
  36.2 8.4 %copy-start = (bf16[1024,2048]{1,0:T(8,128)(2,1)S(1)}, bf16[1024,2048]{1,0:T(8,128)(2,1)}, u32[]{:S(2)}) copy-start(bf16[1024,2048]{1,0:T(8,128)(2,1)} %w_ref.1) | copy-start | bytes 12582916
  36.2 2.4 %collective-permute-start.12 = (bf16[2,128,384]{2,1,0:T(8,128)(2,1)S(1)}, bf16[2,128,384]{2,1,0:T(8,128)(2,1)S(1)}, u32[]{:S(2)}, u32[]{:S(2)}) collective-permute-start(bf16[2,128,384]{2,1,0:T(8,128)(2,1)S(1)} %collective-permute-done.5.refs_1_), channel_id=1, source_target_pairs={{0,1},{1,0},{2,3},{3,2},{4,5},{5,4},{6,7},{7,6},{8,9},{9,8},{10,11... | collective-permute-start | bytes 589832 | tf_op jit(solution)/shard_map/ppermute | solution.py:816
  37.6 1.4 %collective-permute-start.13 = (bf16[2,128,384]{2,1,0:T(8,128)(2,1)S(1)}, bf16[2,128,384]{2,1,0:T(8,128)(2,1)S(1)}, u32[]{:S(2)}, u32[]{:S(2)}) collective-permute-start(bf16[2,128,384]{2,1,0:T(8,128)(2,1)S(1)} %collective-permute-done.6.refs_2_), channel_id=1, source_target_pairs={{0,1},{1,0},{2,3},{3,2},{4,5},{5,4},{6,7},{7,6},{8,9},{9,8},{10,11... | collective-permute-start | bytes 589832 | tf_op jit(solution)/shard_map/ppermute | solution.py:816
  41.8 5.5 %collective-permute-start.14 = (f32[128,128]{1,0:T(8,128)S(1)}, f32[128,128]{1,0:T(8,128)S(1)}, u32[]{:S(2)}, u32[]{:S(2)}) collective-permute-start(f32[128,128]{1,0:T(8,128)S(1)} %get-tuple-element.94), channel_id=1, source_target_pairs={{0,24},{8,0},{16,8},{24,16},{1,25},{9,1},{17,9},{25,17},{2,26},{10... | collective-permute-start | bytes 196616 | tf_op jit(solution)/shard_map/ppermute | solution.py:812
  43.1 4.6 %collective-permute-start.15 = (f32[128,128]{1,0:T(8,128)S(1)}, f32[128,128]{1,0:T(8,128)S(1)}, u32[]{:S(2)}, u32[]{:S(2)}) collective-permute-start(f32[128,128]{1,0:T(8,128)S(1)} %get-tuple-element.95), channel_id=1, source_target_pairs={{0,16},{8,24},{16,0},{24,8},{1,17},{9,25},{17,1},{25,9},{2,18},{10... | collective-permute-start | bytes 196616 | tf_op jit(solution)/shard_map/ppermute | solution.py:812
  44.6 5.0 %collective-permute-start.16 = (f32[128,128]{1,0:T(8,128)S(1)}, f32[128,128]{1,0:T(8,128)S(1)}, u32[]{:S(2)}, u32[]{:S(2)}) collective-permute-start(f32[128,128]{1,0:T(8,128)S(1)} %get-tuple-element.96), channel_id=1, source_target_pairs={{0,8},{8,16},{16,24},{24,0},{1,9},{9,17},{17,25},{25,1},{2,10},{10... | collective-permute-start | bytes 196616 | tf_op jit(solution)/shard_map/ppermute | solution.py:812
  45.2 4.4 %copy-start.3 = (bf16[1024,256]{1,0:T(8,128)(2,1)S(1)}, bf16[1024,256]{1,0:T(8,128)(2,1)}, u32[]{:S(2)}) copy-start(bf16[1024,256]{1,0:T(8,128)(2,1)} %w_score.3) | copy-start | bytes 1572868
  45.2 4.4 %copy-start.4 = (bf16[1,128,1024]{2,1,0:T(8,128)(2,1)S(1)}, bf16[1,128,1024]{2,1,0:T(8,128)(2,1)}, u32[]{:S(2)}) copy-start(bf16[1,128,1024]{2,1,0:T(8,128)(2,1)} %param.9) | copy-start | bytes 786436
  45.2 4.4 %copy-start.5 = (bf16[1,128,1024]{2,1,0:T(8,128)(2,1)S(1)}, bf16[1,128,1024]{2,1,0:T(8,128)(2,1)}, u32[]{:S(2)}) copy-start(bf16[1,128,1024]{2,1,0:T(8,128)(2,1)} %param.16) | copy-start | bytes 786436
  45.2 4.4 %copy-start.6 = (bf16[512,1024]{1,0:T(8,128)(2,1)S(1)}, bf16[512,1024]{1,0:T(8,128)(2,1)}, u32[]{:S(2)}) copy-start(bf16[512,1024]{1,0:T(8,128)(2,1)} %w_out.1) | copy-start | bytes 3145732
  45.2 4.4 %copy-start.10 = (f32[256]{0:T(256)S(1)}, f32[256]{0:T(256)}, u32[]{:S(2)}) copy-start(f32[256]{0:T(256)} %param.15) | copy-start | bytes 3076
  45.2 4.4 %copy-start.11 = (f32[1,128]{1,0:T(1,128)S(1)}, f32[1,128]{1,0:T(1,128)}, u32[]{:S(2)}) copy-start(f32[1,128]{1,0:T(1,128)} %score.1) | copy-start | bytes 1540
  51.6 4.9 %collective-permute-start.18 = (bf16[128,256]{1,0:T(8,128)(2,1)S(1)}, bf16[128,256]{1,0:T(8,128)(2,1)S(1)}, u32[]{:S(2)}, u32[]{:S(2)}) collective-permute-start(bf16[128,256]{1,0:T(8,128)(2,1)S(1)} %get-tuple-element.110), channel_id=1, source_target_pairs={{0,8},{8,16},{16,24},{24,0},{1,9},{9,17},{17,25},{25,1},{2,10},{10... | collective-permute-start | bytes 196616 | tf_op jit(solution)/shard_map/ppermute | solution.py:812
  51.7 5.3 %collective-permute-start.19 = (bf16[128,256]{1,0:T(8,128)(2,1)S(1)}, bf16[128,256]{1,0:T(8,128)(2,1)S(1)}, u32[]{:S(2)}, u32[]{:S(2)}) collective-permute-start(bf16[128,256]{1,0:T(8,128)(2,1)S(1)} %get-tuple-element.111), channel_id=1, source_target_pairs={{0,16},{8,24},{16,0},{24,8},{1,17},{9,25},{17,1},{25,9},{2,18},{10... | collective-permute-start | bytes 196616 | tf_op jit(solution)/shard_map/ppermute | solution.py:812
  53.3 4.3 %collective-permute-start.20 = (bf16[128,256]{1,0:T(8,128)(2,1)S(1)}, bf16[128,256]{1,0:T(8,128)(2,1)S(1)}, u32[]{:S(2)}, u32[]{:S(2)}) collective-permute-start(bf16[128,256]{1,0:T(8,128)(2,1)S(1)} %get-tuple-element.112), channel_id=1, source_target_pairs={{0,24},{8,0},{16,8},{24,16},{1,25},{9,1},{17,9},{25,17},{2,26},{10... | collective-permute-start | bytes 196616 | tf_op jit(solution)/shard_map/ppermute | solution.py:812
  57.6 11.2 %collective-permute-start.24 = (bf16[144,2816]{1,0:T(8,128)(2,1)S(1)}, bf16[144,2816]{1,0:T(8,128)(2,1)S(1)}, u32[]{:S(2)}, u32[]{:S(2)}) collective-permute-start(bf16[144,2816]{1,0:T(8,128)(2,1)S(1)} %get-tuple-element.118.own), channel_id=1, source_target_pairs={{0,1},{1,0},{2,3},{3,2},{4,5},{5,4},{6,7},{7,6},{8,9},{9,8},{10,11... | collective-permute-start | bytes 2433032 | tf_op jit(solution)/shard_map/ppermute | solution.py:816
  60.1 9.8 %collective-permute-start.21 = (bf16[4,128,128]{2,1,0:T(8,128)(2,1)S(1)}, bf16[4,128,128]{2,1,0:T(8,128)(2,1)S(1)}, u32[]{:S(2)}, u32[]{:S(2)}) collective-permute-start(bf16[4,128,128]{2,1,0:T(8,128)(2,1)S(1)} %join.3.refs_0_), channel_id=1, source_target_pairs={{0,2},{2,4},{4,6},{6,0},{1,3},{3,5},{5,7},{7,1},{8,10},{10,12},{12... | collective-permute-start | bytes 393224 | tf_op jit(solution)/shard_map/ppermute | solution.py:812
  60.5 9.6 %collective-permute-start.22 = (bf16[4,128,128]{2,1,0:T(8,128)(2,1)S(1)}, bf16[4,128,128]{2,1,0:T(8,128)(2,1)S(1)}, u32[]{:S(2)}, u32[]{:S(2)}) collective-permute-start(bf16[4,128,128]{2,1,0:T(8,128)(2,1)S(1)} %join.3.refs_0_), channel_id=1, source_target_pairs={{0,4},{2,6},{4,0},{6,2},{1,5},{3,7},{5,1},{7,3},{8,12},{10,14},{12... | collective-permute-start | bytes 393224 | tf_op jit(solution)/shard_map/ppermute | solution.py:812
  63.6 6.5 %collective-permute-start.23 = (bf16[4,128,128]{2,1,0:T(8,128)(2,1)S(1)}, bf16[4,128,128]{2,1,0:T(8,128)(2,1)S(1)}, u32[]{:S(2)}, u32[]{:S(2)}) collective-permute-start(bf16[4,128,128]{2,1,0:T(8,128)(2,1)S(1)} %join.3.refs_0_), channel_id=1, source_target_pairs={{0,6},{2,0},{4,2},{6,4},{1,7},{3,1},{5,3},{7,5},{8,14},{10,8},{12,... | collective-permute-start | bytes 393224 | tf_op jit(solution)/shard_map/ppermute | solution.py:812
  64.4 7.0 %collective-permute-start.25 = (bf16[4,128,128]{2,1,0:T(8,128)(2,1)S(1)}, bf16[4,128,128]{2,1,0:T(8,128)(2,1)S(1)}, u32[]{:S(2)}, u32[]{:S(2)}) collective-permute-start(bf16[4,128,128]{2,1,0:T(8,128)(2,1)S(1)} %join.3.refs_0_), channel_id=1, source_target_pairs={{0,1},{1,0},{2,3},{3,2},{4,5},{5,4},{6,7},{7,6},{8,9},{9,8},{10,11... | collective-permute-start | bytes 393224 | tf_op jit(solution)/shard_map/ppermute | solution.py:816
  70.1 1.8 %collective-permute-start.26 = (bf16[4,128,128]{2,1,0:T(8,128)(2,1)S(1)}, bf16[4,128,128]{2,1,0:T(8,128)(2,1)S(1)}, u32[]{:S(2)}, u32[]{:S(2)}) collective-permute-start(bf16[4,128,128]{2,1,0:T(8,128)(2,1)S(1)} %collective-permute-done.21.refs_1_), channel_id=1, source_target_pairs={{0,1},{1,0},{2,3},{3,2},{4,5},{5,4},{6,7},{7,6},{8,9},{9,8},{10,11... | collective-permute-start | bytes 393224 | tf_op jit(solution)/shard_map/ppermute | solution.py:816
  70.9 1.3 %collective-permute-start.27 = (bf16[4,128,128]{2,1,0:T(8,128)(2,1)S(1)}, bf16[4,128,128]{2,1,0:T(8,128)(2,1)S(1)}, u32[]{:S(2)}, u32[]{:S(2)}) collective-permute-start(bf16[4,128,128]{2,1,0:T(8,128)(2,1)S(1)} %collective-permute-done.22.refs_2_), channel_id=1, source_target_pairs={{0,1},{1,0},{2,3},{3,2},{4,5},{5,4},{6,7},{7,6},{8,9},{9,8},{10,11... | collective-permute-start | bytes 393224 | tf_op jit(solution)/shard_map/ppermute | solution.py:816
  70.9 1.5 %collective-permute-start.28 = (bf16[4,128,128]{2,1,0:T(8,128)(2,1)S(1)}, bf16[4,128,128]{2,1,0:T(8,128)(2,1)S(1)}, u32[]{:S(2)}, u32[]{:S(2)}) collective-permute-start(bf16[4,128,128]{2,1,0:T(8,128)(2,1)S(1)} %collective-permute-done.23.refs_3_), channel_id=1, source_target_pairs={{0,1},{1,0},{2,3},{3,2},{4,5},{5,4},{6,7},{7,6},{8,9},{9,8},{10,11... | collective-permute-start | bytes 393224 | tf_op jit(solution)/shard_map/ppermute | solution.py:816
  78.7 2.1 %copy-start.12 = (bf16[128,384]{1,0:T(8,128)(2,1)}, bf16[128,384]{1,0:T(8,128)(2,1)S(1)}, u32[]{:S(2)}) copy-start(bf16[128,384]{1,0:T(8,128)(2,1)S(1)} %get-tuple-element.135) | copy-start | bytes 294916
  78.7 5.4 %copy-start.14 = (bf16[128,384]{1,0:T(8,128)(2,1)}, bf16[128,384]{1,0:T(8,128)(2,1)S(1)}, u32[]{:S(2)}) copy-start(bf16[128,384]{1,0:T(8,128)(2,1)S(1)} %get-tuple-element.134) | copy-start | bytes 294916
  80.8 2.0 %collective-permute-start.29 = (bf16[32,16,512]{2,1,0:T(8,128)(2,1)S(1)}, bf16[32,16,512]{2,1,0:T(8,128)(2,1)S(1)}, u32[]{:S(2)}, u32[]{:S(2)}) collective-permute-start(bf16[32,16,512]{2,1,0:T(8,128)(2,1)S(1)} %get-tuple-element.132), channel_id=1, source_target_pairs={{0,1},{1,0},{2,3},{3,2},{4,5},{5,4},{6,7},{7,6},{8,9},{9,8},{10,11... | collective-permute-start | bytes 1572872 | tf_op jit(solution)/shard_map/ppermute | solution.py:816
  84.1 6.4 %copy-start.15 = (bf16[128,384]{1,0:T(8,128)(2,1)S(1)}, bf16[128,384]{1,0:T(8,128)(2,1)}, u32[]{:S(2)}) copy-start(bf16[128,384]{1,0:T(8,128)(2,1)} %copy-done.14) | copy-start | bytes 294916
  84.1 9.2 %copy-start.13 = (bf16[128,384]{1,0:T(8,128)(2,1)S(1)}, bf16[128,384]{1,0:T(8,128)(2,1)}, u32[]{:S(2)}) copy-start(bf16[128,384]{1,0:T(8,128)(2,1)} %copy-done.12) | copy-start | bytes 294916
  84.1 31.0 %all-to-all-start = ((bf16[32,48,512]{2,1,0:T(8,128)(2,1)}), bf16[32,48,512]{2,1,0:T(8,128)(2,1)S(1)}, u32[]{:S(2)}, u32[]{:S(2)}) async-start(bf16[32,48,512]{2,1,0:T(8,128)(2,1)} %merge.1), calls=%async_computation | async-start | bytes 3145728 | tf_op jit(solution)/shard_map/all_to_all | solution.py:876
  90.6 21.4 %collective-permute-start.30 = (bf16[128,384]{1,0:T(8,128)(2,1)S(1)}, bf16[128,384]{1,0:T(8,128)(2,1)S(1)}, u32[]{:S(2)}, u32[]{:S(2)}) collective-permute-start(bf16[128,384]{1,0:T(8,128)(2,1)S(1)} %copy-done.15), channel_id=1, source_target_pairs={{0,24},{8,0},{16,8},{24,16},{1,25},{9,1},{17,9},{25,17},{2,26},{10... | collective-permute-start | bytes 294920 | tf_op jit(solution)/shard_map/ppermute | solution.py:812
  93.3 20.1 %collective-permute-start.31 = (bf16[128,384]{1,0:T(8,128)(2,1)S(1)}, bf16[128,384]{1,0:T(8,128)(2,1)S(1)}, u32[]{:S(2)}, u32[]{:S(2)}) collective-permute-start(bf16[128,384]{1,0:T(8,128)(2,1)S(1)} %copy-done.13), channel_id=1, source_target_pairs={{0,16},{8,24},{16,0},{24,8},{1,17},{9,25},{17,1},{25,9},{2,18},{10... | collective-permute-start | bytes 294920 | tf_op jit(solution)/shard_map/ppermute | solution.py:812
  93.8 21.3 %collective-permute-start.32 = (bf16[128,384]{1,0:T(8,128)(2,1)S(1)}, bf16[128,384]{1,0:T(8,128)(2,1)S(1)}, u32[]{:S(2)}, u32[]{:S(2)}) collective-permute-start(bf16[128,384]{1,0:T(8,128)(2,1)S(1)} %get-tuple-element.136), channel_id=1, source_target_pairs={{0,8},{8,16},{16,24},{24,0},{1,9},{9,17},{17,25},{25,1},{2,10},{10... | collective-permute-start | bytes 294920 | tf_op jit(solution)/shard_map/ppermute | solution.py:812
  116.0 16.5 %all-to-all-start.1 = ((bf16[8,96,128]{2,1,0:T(8,128)(2,1)}), bf16[8,96,128]{2,1,0:T(8,128)(2,1)S(1)}, u32[]{:S(2)}, u32[]{:S(2)}) async-start(bf16[8,96,128]{2,1,0:T(8,128)(2,1)} %pack.1), calls=%async_computation.1 | async-start | bytes 393216 | tf_op jit(solution)/shard_map/all_to_all | solution.py:880
  123.9 2.2 %copy-start.1 = (bf16[1024,2048]{1,0:T(8,128)(2,1)S(1)}, bf16[1024,2048]{1,0:T(8,128)(2,1)}, u32[]{:S(2)}) copy-start(bf16[1024,2048]{1,0:T(8,128)(2,1)} %w_ref.1) | copy-start | bytes 12582916
where the time goes:
time: 134 us; the launch traced here: 133 us
  starting transfers between devices  56 us (42%)
  waiting for transfers between devices  38.3 us (29%)
  Pallas kernels  34.7 us (26%)
  local copies, waits for them, and re-layouts  3.15 us (2%)
    ppermute x22, waiting for transfers between devices, shifted(): lax.ppermute(value, axis, [(i, (i + by) % size) for i in range(size)])  31.4 us
    ppermute x22, starting transfers between devices, shifted(): lax.ppermute(value, axis, [(i, (i + by) % size) for i in range(size)])  29.2 us
    ppermute x11, starting transfers between devices, swapped(): lax.ppermute(value, axis, [(i, i ^ bit) for i in range(lax.axis_size(axis...  12.5 us
    all_to_all x1, starting transfers between devices, on_device(): last = lax.all_to_all(pack(partial), 'dp', 0, 0, tiled=True)  7.9 us
    all_to_all x1, starting transfers between devices, on_device(): partial = lax.all_to_all(partial, SEQ, 0, 0, tiled=True)  6.41 us
    pallas_call x1, Pallas kernels, key_grads(): pl.pallas_call(key_kernel, in_specs=[SMEM] * 3 + [VMEM] * 8 + [HBM] * 3 +...  6.28 us
    ppermute x11, waiting for transfers between devices, swapped(): lax.ppermute(value, axis, [(i, i ^ bit) for i in range(lax.axis_size(axis...  4.27 us
    pallas_call x1, Pallas kernels, input_grads(): pl.pallas_call(input_kernel, grid=(4,), in_specs=[SMEM] + [whole((ROWS, 3...  3.8 us
  transfers between devices with their start and end apart: 35, of which 20 were waited for; matrix products, arithmetic and copies ran while one was open for 0% of the time, Pallas kernels for 14%

commit v1 on v0

--- a/solution.py
+++ b/solution.py
@@ -447,22 +447,14 @@
 
 
 def query_kernel(idx, len_ref, tgt_ref, *refs):
-    held, d_refs, (k_hbm, v_hbm), out_refs = refs[0], refs[1:5], refs[5:7], refs[7:11]
-    k_all, v_all, q_own, d_own, total, marks, sems = refs[11:18]
-    copies = copy_all(
-        [
-            pltpu.make_async_copy(k_hbm, k_all, sems.at[0]),
-            pltpu.make_async_copy(v_hbm, v_all, sems.at[1]),
-        ]
-    )
+    held, d_refs, (k_all, v_all), out_refs = refs[0], refs[1:5], refs[5:7], refs[7:11]
+    q_own, d_own, total, marks = refs[11:15]
     hist = Histories(len_ref, tgt_ref)
     for k in range(4):
         q_own[k] = held[k, :, 2 * DH : 3 * DH]
         d_own[k] = d_refs[k][:, 0:DH]
     total[...] = jnp.zeros_like(total)
     lows, highs = set_marks(idx, hist, marks)
-    for copy in copies:
-        copy.wait()
 
     def body(k, t, valid):
         at = tile_at(t)
@@ -482,16 +474,11 @@
 def query_grads(idx, lengths, targets, held, d_att, k_all, v_all):
     return pl.pallas_call(
         query_kernel,
-        in_specs=[SMEM] * 3 + [VMEM] * 5 + [HBM] * 2,
+        in_specs=[SMEM] * 3 + [VMEM] * 7,
         out_specs=[VMEM] * 4,
         out_shape=[shape((ROWS, DH), f32)] * 4,
-        scratch_shapes=[pltpu.VMEM((TOKENS, DH), bf16)] * 2
-        + [pltpu.VMEM((4, ROWS, DH), bf16)] * 2
-        + [
-            pltpu.VMEM((4, ROWS, DH), f32),
-            pltpu.VMEM((2, 4, ROWS, 128), jnp.int32),
-            pltpu.SemaphoreType.DMA((2,)),
-        ],
+        scratch_shapes=[pltpu.VMEM((4, ROWS, DH), bf16)] * 2
+        + [pltpu.VMEM((4, ROWS, DH), f32), pltpu.VMEM((2, 4, ROWS, 128), jnp.int32)],
         compiler_params=PARAMS,
         cost_estimate=cost(3),
         name="query_grads",
@@ -606,31 +593,24 @@
     )(idx, own, got)
 
 
-def weights_kernel(idx, n0, n1, n2, n3, d_pre, keep, send, left):
+def weights_kernel(away, idx, n0, n1, n2, n3, d_pre, out, left):
     for k, ref in enumerate((n0, n1, n2, n3)):
         left[k * ROWS : (k + 1) * ROWS, :] = ref[...]
+    half = idx[2] if away == 0 else 1 - idx[2]
+    right = d_pre[:, pl.ds(pl.multiple_of(half * 256, 256), 256)]
     for n in range(4):
-        part = dot_first(left[:, n * 256 : (n + 1) * 256], d_pre[...])
-        for c in range(2):
-
-            @pl.when(idx[2] == c)
-            def _(c=c, n=n, part=part):
-                for i in range(8):
-                    rows = [part[i * 32 : i * 32 + 16], part[i * 32 + 16 : (i + 1) * 32]]
-                    halves_of = [
-                        jnp.concatenate([v[:, d * 256 : (d + 1) * 256] for v in rows], axis=1)
-                        for d in (c, 1 - c)
-                    ]
-                    keep[n * 8 + i] = halves_of[0]
-                    send[n * 8 + i] = halves_of[1].astype(bf16)
-
-
-def weights(idx, normed, d_pre):
-    return pl.pallas_call(
-        weights_kernel,
+        part = dot_first(left[:, n * 256 : (n + 1) * 256], right)
+        for i in range(8):
+            rows = [part[i * 32 : i * 32 + 16], part[i * 32 + 16 : (i + 1) * 32]]
+            out[n * 8 + i] = jnp.concatenate(rows, axis=1).astype(out.dtype)
+
+
+def weights(away, idx, normed, d_pre):
+    return pl.pallas_call(
+        functools.partial(weights_kernel, away),
         in_specs=[SMEM] + [VMEM] * 5,
-        out_specs=[VMEM] * 2,
-        out_shape=[shape((32, 16, 512), f32), shape((32, 16, 512), bf16)],
+        out_specs=VMEM,
+        out_shape=shape((32, 16, 512), bf16 if away else f32),
         scratch_shapes=[pltpu.VMEM((512, 1024), bf16)],
         compiler_params=PARAMS,
         cost_estimate=cost(0.02),
@@ -692,7 +672,7 @@
         out_specs=VMEM,
         out_shape=shape((8, 96, 128), bf16),
         compiler_params=PARAMS,
-        cost_estimate=cost(0.3),
+        cost_estimate=cost(2),
         name="pack",
     )(value)
 
@@ -722,7 +702,7 @@
             shape((1, 256), f32),
         ],
         compiler_params=PARAMS,
-        cost_estimate=cost(0.3),
+        cost_estimate=cost(1),
         name="last_sum",
     )(value)
 
@@ -768,7 +748,7 @@
         out_shape=shape((ROWS, 1024), bf16),
         scratch_shapes=[pltpu.VMEM((ROWS, 2048), bf16), pltpu.VMEM((ROWS, 1024), f32)],
         compiler_params=PARAMS,
-        cost_estimate=cost(1),
+        cost_estimate=cost(4),
         name="input_grads",
     )(idx, *back, gate, w_in, x, grad, d_mid, w_score)
 
@@ -864,18 +844,18 @@
     d_own = join(d_att, DH)
     late = [shifted(d_own, "y", k) for k in range(1, 4)]
     d_query = query_grads(idx, lengths, targets, held, d_att, k_all, v_all)
-    early = parts(idx, after(acts, d_query[0]), acts_other)
-    d_pieces = with_core([d_own] + after(late, early))
+    d_pieces = with_core([d_own] + after(late, d_query[0]))
     keyed = key_grads(
         idx, lengths, targets, d_pieces, (k_all, v_all, q_all), slope, d_query, d_att
     )
-    keep, send = weights(idx, normed_all, keyed[4])
+    send = weights(1, idx, normed_all, keyed[4])
     got = swapped(send, "core", 1)
+    keep = weights(0, idx, normed_all, after(keyed[4], send))
+    early = parts(idx, after(acts, send), acts_other)
     partial = merge(keep, got, early)
     back, partial = lax.optimization_barrier((keyed[0:4], partial))
     partial = lax.all_to_all(partial, SEQ, 0, 0, tiled=True)
     back = exchange(back, -1)
-    partial = after(partial, back)
     d_x = input_grads(idx, back, gate_full, w_in, x, grad_out[0], d_mid, w_score)
     last = lax.all_to_all(pack(partial), "dp", 0, 0, tiled=True)
     d_w_in, d_w_out, d_w_score, d_head = last_sum(last)

time: 134 us -> 130 us (0.970)
  waiting for transfers between devices: 38.3 us -> 32.2 us
  starting transfers between devices: 56 us -> 58.5 us
    ppermute x22, waiting for transfers between devices: 31.4 us -> 8.28 us  [shifted(): lax.ppermute(value, axis, [(i, (i + by) % size) for i in range(size)])]
    all_to_all x1, waiting for transfers between devices: 0.01 us -> 18.8 us  [on_device(): partial = lax.all_to_all(partial, SEQ, 0, 0, tiled=True)]
    ppermute x22, starting transfers between devices: 29.2 us -> 31.3 us  [shifted(): lax.ppermute(value, axis, [(i, (i + by) % size) for i in range(size)])]
    ppermute x11, waiting for transfers between devices: 4.27 us -> 2.38 us  [swapped(): lax.ppermute(value, axis, [(i, i ^ bit) for i in range(lax.axis_size(axis...]
    pallas_call x2 -> x3, Pallas kernels: 5.54 us -> 5.43 us  [the longest x1 3.35 us: query_grads(): pl.pallas_call(query_kernel, in_specs=[SMEM] * 3 + [VMEM] * 7, out_specs=...]
    unnamed x32 -> x24, local copies, waits for them, and re-layouts: 3.15 us -> 3.14 us
  transfers between devices with their start and end apart: 35 -> 35, of which waited for: 20 -> 14; matrix products, arithmetic and copies ran while one was open for 0% -> 0% of each run, Pallas kernels for 14% -> 21%
where the time goes in v1:
time: 130 us
  starting transfers between devices  58.5 us (45%)
  Pallas kernels  34.6 us (27%)
  waiting for transfers between devices  32.2 us (25%)
  local copies, waits for them, and re-layouts  3.14 us (2%)
    ppermute x22, starting transfers between devices, shifted(): lax.ppermute(value, axis, [(i, (i + by) % size) for i in range(size)])  31.3 us
    all_to_all x1, waiting for transfers between devices, on_device(): partial = lax.all_to_all(partial, SEQ, 0, 0, tiled=True)  18.8 us
    ppermute x11, starting transfers between devices, swapped(): lax.ppermute(value, axis, [(i, i ^ bit) for i in range(lax.axis_size(axis...  12.7 us
    all_to_all x1, starting transfers between devices, on_device(): last = lax.all_to_all(pack(partial), 'dp', 0, 0, tiled=True)  8.58 us
    ppermute x22, waiting for transfers between devices, shifted(): lax.ppermute(value, axis, [(i, (i + by) % size) for i in range(size)])  8.28 us
    pallas_call x1, Pallas kernels, key_grads(): pl.pallas_call(key_kernel, in_specs=[SMEM] * 3 + [VMEM] * 8 + [HBM] * 3 +...  6.29 us
    all_to_all x1, starting transfers between devices, on_device(): partial = lax.all_to_all(partial, SEQ, 0, 0, tiled=True)  5.94 us
    pallas_call x1, Pallas kernels, input_grads(): pl.pallas_call(input_kernel, grid=(4,), in_specs=[SMEM] + [whole((ROWS, 3...  3.79 us
  transfers between devices with their start and end apart: 35, of which 14 were waited for; matrix products, arithmetic and copies ran while one was open for 0% of the time, Pallas kernels for 21%

profile of v1, /device:TPU:1, one launch (start us, length us, event | category | flops | bytes accessed | tf_op | source)
XLA Modules:
  0.0 129.5 jit_solution(17221442839819980118)
XLA Ops:
  0.7 3.4 %project.1 = (bf16[128,1024]{1,0:T(8,128)(2,1)}, bf16[128,384]{1,0:T(8,128)(2,1)}, bf16[128,384]{1,0:T(8,128)(2,1)}, bf16[128,384]{1,0:T(8,128)(2,1)}, bf16[128,384]{1,0:T(8,128)(2,1)}) custom-call(bf16[128,1024]{1,0:T(8,128)(2,1)} %bitcast.10, bf16[1024,2048]{1,0:T(8,128)(2,1)} %w_ref.1), custom_call_target="tpu_custom_call" | custom-call | flops 3449999872 | tf_op jit(solution)/shard_map/project/pallas_call | solution.py:123
  4.0 2.1 %collective-permute-start = (bf16[128,384]{1,0:T(8,128)(2,1)}, bf16[128,384]{1,0:T(8,128)(2,1)S(1)}, u32[]{:S(2)}, u32[]{:S(2)}) collective-permute-start(bf16[128,384]{1,0:T(8,128)(2,1)} %get-tuple-element.74), channel_id=1, source_target_pairs={{0,8},{8,16},{16,24},{24,0},{1,9},{9,17},{17,25},{25,1},{2,10},{10... | collective-permute-start | bytes 294920 | tf_op jit(solution)/shard_map/ppermute | solution.py:792
  6.1 2.5 %collective-permute-start.1 = (bf16[128,384]{1,0:T(8,128)(2,1)}, bf16[128,384]{1,0:T(8,128)(2,1)S(1)}, u32[]{:S(2)}, u32[]{:S(2)}) collective-permute-start(bf16[128,384]{1,0:T(8,128)(2,1)} %get-tuple-element.75), channel_id=1, source_target_pairs={{0,16},{8,24},{16,0},{24,8},{1,17},{9,25},{17,1},{25,9},{2,18},{10... | collective-permute-start | bytes 294920 | tf_op jit(solution)/shard_map/ppermute | solution.py:792
  8.6 1.1 collective-permute-start.2
  9.8 3.1 %collective-permute-done.1.refs_2_ = bf16[128,384]{1,0:T(8,128)(2,1)S(1)} collective-permute-done((bf16[128,384]{1,0:T(8,128)(2,1)}, bf16[128,384]{1,0:T(8,128)(2,1)S(1)}, u32[]{:S(2)}, u32[]{:S(2)}) %collective-permute-start.1) | collective-permute-done | bytes 98336 | tf_op jit(solution)/shard_map/ppermute | solution.py:792
  12.8 0.9 copy-done.7
  13.8 1.4 %collective-permute-start.3 = (bf16[4,128,384]{2,1,0:T(8,128)(2,1)S(1)}, bf16[4,128,384]{2,1,0:T(8,128)(2,1)S(1)}, u32[]{:S(2)}, u32[]{:S(2)}) collective-permute-start(bf16[4,128,384]{2,1,0:T(8,128)(2,1)S(1)} %join.2.refs_0_), channel_id=1, source_target_pairs={{0,2},{2,4},{4,6},{6,0},{1,3},{3,5},{5,7},{7,1},{8,10},{10,12},{12... | collective-permute-start | bytes 1179656 | tf_op jit(solution)/shard_map/ppermute | solution.py:792
  15.2 1.5 %collective-permute-start.4 = (bf16[4,128,384]{2,1,0:T(8,128)(2,1)S(1)}, bf16[4,128,384]{2,1,0:T(8,128)(2,1)S(1)}, u32[]{:S(2)}, u32[]{:S(2)}) collective-permute-start(bf16[4,128,384]{2,1,0:T(8,128)(2,1)S(1)} %join.2.refs_0_), channel_id=1, source_target_pairs={{0,6},{2,0},{4,2},{6,4},{1,7},{3,1},{5,3},{7,5},{8,14},{10,8},{12,... | collective-permute-start | bytes 1179656 | tf_op jit(solution)/shard_map/ppermute | solution.py:792
  16.7 0.8 collective-permute-start.7
  17.5 1.9 %collective-permute-start.8 = (bf16[128,1024]{1,0:T(8,128)(2,1)}, bf16[128,1024]{1,0:T(8,128)(2,1)S(1)}, u32[]{:S(2)}, u32[]{:S(2)}) collective-permute-start(bf16[128,1024]{1,0:T(8,128)(2,1)} %get-tuple-element.104.n0.normed_ref), channel_id=1, source_target_pairs={{0,24},{8,0},{16,8},{24,16},{1,25},{9,1},{17,9},{25,17},{2,26},{10... | collective-permute-start | bytes 786440 | tf_op jit(solution)/shard_map/ppermute | solution.py:792
  19.4 3.4 %collective-permute-start.9 = (bf16[4,128,384]{2,1,0:T(8,128)(2,1)S(1)}, bf16[4,128,384]{2,1,0:T(8,128)(2,1)S(1)}, u32[]{:S(2)}, u32[]{:S(2)}) collective-permute-start(bf16[4,128,384]{2,1,0:T(8,128)(2,1)S(1)} %join.2.refs_0_), channel_id=1, source_target_pairs={{0,1},{1,0},{2,3},{3,2},{4,5},{5,4},{6,7},{7,6},{8,9},{9,8},{10,11... | collective-permute-start | bytes 1179656 | tf_op jit(solution)/shard_map/ppermute | solution.py:796
  22.8 0.6 collective-permute-done.3.back.refs_1_
  23.4 3.3 %collective-permute-start.10 = (bf16[4,128,384]{2,1,0:T(8,128)(2,1)S(1)}, bf16[4,128,384]{2,1,0:T(8,128)(2,1)S(1)}, u32[]{:S(2)}, u32[]{:S(2)}) collective-permute-start(bf16[4,128,384]{2,1,0:T(8,128)(2,1)S(1)} %collective-permute-done.3.back.refs_1_), channel_id=1, source_target_pairs={{0,1},{1,0},{2,3},{3,2},{4,5},{5,4},{6,7},{7,6},{8,9},{9,8},{10,11... | collective-permute-start | bytes 1179656 | tf_op jit(solution)/shard_map/ppermute | solution.py:796
  26.7 0.8 halves.1
  27.5 1.3 collective-permute-start.5
  28.8 1.5 %collective-permute-start.6 = (bf16[2,128,384]{2,1,0:T(8,128)(2,1)}, bf16[2,128,384]{2,1,0:T(8,128)(2,1)S(1)}, u32[]{:S(2)}, u32[]{:S(2)}) collective-permute-start(bf16[2,128,384]{2,1,0:T(8,128)(2,1)} %get-tuple-element.78), channel_id=1, source_target_pairs={{0,6},{2,0},{4,2},{6,4},{1,7},{3,1},{5,3},{7,5},{8,14},{10,8},{12,... | collective-permute-start | bytes 589832 | tf_op jit(solution)/shard_map/ppermute | solution.py:792
  30.4 2.4 %collective-permute-start.17 = (bf16[128,1024]{1,0:T(8,128)(2,1)S(1)}, bf16[128,1024]{1,0:T(8,128)(2,1)S(1)}, u32[]{:S(2)}, u32[]{:S(2)}) collective-permute-start(bf16[128,1024]{1,0:T(8,128)(2,1)S(1)} %copy-done.2), channel_id=1, source_target_pairs={{0,16},{8,24},{16,0},{24,8},{1,17},{9,25},{17,1},{25,9},{2,18},{10... | collective-permute-start | bytes 786440 | tf_op jit(solution)/shard_map/ppermute | solution.py:792
  32.9 3.5 %attend_near.1 = (f32[4,128,128]{2,1,0:T(8,128)S(1)}, bf16[4096,128]{1,0:T(8,128)(2,1)S(1)}, bf16[4096,128]{1,0:T(8,128)(2,1)S(1)}, bf16[4096,128]{1,0:T(8,128)(2,1)S(1)}) custom-call(s32[3]{0:T(128)S(1)} %pad_add_fusion.idx, s32[8]{0:T(128)S(1)} %bitcast.15, s32[8]{0:T(128)S(1)} %bitcast.20, bf16[4,128,384]{2,1,0:T(8,128)(2,1)S(1)} %join.2.refs_0_, ...), custom_call_target="tpu_custom_call" | custom-call | flops 575000000 | tf_op jit(solution)/shard_map/attend_near/pallas_call | solution.py:292
  36.4 1.5 %collective-permute-start.12 = (bf16[2,128,384]{2,1,0:T(8,128)(2,1)S(1)}, bf16[2,128,384]{2,1,0:T(8,128)(2,1)S(1)}, u32[]{:S(2)}, u32[]{:S(2)}) collective-permute-start(bf16[2,128,384]{2,1,0:T(8,128)(2,1)S(1)} %collective-permute-done.5.refs_1_), channel_id=1, source_target_pairs={{0,1},{1,0},{2,3},{3,2},{4,5},{5,4},{6,7},{7,6},{8,9},{9,8},{10,11... | collective-permute-start | bytes 589832 | tf_op jit(solution)/shard_map/ppermute | solution.py:796
  37.8 0.1 collective-permute-start.13
  37.9 1.0 collective-permute-done.12.refs_3_
  38.9 0.4 collective-permute-done.13.refs_4_
  39.3 2.8 %attend_far.1 = (f32[128,128]{1,0:T(8,128)S(1)}, f32[128,128]{1,0:T(8,128)S(1)}, f32[128,128]{1,0:T(8,128)S(1)}, f32[128,128]{1,0:T(8,128)S(1)}, bf16[4096,128]{...) custom-call(s32[3]{0:T(128)S(1)} %pad_add_fusion.idx, ...), custom_call_target="tpu_custom_call", output_to_operand_aliasing={{4}: (9, {}), {5}: (10, {}), {6}: (11, {})} | custom-call | flops 575000000 | tf_op jit(solution)/shard_map/attend_far/pallas_call | solution.py:348
  42.1 1.0 collective-permute-start.14
  43.0 1.5 %collective-permute-start.15 = (f32[128,128]{1,0:T(8,128)S(1)}, f32[128,128]{1,0:T(8,128)S(1)}, u32[]{:S(2)}, u32[]{:S(2)}) collective-permute-start(f32[128,128]{1,0:T(8,128)S(1)} %get-tuple-element.93), channel_id=1, source_target_pairs={{0,16},{8,24},{16,0},{24,8},{1,17},{9,25},{17,1},{25,9},{2,18},{10... | collective-permute-start | bytes 196616 | tf_op jit(solution)/shard_map/ppermute | solution.py:792
  44.6 0.5 gates.1
  45.2 2.1 %slopes.1.refs_11_ = f32[4,128,384]{2,1,0:T(8,128)S(1)} custom-call(s32[3]{0:T(128)S(1)} %pad_add_fusion.idx, bf16[128,1024]{1,0:T(8,128)(2,1)S(1)} %copy-done.2, bf16[128,1024]{1,0:T(8,128)(2,1)S(1)} %collective-permute-done.7.n1, bf16[128,1024]{1,0:T(8,128)(2,1)S(1)} %collective-permute-done.17.n2, bf16[128,1024]{1,0:T(8,128)(2,1)S(1)} %collective-permute-done.8.n3, ...), custom_call_target="tpu_custom_call" | custom-call | flops 575000000 | tf_op jit(solution)/shard_map/slopes/pallas_call | solution.py:177
  47.3 0.4 collective-permute-done.15.a2
  47.7 1.9 %collective-permute-done.16.a3 = f32[128,128]{1,0:T(8,128)S(1)} collective-permute-done((f32[128,128]{1,0:T(8,128)S(1)}, f32[128,128]{1,0:T(8,128)S(1)}, u32[]{:S(2)}, u32[]{:S(2)}) %collective-permute-start.16) | collective-permute-done | bytes 65568 | tf_op jit(solution)/shard_map/ppermute | solution.py:792
  49.6 2.0 %middle.1 = (bf16[128,256]{1,0:T(8,128)(2,1)S(1)}, bf16[128,256]{1,0:T(8,128)(2,1)S(1)}, bf16[128,256]{1,0:T(8,128)(2,1)S(1)}, bf16[128,256]{1,0:T(8,128)(2,1)S(...) custom-call(s32[3]{0:T(128)S(1)} %pad_add_fusion.idx, ...), custom_call_target="tpu_custom_call" | custom-call | flops 575000000 | tf_op jit(solution)/shard_map/middle/pallas_call | solution.py:428
  51.6 0.1 collective-permute-start.18
  51.6 1.7 %collective-permute-start.19 = (bf16[128,256]{1,0:T(8,128)(2,1)S(1)}, bf16[128,256]{1,0:T(8,128)(2,1)S(1)}, u32[]{:S(2)}, u32[]{:S(2)}) collective-permute-start(bf16[128,256]{1,0:T(8,128)(2,1)S(1)} %get-tuple-element.109), channel_id=1, source_target_pairs={{0,16},{8,24},{16,0},{24,8},{1,17},{9,25},{17,1},{25,9},{2,18},{10... | collective-permute-start | bytes 196616 | tf_op jit(solution)/shard_map/ppermute | solution.py:792
  53.3 1.9 %collective-permute-start.20 = (bf16[128,256]{1,0:T(8,128)(2,1)S(1)}, bf16[128,256]{1,0:T(8,128)(2,1)S(1)}, u32[]{:S(2)}, u32[]{:S(2)}) collective-permute-start(bf16[128,256]{1,0:T(8,128)(2,1)S(1)} %get-tuple-element.110), channel_id=1, source_target_pairs={{0,24},{8,0},{16,8},{24,16},{1,25},{9,1},{17,9},{25,17},{2,26},{10... | collective-permute-start | bytes 196616 | tf_op jit(solution)/shard_map/ppermute | solution.py:792
  55.2 1.3 collective-permute-done.18.refs_1_.refs_2_.refs_17_
  56.4 0.4 collective-permute-done.19.refs_2_.refs_3_.refs_18_
  56.9 0.7 collective-permute-done.20.refs_3_.refs_4_.refs_19_
  57.6 0.8 collective-permute-start.21
  58.3 3.2 %collective-permute-start.22 = (bf16[4,128,128]{2,1,0:T(8,128)(2,1)S(1)}, bf16[4,128,128]{2,1,0:T(8,128)(2,1)S(1)}, u32[]{:S(2)}, u32[]{:S(2)}) collective-permute-start(bf16[4,128,128]{2,1,0:T(8,128)(2,1)S(1)} %join.3.refs_0_), channel_id=1, source_target_pairs={{0,4},{2,6},{4,0},{6,2},{1,5},{3,7},{5,1},{7,3},{8,12},{10,14},{12... | collective-permute-start | bytes 393224 | tf_op jit(solution)/shard_map/ppermute | solution.py:792
  61.5 0.8 collective-permute-start.23
  62.3 2.9 %collective-permute-start.24 = (bf16[4,128,128]{2,1,0:T(8,128)(2,1)S(1)}, bf16[4,128,128]{2,1,0:T(8,128)(2,1)S(1)}, u32[]{:S(2)}, u32[]{:S(2)}) collective-permute-start(bf16[4,128,128]{2,1,0:T(8,128)(2,1)S(1)} %join.3.refs_0_), channel_id=1, source_target_pairs={{0,1},{1,0},{2,3},{3,2},{4,5},{5,4},{6,7},{7,6},{8,9},{9,8},{10,11... | collective-permute-start | bytes 393224 | tf_op jit(solution)/shard_map/ppermute | solution.py:796
  65.2 3.3 %query_grads.1 = (f32[128,128]{1,0:T(8,128)S(1)}, f32[128,128]{1,0:T(8,128)S(1)}, f32[128,128]{1,0:T(8,128)S(1)}, f32[128,128]{1,0:T(8,128)S(1)}) custom-call(s32[3]{0:T(128)S(1)} %pad_add_fusion.idx, s32[8]{0:T(128)S(1)} %bitcast.18, s32[8]{0:T(128)S(1)} %bitcast.23, bf16[4,128,384]{2,1,0:T(8,128)(2,1)S(1)} %join.2.refs_0_, ...), custom_call_target="tpu_custom_call" | custom-call | flops 3449999872 | tf_op jit(solution)/shard_map/query_grads/pallas_call | solution.py:475
  68.6 0.6 collective-permute-start.25
  69.2 0.1 collective-permute-start.26
  69.3 0.4 collective-permute-start.27
  69.7 0.5 collective-permute-done.25.refs_5_
  70.2 0.4 collective-permute-done.26.refs_6_
  70.6 0.2 collective-permute-done.27.refs_7_
  70.8 6.3 %key_grads.1 = (bf16[128,384]{1,0:T(8,128)(2,1)S(1)}, bf16[128,384]{1,0:T(8,128)(2,1)S(1)}, bf16[128,384]{1,0:T(8,128)(2,1)S(1)}, bf16[128,384]{1,0:T(8,128)(2,1)S(1)}, bf16[512,512]{1,0:T(8,128)(2,1)S(1)}) custom-call(s32[3]{0:T(128)S(1)} %pad_add_fusion.idx, s32[8]{0:T(128)S(1)} %bitcast.19, s32[8]{0:T(128)S(1)} %bitcast.24, ...), custom_call_target="tpu_custom_call" | custom-call | flops 23000000 | tf_op jit(solution)/shard_map/key_grads/pallas_call | solution.py:546
  77.0 1.0 weights.2
  78.1 0.4 collective-permute-start.28
  78.5 1.0 weights.3.keep
  79.6 1.1 parts.1.early
  80.7 1.3 %merge.1 = bf16[32,48,512]{2,1,0:T(8,128)(2,1)} custom-call(f32[32,16,512]{2,1,0:T(8,128)S(1)} %weights.3.keep, bf16[32,16,512]{2,1,0:T(8,128)(2,1)S(1)} %collective-permute-done.28.got, bf16[32,32,512]{2,1,0:T(8,128)(2,1)S(1)} %parts.1.early), custom_call_target="tpu_custom_call" | custom-call | flops 345000000 | tf_op jit(solution)/shard_map/merge/pallas_call | solution.py:628
  82.0 5.9 %all-to-all-start = ((bf16[32,48,512]{2,1,0:T(8,128)(2,1)}), bf16[32,48,512]{2,1,0:T(8,128)(2,1)S(1)}, u32[]{:S(2)}, u32[]{:S(2)}) async-start(bf16[32,48,512]{2,1,0:T(8,128)(2,1)} %merge.1), calls=%async_computation | async-start | bytes 3145728 | tf_op jit(solution)/shard_map/all_to_all | solution.py:857
  88.0 2.7 %collective-permute-start.30 = (bf16[128,384]{1,0:T(8,128)(2,1)S(1)}, bf16[128,384]{1,0:T(8,128)(2,1)S(1)}, u32[]{:S(2)}, u32[]{:S(2)}) collective-permute-start(bf16[128,384]{1,0:T(8,128)(2,1)S(1)} %get-tuple-element.131), channel_id=1, source_target_pairs={{0,24},{8,0},{16,8},{24,16},{1,25},{9,1},{17,9},{25,17},{2,26},{10... | collective-permute-start | bytes 294920 | tf_op jit(solution)/shard_map/ppermute | solution.py:792
  90.7 0.5 collective-permute-start.31
  91.2 0.6 collective-permute-start.32
  91.8 18.8 %all-to-all-done.ref = bf16[32,48,512]{2,1,0:T(8,128)(2,1)S(1)} async-done(((bf16[32,48,512]{2,1,0:T(8,128)(2,1)}), bf16[32,48,512]{2,1,0:T(8,128)(2,1)S(1)}, u32[]{:S(2)}, u32[]{:S(2)}) %all-to-all-start) | async-done | bytes 1572896 | tf_op jit(solution)/shard_map/all_to_all | solution.py:857
  110.6 0.9 pack.1
  111.5 8.6 %all-to-all-start.1 = ((bf16[8,96,128]{2,1,0:T(8,128)(2,1)}), bf16[8,96,128]{2,1,0:T(8,128)(2,1)S(1)}, u32[]{:S(2)}, u32[]{:S(2)}) async-start(bf16[8,96,128]{2,1,0:T(8,128)(2,1)} %pack.1), calls=%async_computation.1 | async-start | bytes 393216 | tf_op jit(solution)/shard_map/all_to_all | solution.py:860
  120.2 2.2 %copy-done.1 = bf16[1024,2048]{1,0:T(8,128)(2,1)S(1)} copy-done((bf16[1024,2048]{1,0:T(8,128)(2,1)S(1)}, bf16[1024,2048]{1,0:T(8,128)(2,1)}, u32[]{:S(2)}) %copy-start.1) | copy-done | bytes 4194328
  122.3 3.8 %input_grads.1 = bf16[128,1024]{1,0:T(8,128)(2,1)} custom-call(s32[3]{0:T(128)S(1)} %pad_add_fusion.idx, bf16[128,384]{1,0:T(8,128)(2,1)S(1)} %get-tuple-element.130.b0, bf16[128,384]{1,0:T(8,128)(2,1)S(1)} %collective-permute-done.30.b1, bf16[128,384]{1,0:T(8,128)(2,1)S(1)} %collective-permute-done.31.b2, bf16[128,384]{1,0:T(8,128)(2,1)S(1)} %collective-permute-done.32.b3, ...), custom_call_target="tpu_custom_call" | custom-call | flops 4600000000 | tf_op jit(solution)/shard_map/input_grads/pallas_call | solution.py:734
  126.1 2.7 %all-to-all-done.1.ref = bf16[8,96,128]{2,1,0:T(8,128)(2,1)S(1)} async-done(((bf16[8,96,128]{2,1,0:T(8,128)(2,1)}), bf16[8,96,128]{2,1,0:T(8,128)(2,1)S(1)}, u32[]{:S(2)}, u32[]{:S(2)}) %all-to-all-start.1) | async-done | bytes 196640 | tf_op jit(solution)/shard_map/all_to_all | solution.py:860
  128.8 0.7 last_sum.1
  (49 shorter events, 0.3 us)
Async XLA Ops:
  0.6 32.2 %copy-start.8 = (s32[1,8]{1,0:T(1,128)S(1)}, s32[1,8]{1,0:T(1,128)}, u32[]{:S(2)}) copy-start(s32[1,8]{1,0:T(1,128)} %param.10) | copy-start | bytes 100
  0.6 32.2 %copy-start.9 = (s32[1,8]{1,0:T(1,128)S(1)}, s32[1,8]{1,0:T(1,128)}, u32[]{:S(2)}) copy-start(s32[1,8]{1,0:T(1,128)} %param.11) | copy-start | bytes 100
  4.0 26.4 %copy-start.2 = (bf16[128,1024]{1,0:T(8,128)(2,1)S(1)}, bf16[128,1024]{1,0:T(8,128)(2,1)}, u32[]{:S(2)}) copy-start(bf16[128,1024]{1,0:T(8,128)(2,1)} %get-tuple-element.104.n0.normed_ref) | copy-start | bytes 786436
  4.0 5.7 %collective-permute-start = (bf16[128,384]{1,0:T(8,128)(2,1)}, bf16[128,384]{1,0:T(8,128)(2,1)S(1)}, u32[]{:S(2)}, u32[]{:S(2)}) collective-permute-start(bf16[128,384]{1,0:T(8,128)(2,1)} %get-tuple-element.74), channel_id=1, source_target_pairs={{0,8},{8,16},{16,24},{24,0},{1,9},{9,17},{17,25},{25,1},{2,10},{10... | collective-permute-start | bytes 294920 | tf_op jit(solution)/shard_map/ppermute | solution.py:792
  6.1 6.7 %collective-permute-start.1 = (bf16[128,384]{1,0:T(8,128)(2,1)}, bf16[128,384]{1,0:T(8,128)(2,1)S(1)}, u32[]{:S(2)}, u32[]{:S(2)}) collective-permute-start(bf16[128,384]{1,0:T(8,128)(2,1)} %get-tuple-element.75), channel_id=1, source_target_pairs={{0,16},{8,24},{16,0},{24,8},{1,17},{9,25},{17,1},{25,9},{2,18},{10... | collective-permute-start | bytes 294920 | tf_op jit(solution)/shard_map/ppermute | solution.py:792
  8.6 4.2 %collective-permute-start.2 = (bf16[128,384]{1,0:T(8,128)(2,1)}, bf16[128,384]{1,0:T(8,128)(2,1)S(1)}, u32[]{:S(2)}, u32[]{:S(2)}) collective-permute-start(bf16[128,384]{1,0:T(8,128)(2,1)} %get-tuple-element.76), channel_id=1, source_target_pairs={{0,24},{8,0},{16,8},{24,16},{1,25},{9,1},{17,9},{25,17},{2,26},{10... | collective-permute-start | bytes 294920 | tf_op jit(solution)/shard_map/ppermute | solution.py:792
  12.8 0.9 copy-start.7
  13.8 9.6 %collective-permute-start.3 = (bf16[4,128,384]{2,1,0:T(8,128)(2,1)S(1)}, bf16[4,128,384]{2,1,0:T(8,128)(2,1)S(1)}, u32[]{:S(2)}, u32[]{:S(2)}) collective-permute-start(bf16[4,128,384]{2,1,0:T(8,128)(2,1)S(1)} %join.2.refs_0_), channel_id=1, source_target_pairs={{0,2},{2,4},{4,6},{6,0},{1,3},{3,5},{5,7},{7,1},{8,10},{10,12},{12... | collective-permute-start | bytes 1179656 | tf_op jit(solution)/shard_map/ppermute | solution.py:792
  15.2 11.5 %collective-permute-start.4 = (bf16[4,128,384]{2,1,0:T(8,128)(2,1)S(1)}, bf16[4,128,384]{2,1,0:T(8,128)(2,1)S(1)}, u32[]{:S(2)}, u32[]{:S(2)}) collective-permute-start(bf16[4,128,384]{2,1,0:T(8,128)(2,1)S(1)} %join.2.refs_0_), channel_id=1, source_target_pairs={{0,6},{2,0},{4,2},{6,4},{1,7},{3,1},{5,3},{7,5},{8,14},{10,8},{12,... | collective-permute-start | bytes 1179656 | tf_op jit(solution)/shard_map/ppermute | solution.py:792
  16.7 10.8 %collective-permute-start.7 = (bf16[128,1024]{1,0:T(8,128)(2,1)}, bf16[128,1024]{1,0:T(8,128)(2,1)S(1)}, u32[]{:S(2)}, u32[]{:S(2)}) collective-permute-start(bf16[128,1024]{1,0:T(8,128)(2,1)} %get-tuple-element.104.n0.normed_ref), channel_id=1, source_target_pairs={{0,8},{8,16},{16,24},{24,0},{1,9},{9,17},{17,25},{25,1},{2,10},{10... | collective-permute-start | bytes 786440 | tf_op jit(solution)/shard_map/ppermute | solution.py:792
  17.5 11.3 %collective-permute-start.8 = (bf16[128,1024]{1,0:T(8,128)(2,1)}, bf16[128,1024]{1,0:T(8,128)(2,1)S(1)}, u32[]{:S(2)}, u32[]{:S(2)}) collective-permute-start(bf16[128,1024]{1,0:T(8,128)(2,1)} %get-tuple-element.104.n0.normed_ref), channel_id=1, source_target_pairs={{0,24},{8,0},{16,8},{24,16},{1,25},{9,1},{17,9},{25,17},{2,26},{10... | collective-permute-start | bytes 786440 | tf_op jit(solution)/shard_map/ppermute | solution.py:792
  19.4 11.0 %collective-permute-start.9 = (bf16[4,128,384]{2,1,0:T(8,128)(2,1)S(1)}, bf16[4,128,384]{2,1,0:T(8,128)(2,1)S(1)}, u32[]{:S(2)}, u32[]{:S(2)}) collective-permute-start(bf16[4,128,384]{2,1,0:T(8,128)(2,1)S(1)} %join.2.refs_0_), channel_id=1, source_target_pairs={{0,1},{1,0},{2,3},{3,2},{4,5},{5,4},{6,7},{7,6},{8,9},{9,8},{10,11... | collective-permute-start | bytes 1179656 | tf_op jit(solution)/shard_map/ppermute | solution.py:796
  23.4 9.4 %collective-permute-start.10 = (bf16[4,128,384]{2,1,0:T(8,128)(2,1)S(1)}, bf16[4,128,384]{2,1,0:T(8,128)(2,1)S(1)}, u32[]{:S(2)}, u32[]{:S(2)}) collective-permute-start(bf16[4,128,384]{2,1,0:T(8,128)(2,1)S(1)} %collective-permute-done.3.back.refs_1_), channel_id=1, source_target_pairs={{0,1},{1,0},{2,3},{3,2},{4,5},{5,4},{6,7},{7,6},{8,9},{9,8},{10,11... | collective-permute-start | bytes 1179656 | tf_op jit(solution)/shard_map/ppermute | solution.py:796
  26.7 6.1 %collective-permute-start.11 = (bf16[4,128,384]{2,1,0:T(8,128)(2,1)S(1)}, bf16[4,128,384]{2,1,0:T(8,128)(2,1)S(1)}, u32[]{:S(2)}, u32[]{:S(2)}) collective-permute-start(bf16[4,128,384]{2,1,0:T(8,128)(2,1)S(1)} %collective-permute-done.4.ahead.refs_2_), channel_id=1, source_target_pairs={{0,1},{1,0},{2,3},{3,2},{4,5},{5,4},{6,7},{7,6},{8,9},{9,8},{10,11... | collective-permute-start | bytes 1179656 | tf_op jit(solution)/shard_map/ppermute | solution.py:796
  27.5 8.8 %collective-permute-start.5 = (bf16[2,128,384]{2,1,0:T(8,128)(2,1)}, bf16[2,128,384]{2,1,0:T(8,128)(2,1)S(1)}, u32[]{:S(2)}, u32[]{:S(2)}) collective-permute-start(bf16[2,128,384]{2,1,0:T(8,128)(2,1)} %get-tuple-element.77), channel_id=1, source_target_pairs={{0,2},{2,4},{4,6},{6,0},{1,3},{3,5},{5,7},{7,1},{8,10},{10,12},{12... | collective-permute-start | bytes 589832 | tf_op jit(solution)/shard_map/ppermute | solution.py:792
  28.8 7.5 %collective-permute-start.6 = (bf16[2,128,384]{2,1,0:T(8,128)(2,1)}, bf16[2,128,384]{2,1,0:T(8,128)(2,1)S(1)}, u32[]{:S(2)}, u32[]{:S(2)}) collective-permute-start(bf16[2,128,384]{2,1,0:T(8,128)(2,1)} %get-tuple-element.78), channel_id=1, source_target_pairs={{0,6},{2,0},{4,2},{6,4},{1,7},{3,1},{5,3},{7,5},{8,14},{10,8},{12,... | collective-permute-start | bytes 589832 | tf_op jit(solution)/shard_map/ppermute | solution.py:792
  30.4 14.1 %collective-permute-start.17 = (bf16[128,1024]{1,0:T(8,128)(2,1)S(1)}, bf16[128,1024]{1,0:T(8,128)(2,1)S(1)}, u32[]{:S(2)}, u32[]{:S(2)}) collective-permute-start(bf16[128,1024]{1,0:T(8,128)(2,1)S(1)} %copy-done.2), channel_id=1, source_target_pairs={{0,16},{8,24},{16,0},{24,8},{1,17},{9,25},{17,1},{25,9},{2,18},{10... | collective-permute-start | bytes 786440 | tf_op jit(solution)/shard_map/ppermute | solution.py:792
  36.4 8.2 %copy-start = (bf16[1024,2048]{1,0:T(8,128)(2,1)S(1)}, bf16[1024,2048]{1,0:T(8,128)(2,1)}, u32[]{:S(2)}) copy-start(bf16[1024,2048]{1,0:T(8,128)(2,1)} %w_ref.1) | copy-start | bytes 12582916
  36.4 2.5 %collective-permute-start.12 = (bf16[2,128,384]{2,1,0:T(8,128)(2,1)S(1)}, bf16[2,128,384]{2,1,0:T(8,128)(2,1)S(1)}, u32[]{:S(2)}, u32[]{:S(2)}) collective-permute-start(bf16[2,128,384]{2,1,0:T(8,128)(2,1)S(1)} %collective-permute-done.5.refs_1_), channel_id=1, source_target_pairs={{0,1},{1,0},{2,3},{3,2},{4,5},{5,4},{6,7},{7,6},{8,9},{9,8},{10,11... | collective-permute-start | bytes 589832 | tf_op jit(solution)/shard_map/ppermute | solution.py:796
  37.8 1.4 %collective-permute-start.13 = (bf16[2,128,384]{2,1,0:T(8,128)(2,1)S(1)}, bf16[2,128,384]{2,1,0:T(8,128)(2,1)S(1)}, u32[]{:S(2)}, u32[]{:S(2)}) collective-permute-start(bf16[2,128,384]{2,1,0:T(8,128)(2,1)S(1)} %collective-permute-done.6.refs_2_), channel_id=1, source_target_pairs={{0,1},{1,0},{2,3},{3,2},{4,5},{5,4},{6,7},{7,6},{8,9},{9,8},{10,11... | collective-permute-start | bytes 589832 | tf_op jit(solution)/shard_map/ppermute | solution.py:796
  42.1 5.2 %collective-permute-start.14 = (f32[128,128]{1,0:T(8,128)S(1)}, f32[128,128]{1,0:T(8,128)S(1)}, u32[]{:S(2)}, u32[]{:S(2)}) collective-permute-start(f32[128,128]{1,0:T(8,128)S(1)} %get-tuple-element.92), channel_id=1, source_target_pairs={{0,24},{8,0},{16,8},{24,16},{1,25},{9,1},{17,9},{25,17},{2,26},{10... | collective-permute-start | bytes 196616 | tf_op jit(solution)/shard_map/ppermute | solution.py:792
  43.0 4.6 %collective-permute-start.15 = (f32[128,128]{1,0:T(8,128)S(1)}, f32[128,128]{1,0:T(8,128)S(1)}, u32[]{:S(2)}, u32[]{:S(2)}) collective-permute-start(f32[128,128]{1,0:T(8,128)S(1)} %get-tuple-element.93), channel_id=1, source_target_pairs={{0,16},{8,24},{16,0},{24,8},{1,17},{9,25},{17,1},{25,9},{2,18},{10... | collective-permute-start | bytes 196616 | tf_op jit(solution)/shard_map/ppermute | solution.py:792
  44.5 5.0 %collective-permute-start.16 = (f32[128,128]{1,0:T(8,128)S(1)}, f32[128,128]{1,0:T(8,128)S(1)}, u32[]{:S(2)}, u32[]{:S(2)}) collective-permute-start(f32[128,128]{1,0:T(8,128)S(1)} %get-tuple-element.94), channel_id=1, source_target_pairs={{0,8},{8,16},{16,24},{24,0},{1,9},{9,17},{17,25},{25,1},{2,10},{10... | collective-permute-start | bytes 196616 | tf_op jit(solution)/shard_map/ppermute | solution.py:792
  45.1 4.4 %copy-start.3 = (bf16[512,1024]{1,0:T(8,128)(2,1)S(1)}, bf16[512,1024]{1,0:T(8,128)(2,1)}, u32[]{:S(2)}) copy-start(bf16[512,1024]{1,0:T(8,128)(2,1)} %w_out.1) | copy-start | bytes 3145732
  45.1 4.4 %copy-start.4 = (bf16[1024,256]{1,0:T(8,128)(2,1)S(1)}, bf16[1024,256]{1,0:T(8,128)(2,1)}, u32[]{:S(2)}) copy-start(bf16[1024,256]{1,0:T(8,128)(2,1)} %w_score.3) | copy-start | bytes 1572868
  45.1 4.4 %copy-start.5 = (bf16[1,128,1024]{2,1,0:T(8,128)(2,1)S(1)}, bf16[1,128,1024]{2,1,0:T(8,128)(2,1)}, u32[]{:S(2)}) copy-start(bf16[1,128,1024]{2,1,0:T(8,128)(2,1)} %param.9) | copy-start | bytes 786436
  45.1 4.4 %copy-start.6 = (bf16[1,128,1024]{2,1,0:T(8,128)(2,1)S(1)}, bf16[1,128,1024]{2,1,0:T(8,128)(2,1)}, u32[]{:S(2)}) copy-start(bf16[1,128,1024]{2,1,0:T(8,128)(2,1)} %param.16) | copy-start | bytes 786436
  45.1 4.4 %copy-start.10 = (f32[256]{0:T(256)S(1)}, f32[256]{0:T(256)}, u32[]{:S(2)}) copy-start(f32[256]{0:T(256)} %param.15) | copy-start | bytes 3076
  45.2 4.4 %copy-start.11 = (f32[1,128]{1,0:T(1,128)S(1)}, f32[1,128]{1,0:T(1,128)}, u32[]{:S(2)}) copy-start(f32[1,128]{1,0:T(1,128)} %score.1) | copy-start | bytes 1540
  51.6 4.9 %collective-permute-start.18 = (bf16[128,256]{1,0:T(8,128)(2,1)S(1)}, bf16[128,256]{1,0:T(8,128)(2,1)S(1)}, u32[]{:S(2)}, u32[]{:S(2)}) collective-permute-start(bf16[128,256]{1,0:T(8,128)(2,1)S(1)} %get-tuple-element.108), channel_id=1, source_target_pairs={{0,8},{8,16},{16,24},{24,0},{1,9},{9,17},{17,25},{25,1},{2,10},{10... | collective-permute-start | bytes 196616 | tf_op jit(solution)/shard_map/ppermute | solution.py:792
  51.6 5.2 %collective-permute-start.19 = (bf16[128,256]{1,0:T(8,128)(2,1)S(1)}, bf16[128,256]{1,0:T(8,128)(2,1)S(1)}, u32[]{:S(2)}, u32[]{:S(2)}) collective-permute-start(bf16[128,256]{1,0:T(8,128)(2,1)S(1)} %get-tuple-element.109), channel_id=1, source_target_pairs={{0,16},{8,24},{16,0},{24,8},{1,17},{9,25},{17,1},{25,9},{2,18},{10... | collective-permute-start | bytes 196616 | tf_op jit(solution)/shard_map/ppermute | solution.py:792
  53.3 4.2 %collective-permute-start.20 = (bf16[128,256]{1,0:T(8,128)(2,1)S(1)}, bf16[128,256]{1,0:T(8,128)(2,1)S(1)}, u32[]{:S(2)}, u32[]{:S(2)}) collective-permute-start(bf16[128,256]{1,0:T(8,128)(2,1)S(1)} %get-tuple-element.110), channel_id=1, source_target_pairs={{0,24},{8,0},{16,8},{24,16},{1,25},{9,1},{17,9},{25,17},{2,26},{10... | collective-permute-start | bytes 196616 | tf_op jit(solution)/shard_map/ppermute | solution.py:792
  57.6 11.0 %collective-permute-start.21 = (bf16[4,128,128]{2,1,0:T(8,128)(2,1)S(1)}, bf16[4,128,128]{2,1,0:T(8,128)(2,1)S(1)}, u32[]{:S(2)}, u32[]{:S(2)}) collective-permute-start(bf16[4,128,128]{2,1,0:T(8,128)(2,1)S(1)} %join.3.refs_0_), channel_id=1, source_target_pairs={{0,2},{2,4},{4,6},{6,0},{1,3},{3,5},{5,7},{7,1},{8,10},{10,12},{12... | collective-permute-start | bytes 393224 | tf_op jit(solution)/shard_map/ppermute | solution.py:792
  58.3 10.3 %collective-permute-start.22 = (bf16[4,128,128]{2,1,0:T(8,128)(2,1)S(1)}, bf16[4,128,128]{2,1,0:T(8,128)(2,1)S(1)}, u32[]{:S(2)}, u32[]{:S(2)}) collective-permute-start(bf16[4,128,128]{2,1,0:T(8,128)(2,1)S(1)} %join.3.refs_0_), channel_id=1, source_target_pairs={{0,4},{2,6},{4,0},{6,2},{1,5},{3,7},{5,1},{7,3},{8,12},{10,14},{12... | collective-permute-start | bytes 393224 | tf_op jit(solution)/shard_map/ppermute | solution.py:792
  61.5 7.1 %collective-permute-start.23 = (bf16[4,128,128]{2,1,0:T(8,128)(2,1)S(1)}, bf16[4,128,128]{2,1,0:T(8,128)(2,1)S(1)}, u32[]{:S(2)}, u32[]{:S(2)}) collective-permute-start(bf16[4,128,128]{2,1,0:T(8,128)(2,1)S(1)} %join.3.refs_0_), channel_id=1, source_target_pairs={{0,6},{2,0},{4,2},{6,4},{1,7},{3,1},{5,3},{7,5},{8,14},{10,8},{12,... | collective-permute-start | bytes 393224 | tf_op jit(solution)/shard_map/ppermute | solution.py:792
  62.3 7.4 %collective-permute-start.24 = (bf16[4,128,128]{2,1,0:T(8,128)(2,1)S(1)}, bf16[4,128,128]{2,1,0:T(8,128)(2,1)S(1)}, u32[]{:S(2)}, u32[]{:S(2)}) collective-permute-start(bf16[4,128,128]{2,1,0:T(8,128)(2,1)S(1)} %join.3.refs_0_), channel_id=1, source_target_pairs={{0,1},{1,0},{2,3},{3,2},{4,5},{5,4},{6,7},{7,6},{8,9},{9,8},{10,11... | collective-permute-start | bytes 393224 | tf_op jit(solution)/shard_map/ppermute | solution.py:796
  65.2 14.3 %collective-permute-start.29 = (bf16[144,2816]{1,0:T(8,128)(2,1)S(1)}, bf16[144,2816]{1,0:T(8,128)(2,1)S(1)}, u32[]{:S(2)}, u32[]{:S(2)}) collective-permute-start(bf16[144,2816]{1,0:T(8,128)(2,1)S(1)} %get-tuple-element.129.own), channel_id=1, source_target_pairs={{0,1},{1,0},{2,3},{3,2},{4,5},{5,4},{6,7},{7,6},{8,9},{9,8},{10,11... | collective-permute-start | bytes 2433032 | tf_op jit(solution)/shard_map/ppermute | solution.py:796
  68.6 1.6 %collective-permute-start.25 = (bf16[4,128,128]{2,1,0:T(8,128)(2,1)S(1)}, bf16[4,128,128]{2,1,0:T(8,128)(2,1)S(1)}, u32[]{:S(2)}, u32[]{:S(2)}) collective-permute-start(bf16[4,128,128]{2,1,0:T(8,128)(2,1)S(1)} %collective-permute-done.21.refs_1_), channel_id=1, source_target_pairs={{0,1},{1,0},{2,3},{3,2},{4,5},{5,4},{6,7},{7,6},{8,9},{9,8},{10,11... | collective-permute-start | bytes 393224 | tf_op jit(solution)/shard_map/ppermute | solution.py:796
  69.2 1.3 %collective-permute-start.26 = (bf16[4,128,128]{2,1,0:T(8,128)(2,1)S(1)}, bf16[4,128,128]{2,1,0:T(8,128)(2,1)S(1)}, u32[]{:S(2)}, u32[]{:S(2)}) collective-permute-start(bf16[4,128,128]{2,1,0:T(8,128)(2,1)S(1)} %collective-permute-done.22.refs_2_), channel_id=1, source_target_pairs={{0,1},{1,0},{2,3},{3,2},{4,5},{5,4},{6,7},{7,6},{8,9},{9,8},{10,11... | collective-permute-start | bytes 393224 | tf_op jit(solution)/shard_map/ppermute | solution.py:796
  69.3 1.4 %collective-permute-start.27 = (bf16[4,128,128]{2,1,0:T(8,128)(2,1)S(1)}, bf16[4,128,128]{2,1,0:T(8,128)(2,1)S(1)}, u32[]{:S(2)}, u32[]{:S(2)}) collective-permute-start(bf16[4,128,128]{2,1,0:T(8,128)(2,1)S(1)} %collective-permute-done.23.refs_3_), channel_id=1, source_target_pairs={{0,1},{1,0},{2,3},{3,2},{4,5},{5,4},{6,7},{7,6},{8,9},{9,8},{10,11... | collective-permute-start | bytes 393224 | tf_op jit(solution)/shard_map/ppermute | solution.py:796
  78.1 2.6 %collective-permute-start.28 = (bf16[32,16,512]{2,1,0:T(8,128)(2,1)S(1)}, bf16[32,16,512]{2,1,0:T(8,128)(2,1)S(1)}, u32[]{:S(2)}, u32[]{:S(2)}) collective-permute-start(bf16[32,16,512]{2,1,0:T(8,128)(2,1)S(1)} %weights.2), channel_id=1, source_target_pairs={{0,1},{1,0},{2,3},{3,2},{4,5},{5,4},{6,7},{7,6},{8,9},{9,8},{10,11... | collective-permute-start | bytes 1572872 | tf_op jit(solution)/shard_map/ppermute | solution.py:796
  82.0 28.6 %all-to-all-start = ((bf16[32,48,512]{2,1,0:T(8,128)(2,1)}), bf16[32,48,512]{2,1,0:T(8,128)(2,1)S(1)}, u32[]{:S(2)}, u32[]{:S(2)}) async-start(bf16[32,48,512]{2,1,0:T(8,128)(2,1)} %merge.1), calls=%async_computation | async-start | bytes 3145728 | tf_op jit(solution)/shard_map/all_to_all | solution.py:857
  88.0 32.2 %collective-permute-start.30 = (bf16[128,384]{1,0:T(8,128)(2,1)S(1)}, bf16[128,384]{1,0:T(8,128)(2,1)S(1)}, u32[]{:S(2)}, u32[]{:S(2)}) collective-permute-start(bf16[128,384]{1,0:T(8,128)(2,1)S(1)} %get-tuple-element.131), channel_id=1, source_target_pairs={{0,24},{8,0},{16,8},{24,16},{1,25},{9,1},{17,9},{25,17},{2,26},{10... | collective-permute-start | bytes 294920 | tf_op jit(solution)/shard_map/ppermute | solution.py:792
  90.7 29.4 %collective-permute-start.31 = (bf16[128,384]{1,0:T(8,128)(2,1)S(1)}, bf16[128,384]{1,0:T(8,128)(2,1)S(1)}, u32[]{:S(2)}, u32[]{:S(2)}) collective-permute-start(bf16[128,384]{1,0:T(8,128)(2,1)S(1)} %get-tuple-element.132), channel_id=1, source_target_pairs={{0,16},{8,24},{16,0},{24,8},{1,17},{9,25},{17,1},{25,9},{2,18},{10... | collective-permute-start | bytes 294920 | tf_op jit(solution)/shard_map/ppermute | solution.py:792
  91.2 28.9 %collective-permute-start.32 = (bf16[128,384]{1,0:T(8,128)(2,1)S(1)}, bf16[128,384]{1,0:T(8,128)(2,1)S(1)}, u32[]{:S(2)}, u32[]{:S(2)}) collective-permute-start(bf16[128,384]{1,0:T(8,128)(2,1)S(1)} %get-tuple-element.133), channel_id=1, source_target_pairs={{0,8},{8,16},{16,24},{24,0},{1,9},{9,17},{17,25},{25,1},{2,10},{10... | collective-permute-start | bytes 294920 | tf_op jit(solution)/shard_map/ppermute | solution.py:792
  111.5 17.3 %all-to-all-start.1 = ((bf16[8,96,128]{2,1,0:T(8,128)(2,1)}), bf16[8,96,128]{2,1,0:T(8,128)(2,1)S(1)}, u32[]{:S(2)}, u32[]{:S(2)}) async-start(bf16[8,96,128]{2,1,0:T(8,128)(2,1)} %pack.1), calls=%async_computation.1 | async-start | bytes 393216 | tf_op jit(solution)/shard_map/all_to_all | solution.py:860
  120.1 2.2 %copy-start.1 = (bf16[1024,2048]{1,0:T(8,128)(2,1)S(1)}, bf16[1024,2048]{1,0:T(8,128)(2,1)}, u32[]{:S(2)}) copy-start(bf16[1024,2048]{1,0:T(8,128)(2,1)} %w_ref.1) | copy-start | bytes 12582916

commit v2 on v1

--- a/solution.py
+++ b/solution.py
@@ -369,16 +369,17 @@
     return high, (head - high).astype(bf16).astype(f32)
 
 
-def with_head(rows, head, count):
-    high, low = two_of(head)
-    width = ACTS if rows is None else rows.shape[1]
-    line = jnp.concatenate([high, low, jnp.zeros((1, width - 512), f32)], axis=1)
-    line = jnp.concatenate([line, jnp.zeros((count - 1, width), f32)], axis=0)
-    return (line if rows is None else jnp.concatenate([rows, line], axis=0)).astype(bf16)
-
-
-def head_of(value, row):
-    return value[row : row + 1, 0:256] + value[row : row + 1, 256:512]
+def head_rows(head):
+    return jnp.concatenate(list(two_of(head)) + [jnp.zeros((14, 256), f32)], axis=0).astype(bf16)
+
+
+def head_of(rows):
+    rows = rows.astype(f32)
+    return rows[0:1] + rows[1:2]
+
+
+def even_sum(v):
+    return (v[0] + v[2]) + (v[1] + v[3])
 
 
 ACTS = 512 + 1024 + 1024 + 256
@@ -407,7 +408,6 @@
     weight = jnp.where(pos >= hist.pick(hist.firsts, pos), column, 0.0)
     sigma = sigmoid(mid)
     head_part = jnp.sum(weight * (mid * sigma), axis=0, keepdims=True)
-    acts[ROWS : ROWS + 16, :] = with_head(None, head_part, 16)
     d_mid = (weight * head[...] * (sigma * (1.0 + mid * (1.0 - sigma)))).astype(bf16)
     acts[0:ROWS, 2560:2816] = d_mid
     mid_ref[...] = d_mid
@@ -419,8 +419,9 @@
     g_full[...] = work[...].astype(bf16)
     for k in range(4):
         at = pl.ds(pl.multiple_of(lax.rem(idx[0] + k, 4) * DH, DH), DH)
-        d_refs[k][:, 0:DH] = att[:, at].astype(bf16)
-        d_refs[k][:, DH : 2 * DH] = work[:, at].astype(bf16)
+        d_refs[k][0:ROWS, 0:DH] = att[:, at].astype(bf16)
+        d_refs[k][0:ROWS, DH : 2 * DH] = work[:, at].astype(bf16)
+        d_refs[k][ROWS : ROWS + 16, :] = head_rows(head_part)
 
 
 def middle(idx, lengths, targets, attended, gate, slope, x, w_out, w_score, head, grad, score):
@@ -429,10 +430,10 @@
         middle_kernel,
         in_specs=[SMEM] * 3 + [VMEM] * 12,
         out_specs=[VMEM] * 7,
-        out_shape=[shape((ROWS, 2 * DH), bf16)] * 4
+        out_shape=[shape((ROWS + 16, 2 * DH), bf16)] * 4
         + [
             shape((ROWS, width), bf16),
-            shape((ROWS + 16, ACTS), bf16),
+            shape((ROWS, ACTS), bf16),
             shape((ROWS, 256), bf16),
         ],
         scratch_shapes=[pltpu.VMEM((ROWS, width), f32)] * 2,
@@ -452,7 +453,7 @@
     hist = Histories(len_ref, tgt_ref)
     for k in range(4):
         q_own[k] = held[k, :, 2 * DH : 3 * DH]
-        d_own[k] = d_refs[k][:, 0:DH]
+        d_own[k] = d_refs[k][0:ROWS, 0:DH]
     total[...] = jnp.zeros_like(total)
     lows, highs = set_marks(idx, hist, marks)
 
@@ -487,8 +488,8 @@
 
 def key_kernel(idx, len_ref, tgt_ref, *refs):
     d_pieces, (k_hbm, v_hbm, q_hbm, slope_ref) = refs[0:8], refs[8:12]
-    dq_refs, d_refs, back_refs, all_ref = refs[12:16], refs[16:20], refs[20:24], refs[24]
-    q_all, d_all, k_own, v_own, d_key, d_value, sems = refs[25:32]
+    dq_refs, d_refs, back_refs, (all_ref, head_ref) = refs[12:16], refs[16:20], refs[20:24], refs[24:26]
+    q_all, d_all, k_own, v_own, d_key, d_value, sems = refs[26:33]
     copies = [pltpu.make_async_copy(q_hbm, q_all, sems.at[8])]
     for k in range(4):
         at = pl.ds(pl.multiple_of(block_of(idx, k) * ROWS, ROWS), ROWS)
@@ -496,7 +497,16 @@
         copies.append(pltpu.make_async_copy(v_hbm.at[at, :], v_own.at[k], sems.at[k + 4]))
     copy_all(copies)
     hist = Histories(len_ref, tgt_ref)
-    assemble(idx, d_pieces, WHOLE, [(d_all, 0)])
+    heads = []
+    for j, piece in enumerate(d_pieces):
+        at_core = 1 - idx[2] if j >= 4 else idx[2]
+        for k in range(4):
+            block = lax.rem(idx[0] - k + 4, 4) * 8 + lax.rem(idx[1] - j % 4 + 4, 4) * 2 + at_core
+            where = pl.ds(pl.multiple_of(block * ROWS, ROWS), ROWS)
+            d_all[where, :] = piece[k * ROWS : (k + 1) * ROWS, :]
+        rows = [piece[4 * ROWS + i * 16 : 4 * ROWS + (i + 1) * 16, :] for i in range(2)]
+        heads.append(jnp.concatenate([head_of(row) for row in rows], axis=1))
+    head_ref[...] = even_sum(heads[0:4]) + even_sum(heads[4:8])
     d_key[...] = jnp.zeros_like(d_key)
     d_value[...] = jnp.zeros_like(d_value)
     row = lax.broadcasted_iota(jnp.int32, (ROWS, TILE), 0)
@@ -536,7 +546,7 @@
         back_refs[k][:, DH : 2 * DH] = d_q
         back_refs[k][:, 2 * DH : 3 * DH] = d_k
         at = pl.ds(k * ROWS, ROWS)
-        all_ref[at, 0:DH] = d_refs[k][:, DH : 2 * DH]
+        all_ref[at, 0:DH] = d_refs[k][0:ROWS, DH : 2 * DH]
         all_ref[at, DH : 2 * DH] = d_v
         all_ref[at, 2 * DH : 3 * DH] = d_q
         all_ref[at, 3 * DH : 4 * DH] = d_k
@@ -546,8 +556,9 @@
     return pl.pallas_call(
         key_kernel,
         in_specs=[SMEM] * 3 + [VMEM] * 8 + [HBM] * 3 + [VMEM] * 9,
-        out_specs=[VMEM] * 5,
-        out_shape=[shape((ROWS, 3 * DH), bf16)] * 4 + [shape((4 * ROWS, 4 * DH), bf16)],
+        out_specs=[VMEM] * 6,
+        out_shape=[shape((ROWS, 3 * DH), bf16)] * 4
+        + [shape((4 * ROWS, 4 * DH), bf16), shape((1, 256), f32)],
         scratch_shapes=[pltpu.VMEM((TOKENS, DH), bf16)] * 2
         + [pltpu.VMEM((4, ROWS, DH), bf16)] * 2
         + [pltpu.VMEM((4, ROWS, DH), f32)] * 2
@@ -563,20 +574,17 @@
 
 
 def parts_kernel(idx, own, got, out, rows):
-    rows[0:ROWS, :] = own[0:ROWS, :]
-    rows[ROWS : 2 * ROWS, :] = got[0:ROWS, :]
+    rows[0:ROWS, :] = own[...]
+    rows[ROWS : 2 * ROWS, :] = got[...]
     total = rows[:, pl.ds(pl.multiple_of(512 + idx[2] * 512, 512), 512)]
     d_mid = rows[:, pl.ds(pl.multiple_of(2560 + idx[2] * 128, 128), 128)]
-    head = [head_of(ref[ROWS : ROWS + 16, 0:512].astype(f32), 0) for ref in (own, got)]
-    high, low = two_of(head[0] + head[1])
-    line = jnp.concatenate([high, low], axis=1)
-    line = jnp.concatenate([line, jnp.zeros((7, 512), f32)], axis=0)
     for x in range(4):
         part = dot_first(rows[:, x * 128 : (x + 1) * 128], total)
         score = dot_first(rows[:, 1536 + x * 256 : 1792 + x * 256], d_mid)
         for m in range(8):
-            last = [score[m * 32 + j * 8 : m * 32 + (j + 1) * 8] for j in range(4)]
-            block = [part[m * 16 : (m + 1) * 16], jnp.concatenate(last, axis=1), line]
+            own_part = part[m * 16 : (m + 1) * 16]
+            last = [score[m * 32 + j * 16 : m * 32 + (j + 1) * 16] for j in range(2)]
+            block = [own_part[:, 0:256], own_part[:, 256:512], jnp.concatenate(last, axis=1)]
             out[x * 8 + m] = jnp.concatenate(block, axis=0).astype(bf16)
 
 
@@ -585,7 +593,7 @@
         parts_kernel,
         in_specs=[SMEM] + [VMEM] * 2,
         out_specs=VMEM,
-        out_shape=shape((32, 32, 512), bf16),
+        out_shape=shape((32, 48, 256), bf16),
         scratch_shapes=[pltpu.VMEM((2 * ROWS, ACTS), bf16)],
         compiler_params=PARAMS,
         cost_estimate=cost(0.3),
@@ -601,8 +609,7 @@
     for n in range(4):
         part = dot_first(left[:, n * 256 : (n + 1) * 256], right)
         for i in range(8):
-            rows = [part[i * 32 : i * 32 + 16], part[i * 32 + 16 : (i + 1) * 32]]
-            out[n * 8 + i] = jnp.concatenate(rows, axis=1).astype(out.dtype)
+            out[n * 8 + i] = part[i * 32 : (i + 1) * 32].astype(out.dtype)
 
 
 def weights(away, idx, normed, d_pre):
@@ -610,7 +617,7 @@
         functools.partial(weights_kernel, away),
         in_specs=[SMEM] + [VMEM] * 5,
         out_specs=VMEM,
-        out_shape=shape((32, 16, 512), bf16 if away else f32),
+        out_shape=shape((32, 32, 256), bf16 if away else f32),
         scratch_shapes=[pltpu.VMEM((512, 1024), bf16)],
         compiler_params=PARAMS,
         cost_estimate=cost(0.02),
@@ -620,8 +627,8 @@
 
 def merge_kernel(keep, got, early, out):
     for n in range(32):
-        out[n, 0:16, :] = (keep[n] + got[n].astype(f32)).astype(bf16)
-        out[n, 16:48, :] = early[n]
+        out[n, 0:32, :] = (keep[n] + got[n].astype(f32)).astype(bf16)
+        out[n, 32:80, :] = early[n]
 
 
 def merge(keep, got, early):
@@ -629,52 +636,53 @@
         merge_kernel,
         in_specs=[VMEM] * 3,
         out_specs=VMEM,
-        out_shape=shape((32, 48, 512), bf16),
+        out_shape=shape((32, 80, 256), bf16),
         compiler_params=PARAMS,
         cost_estimate=cost(0.3),
         name="merge",
     )(keep, got, early)
 
 
-def pack_kernel(ref, out_ref):
+def pack_kernel(ref, head_ref, out_ref):
     for c in range(2):
         for h in range(HEADS):
-            total = ref[h * 8 + c, 0:16, :].astype(f32)
+            total = ref[h * 8 + c, 0:32, :].astype(f32)
             for n in range(1, 4):
-                total = total + ref[h * 8 + n * 2 + c, 0:16, :].astype(f32)
+                total = total + ref[h * 8 + n * 2 + c, 0:32, :].astype(f32)
             for i in range(2):
                 z, half = divmod((c * 2 + i) * HEADS + h, 2)
-                rows = [total[:, r * 256 + i * 128 : r * 256 + (i + 1) * 128] for r in range(2)]
-                rows = jnp.concatenate(rows, axis=0).astype(bf16)
+                rows = total[:, i * 128 : (i + 1) * 128].astype(bf16)
                 out_ref[z, half * 32 : (half + 1) * 32, :] = rows
     sums = []
     for c in range(2):
-        total = ref[c, 16:48, :].astype(f32)
-        head = head_of(total, 24)
+        total = ref[c, 32:80, :].astype(f32)
         for n in range(c + 2, 32, 2):
-            part = ref[n, 16:48, :].astype(f32)
-            total, head = total + part, head + head_of(part, 24)
+            total = total + ref[n, 32:80, :].astype(f32)
         sums.append(total)
-    high, low = two_of(head)
+    high, low = two_of(head_ref[...])
     head = [high[:, 0:128], high[:, 128:256], low[:, 0:128], low[:, 128:256]]
     head = jnp.concatenate(head + [jnp.zeros((4, 128), f32)], axis=0)
     for z in range(8):
-        total, at = sums[z // 4], z % 4 * 128
-        score = [total[16:24, j * 128 + z % 4 * 32 : j * 128 + z % 4 * 32 + 32] for j in range(4)]
-        rows = [total[0:16, at : at + 128], jnp.concatenate(score, axis=1), head]
+        total, first, at = sums[z // 4], z % 4 // 2 * 16, z % 2 * 128
+        score = [
+            total[32 + i * 8 : 40 + i * 8, j * 128 + z % 4 * 32 : j * 128 + z % 4 * 32 + 32]
+            for j in range(2)
+            for i in range(2)
+        ]
+        rows = [total[first : first + 16, at : at + 128], jnp.concatenate(score, axis=1), head]
         out_ref[z, 64:96, :] = jnp.concatenate(rows, axis=0).astype(bf16)
 
 
-def pack(value):
+def pack(value, head):
     return pl.pallas_call(
         pack_kernel,
-        in_specs=[VMEM],
+        in_specs=[VMEM] * 2,
         out_specs=VMEM,
         out_shape=shape((8, 96, 128), bf16),
         compiler_params=PARAMS,
         cost_estimate=cost(2),
         name="pack",
-    )(value)
+    )(value, head)
 
 
 def last_kernel(ref, in_ref, out_ref, score_ref, head_ref):
@@ -768,6 +776,27 @@
         cost_estimate=cost(0.1),
         name="join",
     )(*arrays)
+
+
+def own_kernel(d0, d1, d2, d3, out):
+    refs = (d0, d1, d2, d3)
+    for k in range(4):
+        out[k * ROWS : (k + 1) * ROWS, :] = refs[k][0:ROWS, 0:DH]
+    rows = head_rows(even_sum([head_of(ref[ROWS : ROWS + 16, :]) for ref in refs]))
+    out[4 * ROWS : 4 * ROWS + 16, :] = rows[:, 0:DH]
+    out[4 * ROWS + 16 : 4 * ROWS + 32, :] = rows[:, DH : 2 * DH]
+
+
+def own_rows(d_att):
+    return pl.pallas_call(
+        own_kernel,
+        in_specs=[VMEM] * 4,
+        out_specs=VMEM,
+        out_shape=shape((4 * ROWS + 32, DH), bf16),
+        compiler_params=PARAMS,
+        cost_estimate=cost(0.1),
+        name="own_rows",
+    )(*d_att)
 
 
 def halves_kernel(back, ahead, low, high):
@@ -841,7 +870,7 @@
     gate_full, acts, d_mid = mid[4:7]
     d_att = exchange(mid[0:4], 1)
     acts_other = swapped(after(acts, d_att), "core", 1)
-    d_own = join(d_att, DH)
+    d_own = own_rows(d_att)
     late = [shifted(d_own, "y", k) for k in range(1, 4)]
     d_query = query_grads(idx, lengths, targets, held, d_att, k_all, v_all)
     d_pieces = with_core([d_own] + after(late, d_query[0]))
@@ -857,7 +886,7 @@
     partial = lax.all_to_all(partial, SEQ, 0, 0, tiled=True)
     back = exchange(back, -1)
     d_x = input_grads(idx, back, gate_full, w_in, x, grad_out[0], d_mid, w_score)
-    last = lax.all_to_all(pack(partial), "dp", 0, 0, tiled=True)
+    last = lax.all_to_all(pack(partial, keyed[5]), "dp", 0, 0, tiled=True)
     d_w_in, d_w_out, d_w_score, d_head = last_sum(last)
     return d_x[None], d_w_in, d_w_out, d_w_score, d_head.reshape(256)
 

time: 130 us -> 131 us (level)
    pallas_call x1, Pallas kernels: 6.29 us -> 4.37 us  [key_grads(): pl.pallas_call(key_kernel, in_specs=[SMEM] * 3 + [VMEM] * 8 + [HBM] * 3 +...]
    all_to_all x1, starting transfers between devices: 5.94 us -> 7.78 us  [on_device(): partial = lax.all_to_all(partial, SEQ, 0, 0, tiled=True)]
    all_to_all x1, waiting for transfers between devices: 2.71 us -> 4.26 us  [on_device(): last = lax.all_to_all(pack(partial, keyed[5]), 'dp', 0, 0, tiled=True)]
  transfers between devices with their start and end apart: 35 -> 35, of which waited for: 14 -> 14; matrix products, arithmetic and copies ran while one was open for 0% -> 0% of each run, Pallas kernels for 21% -> 20%
where the time goes in v2:
time: 131 us; the launch traced here: 130 us
  starting transfers between devices  59.3 us (45%)
  Pallas kernels  33.4 us (25%)
  waiting for transfers between devices  33.2 us (25%)
  local copies, waits for them, and re-layouts  3.14 us (2%)
    ppermute x22, starting transfers between devices, shifted(): lax.ppermute(value, axis, [(i, (i + by) % size) for i in range(size)])  30.9 us
    all_to_all x1, waiting for transfers between devices, on_device(): partial = lax.all_to_all(partial, SEQ, 0, 0, tiled=True)  18.1 us
    ppermute x11, starting transfers between devices, swapped(): lax.ppermute(value, axis, [(i, i ^ bit) for i in range(lax.axis_size(axis...  12.9 us
    ppermute x22, waiting for transfers between devices, shifted(): lax.ppermute(value, axis, [(i, (i + by) % size) for i in range(size)])  8.46 us
    all_to_all x1, starting transfers between devices, on_device(): partial = lax.all_to_all(partial, SEQ, 0, 0, tiled=True)  7.78 us
    all_to_all x1, starting transfers between devices, on_device(): last = lax.all_to_all(pack(partial, keyed[5]), 'dp', 0, 0, tiled=True)  7.67 us
    pallas_call x1, Pallas kernels, key_grads(): pl.pallas_call(key_kernel, in_specs=[SMEM] * 3 + [VMEM] * 8 + [HBM] * 3 +...  4.37 us
    all_to_all x1, waiting for transfers between devices, on_device(): last = lax.all_to_all(pack(partial, keyed[5]), 'dp', 0, 0, tiled=True)  4.26 us
  transfers between devices with their start and end apart: 35, of which 14 were waited for; matrix products, arithmetic and copies ran while one was open for 0% of the time, Pallas kernels for 20%

profile of v2, /device:TPU:1, one launch (start us, length us, event | category | flops | bytes accessed | tf_op | source)
XLA Modules:
  0.0 130.1 jit_solution(4973351412401966981)
XLA Ops:
  0.7 3.4 %project.1 = (bf16[128,1024]{1,0:T(8,128)(2,1)}, bf16[128,384]{1,0:T(8,128)(2,1)}, bf16[128,384]{1,0:T(8,128)(2,1)}, bf16[128,384]{1,0:T(8,128)(2,1)}, bf16[128,384]{1,0:T(8,128)(2,1)}) custom-call(bf16[128,1024]{1,0:T(8,128)(2,1)} %bitcast.10, bf16[1024,2048]{1,0:T(8,128)(2,1)} %w_ref.1), custom_call_target="tpu_custom_call" | custom-call | flops 3449999872 | tf_op jit(solution)/shard_map/project/pallas_call | solution.py:123
  4.0 2.1 %collective-permute-start = (bf16[128,384]{1,0:T(8,128)(2,1)}, bf16[128,384]{1,0:T(8,128)(2,1)S(1)}, u32[]{:S(2)}, u32[]{:S(2)}) collective-permute-start(bf16[128,384]{1,0:T(8,128)(2,1)} %get-tuple-element.75), channel_id=1, source_target_pairs={{0,8},{8,16},{16,24},{24,0},{1,9},{9,17},{17,25},{25,1},{2,10},{10... | collective-permute-start | bytes 294920 | tf_op jit(solution)/shard_map/ppermute | solution.py:821
  6.1 2.5 %collective-permute-start.1 = (bf16[128,384]{1,0:T(8,128)(2,1)}, bf16[128,384]{1,0:T(8,128)(2,1)S(1)}, u32[]{:S(2)}, u32[]{:S(2)}) collective-permute-start(bf16[128,384]{1,0:T(8,128)(2,1)} %get-tuple-element.76), channel_id=1, source_target_pairs={{0,16},{8,24},{16,0},{24,8},{1,17},{9,25},{17,1},{25,9},{2,18},{10... | collective-permute-start | bytes 294920 | tf_op jit(solution)/shard_map/ppermute | solution.py:821
  8.6 1.1 collective-permute-start.2
  9.8 3.1 %collective-permute-done.1.refs_2_ = bf16[128,384]{1,0:T(8,128)(2,1)S(1)} collective-permute-done((bf16[128,384]{1,0:T(8,128)(2,1)}, bf16[128,384]{1,0:T(8,128)(2,1)S(1)}, u32[]{:S(2)}, u32[]{:S(2)}) %collective-permute-start.1) | collective-permute-done | bytes 98336 | tf_op jit(solution)/shard_map/ppermute | solution.py:821
  12.8 0.9 copy-done.7
  13.8 1.4 %collective-permute-start.3 = (bf16[4,128,384]{2,1,0:T(8,128)(2,1)S(1)}, bf16[4,128,384]{2,1,0:T(8,128)(2,1)S(1)}, u32[]{:S(2)}, u32[]{:S(2)}) collective-permute-start(bf16[4,128,384]{2,1,0:T(8,128)(2,1)S(1)} %join.1.refs_0_), channel_id=1, source_target_pairs={{0,2},{2,4},{4,6},{6,0},{1,3},{3,5},{5,7},{7,1},{8,10},{10,12},{12... | collective-permute-start | bytes 1179656 | tf_op jit(solution)/shard_map/ppermute | solution.py:821
  15.2 1.5 %collective-permute-start.4 = (bf16[4,128,384]{2,1,0:T(8,128)(2,1)S(1)}, bf16[4,128,384]{2,1,0:T(8,128)(2,1)S(1)}, u32[]{:S(2)}, u32[]{:S(2)}) collective-permute-start(bf16[4,128,384]{2,1,0:T(8,128)(2,1)S(1)} %join.1.refs_0_), channel_id=1, source_target_pairs={{0,6},{2,0},{4,2},{6,4},{1,7},{3,1},{5,3},{7,5},{8,14},{10,8},{12,... | collective-permute-start | bytes 1179656 | tf_op jit(solution)/shard_map/ppermute | solution.py:821
  16.7 0.8 collective-permute-start.7
  17.5 1.9 %collective-permute-start.8 = (bf16[128,1024]{1,0:T(8,128)(2,1)}, bf16[128,1024]{1,0:T(8,128)(2,1)S(1)}, u32[]{:S(2)}, u32[]{:S(2)}) collective-permute-start(bf16[128,1024]{1,0:T(8,128)(2,1)} %get-tuple-element.105.n0.normed_ref), channel_id=1, source_target_pairs={{0,24},{8,0},{16,8},{24,16},{1,25},{9,1},{17,9},{25,17},{2,26},{10... | collective-permute-start | bytes 786440 | tf_op jit(solution)/shard_map/ppermute | solution.py:821
  19.4 3.4 %collective-permute-start.9 = (bf16[4,128,384]{2,1,0:T(8,128)(2,1)S(1)}, bf16[4,128,384]{2,1,0:T(8,128)(2,1)S(1)}, u32[]{:S(2)}, u32[]{:S(2)}) collective-permute-start(bf16[4,128,384]{2,1,0:T(8,128)(2,1)S(1)} %join.1.refs_0_), channel_id=1, source_target_pairs={{0,1},{1,0},{2,3},{3,2},{4,5},{5,4},{6,7},{7,6},{8,9},{9,8},{10,11... | collective-permute-start | bytes 1179656 | tf_op jit(solution)/shard_map/ppermute | solution.py:825
  22.8 0.6 collective-permute-done.3.back.refs_1_
  23.4 3.3 %collective-permute-start.10 = (bf16[4,128,384]{2,1,0:T(8,128)(2,1)S(1)}, bf16[4,128,384]{2,1,0:T(8,128)(2,1)S(1)}, u32[]{:S(2)}, u32[]{:S(2)}) collective-permute-start(bf16[4,128,384]{2,1,0:T(8,128)(2,1)S(1)} %collective-permute-done.3.back.refs_1_), channel_id=1, source_target_pairs={{0,1},{1,0},{2,3},{3,2},{4,5},{5,4},{6,7},{7,6},{8,9},{9,8},{10,11... | collective-permute-start | bytes 1179656 | tf_op jit(solution)/shard_map/ppermute | solution.py:825
  26.7 0.8 halves.1
  27.5 1.3 collective-permute-start.5
  28.8 1.5 %collective-permute-start.6 = (bf16[2,128,384]{2,1,0:T(8,128)(2,1)}, bf16[2,128,384]{2,1,0:T(8,128)(2,1)S(1)}, u32[]{:S(2)}, u32[]{:S(2)}) collective-permute-start(bf16[2,128,384]{2,1,0:T(8,128)(2,1)} %get-tuple-element.79), channel_id=1, source_target_pairs={{0,6},{2,0},{4,2},{6,4},{1,7},{3,1},{5,3},{7,5},{8,14},{10,8},{12,... | collective-permute-start | bytes 589832 | tf_op jit(solution)/shard_map/ppermute | solution.py:821
  30.4 2.4 %collective-permute-start.17 = (bf16[128,1024]{1,0:T(8,128)(2,1)S(1)}, bf16[128,1024]{1,0:T(8,128)(2,1)S(1)}, u32[]{:S(2)}, u32[]{:S(2)}) collective-permute-start(bf16[128,1024]{1,0:T(8,128)(2,1)S(1)} %copy-done.2), channel_id=1, source_target_pairs={{0,16},{8,24},{16,0},{24,8},{1,17},{9,25},{17,1},{25,9},{2,18},{10... | collective-permute-start | bytes 786440 | tf_op jit(solution)/shard_map/ppermute | solution.py:821
  32.9 3.5 %attend_near.1 = (f32[4,128,128]{2,1,0:T(8,128)S(1)}, bf16[4096,128]{1,0:T(8,128)(2,1)S(1)}, bf16[4096,128]{1,0:T(8,128)(2,1)S(1)}, bf16[4096,128]{1,0:T(8,128)(2,1)S(1)}) custom-call(s32[3]{0:T(128)S(1)} %pad_add_fusion.idx, s32[8]{0:T(128)S(1)} %bitcast.15, s32[8]{0:T(128)S(1)} %bitcast.20, bf16[4,128,384]{2,1,0:T(8,128)(2,1)S(1)} %join.1.refs_0_, ...), custom_call_target="tpu_custom_call" | custom-call | flops 575000000 | tf_op jit(solution)/shard_map/attend_near/pallas_call | solution.py:292
  36.4 1.5 %collective-permute-start.12 = (bf16[2,128,384]{2,1,0:T(8,128)(2,1)S(1)}, bf16[2,128,384]{2,1,0:T(8,128)(2,1)S(1)}, u32[]{:S(2)}, u32[]{:S(2)}) collective-permute-start(bf16[2,128,384]{2,1,0:T(8,128)(2,1)S(1)} %collective-permute-done.5.refs_1_), channel_id=1, source_target_pairs={{0,1},{1,0},{2,3},{3,2},{4,5},{5,4},{6,7},{7,6},{8,9},{9,8},{10,11... | collective-permute-start | bytes 589832 | tf_op jit(solution)/shard_map/ppermute | solution.py:825
  37.8 0.1 collective-permute-start.13
  37.9 1.0 collective-permute-done.12.refs_3_
  38.9 0.4 collective-permute-done.13.refs_4_
  39.3 2.8 %attend_far.1 = (f32[128,128]{1,0:T(8,128)S(1)}, f32[128,128]{1,0:T(8,128)S(1)}, f32[128,128]{1,0:T(8,128)S(1)}, f32[128,128]{1,0:T(8,128)S(1)}, bf16[4096,128]{...) custom-call(s32[3]{0:T(128)S(1)} %pad_add_fusion.idx, ...), custom_call_target="tpu_custom_call", output_to_operand_aliasing={{4}: (9, {}), {5}: (10, {}), {6}: (11, {})} | custom-call | flops 575000000 | tf_op jit(solution)/shard_map/attend_far/pallas_call | solution.py:348
  42.1 1.0 collective-permute-start.14
  43.0 1.5 %collective-permute-start.15 = (f32[128,128]{1,0:T(8,128)S(1)}, f32[128,128]{1,0:T(8,128)S(1)}, u32[]{:S(2)}, u32[]{:S(2)}) collective-permute-start(f32[128,128]{1,0:T(8,128)S(1)} %get-tuple-element.94), channel_id=1, source_target_pairs={{0,16},{8,24},{16,0},{24,8},{1,17},{9,25},{17,1},{25,9},{2,18},{10... | collective-permute-start | bytes 196616 | tf_op jit(solution)/shard_map/ppermute | solution.py:821
  44.6 0.5 gates.1
  45.2 2.1 %slopes.1.refs_11_ = f32[4,128,384]{2,1,0:T(8,128)S(1)} custom-call(s32[3]{0:T(128)S(1)} %pad_add_fusion.idx, bf16[128,1024]{1,0:T(8,128)(2,1)S(1)} %copy-done.2, bf16[128,1024]{1,0:T(8,128)(2,1)S(1)} %collective-permute-done.7.n1, bf16[128,1024]{1,0:T(8,128)(2,1)S(1)} %collective-permute-done.17.n2, bf16[128,1024]{1,0:T(8,128)(2,1)S(1)} %collective-permute-done.8.n3, ...), custom_call_target="tpu_custom_call" | custom-call | flops 575000000 | tf_op jit(solution)/shard_map/slopes/pallas_call | solution.py:177
  47.3 0.4 collective-permute-done.15.a2
  47.7 1.9 %collective-permute-done.16.a3 = f32[128,128]{1,0:T(8,128)S(1)} collective-permute-done((f32[128,128]{1,0:T(8,128)S(1)}, f32[128,128]{1,0:T(8,128)S(1)}, u32[]{:S(2)}, u32[]{:S(2)}) %collective-permute-start.16) | collective-permute-done | bytes 65568 | tf_op jit(solution)/shard_map/ppermute | solution.py:821
  49.6 2.0 %middle.1 = (bf16[144,256]{1,0:T(8,128)(2,1)S(1)}, bf16[144,256]{1,0:T(8,128)(2,1)S(1)}, bf16[144,256]{1,0:T(8,128)(2,1)S(1)}, bf16[144,256]{1,0:T(8,128)(2,1)S(...) custom-call(s32[3]{0:T(128)S(1)} %pad_add_fusion.idx, ...), custom_call_target="tpu_custom_call" | custom-call | flops 575000000 | tf_op jit(solution)/shard_map/middle/pallas_call | solution.py:429
  51.6 0.1 collective-permute-start.18
  51.6 1.7 %collective-permute-start.19 = (bf16[144,256]{1,0:T(8,128)(2,1)S(1)}, bf16[144,256]{1,0:T(8,128)(2,1)S(1)}, u32[]{:S(2)}, u32[]{:S(2)}) collective-permute-start(bf16[144,256]{1,0:T(8,128)(2,1)S(1)} %get-tuple-element.110), channel_id=1, source_target_pairs={{0,16},{8,24},{16,0},{24,8},{1,17},{9,25},{17,1},{25,9},{2,18},{10... | collective-permute-start | bytes 221192 | tf_op jit(solution)/shard_map/ppermute | solution.py:821
  53.3 1.9 %collective-permute-start.20 = (bf16[144,256]{1,0:T(8,128)(2,1)S(1)}, bf16[144,256]{1,0:T(8,128)(2,1)S(1)}, u32[]{:S(2)}, u32[]{:S(2)}) collective-permute-start(bf16[144,256]{1,0:T(8,128)(2,1)S(1)} %get-tuple-element.111), channel_id=1, source_target_pairs={{0,24},{8,0},{16,8},{24,16},{1,25},{9,1},{17,9},{25,17},{2,26},{10... | collective-permute-start | bytes 221192 | tf_op jit(solution)/shard_map/ppermute | solution.py:821
  55.2 1.4 %collective-permute-done.18.d1.refs_2_.refs_17_ = bf16[144,256]{1,0:T(8,128)(2,1)S(1)} collective-permute-done((bf16[144,256]{1,0:T(8,128)(2,1)S(1)}, bf16[144,256]{1,0:T(8,128)(2,1)S(1)}, u32[]{:S(2)}, u32[]{:S(2)}) %collective-permute-start.18) | collective-permute-done | bytes 73760 | tf_op jit(solution)/shard_map/ppermute | solution.py:821
  56.6 0.4 collective-permute-done.19.d2.refs_3_.refs_18_
  57.0 0.7 collective-permute-done.20.d3.refs_4_.refs_19_
  57.7 0.6 collective-permute-start.21
  58.3 1.8 %collective-permute-start.22 = (bf16[544,128]{1,0:T(8,128)(2,1)S(1)}, bf16[544,128]{1,0:T(8,128)(2,1)S(1)}, u32[]{:S(2)}, u32[]{:S(2)}) collective-permute-start(bf16[544,128]{1,0:T(8,128)(2,1)S(1)} %own_rows.1.refs_0_), channel_id=1, source_target_pairs={{0,4},{2,6},{4,0},{6,2},{1,5},{3,7},{5,1},{7,3},{8,12},{10,14},{12... | collective-permute-start | bytes 417800 | tf_op jit(solution)/shard_map/ppermute | solution.py:821
  60.2 2.0 %collective-permute-start.23 = (bf16[544,128]{1,0:T(8,128)(2,1)S(1)}, bf16[544,128]{1,0:T(8,128)(2,1)S(1)}, u32[]{:S(2)}, u32[]{:S(2)}) collective-permute-start(bf16[544,128]{1,0:T(8,128)(2,1)S(1)} %own_rows.1.refs_0_), channel_id=1, source_target_pairs={{0,6},{2,0},{4,2},{6,4},{1,7},{3,1},{5,3},{7,5},{8,14},{10,8},{12,... | collective-permute-start | bytes 417800 | tf_op jit(solution)/shard_map/ppermute | solution.py:821
  62.1 3.2 %collective-permute-start.24 = (bf16[544,128]{1,0:T(8,128)(2,1)S(1)}, bf16[544,128]{1,0:T(8,128)(2,1)S(1)}, u32[]{:S(2)}, u32[]{:S(2)}) collective-permute-start(bf16[544,128]{1,0:T(8,128)(2,1)S(1)} %own_rows.1.refs_0_), channel_id=1, source_target_pairs={{0,1},{1,0},{2,3},{3,2},{4,5},{5,4},{6,7},{7,6},{8,9},{9,8},{10,11... | collective-permute-start | bytes 417800 | tf_op jit(solution)/shard_map/ppermute | solution.py:825
  65.3 4.2 %query_grads.1 = (f32[128,128]{1,0:T(8,128)S(1)}, f32[128,128]{1,0:T(8,128)S(1)}, f32[128,128]{1,0:T(8,128)S(1)}, f32[128,128]{1,0:T(8,128)S(1)}) custom-call(s32[3]{0:T(128)S(1)} %pad_add_fusion.idx, s32[8]{0:T(128)S(1)} %bitcast.18, s32[8]{0:T(128)S(1)} %bitcast.23, bf16[4,128,384]{2,1,0:T(8,128)(2,1)S(1)} %join.1.refs_0_, ...), custom_call_target="tpu_custom_call" | custom-call | flops 3449999872 | tf_op jit(solution)/shard_map/query_grads/pallas_call | solution.py:476
  69.5 0.6 collective-permute-start.25
  70.1 0.1 collective-permute-start.26
  70.2 0.4 collective-permute-start.27
  70.6 0.5 collective-permute-done.25.refs_5_
  71.1 0.4 collective-permute-done.26.refs_6_
  71.5 0.2 collective-permute-done.27.refs_7_
  71.7 4.4 %key_grads.1 = (bf16[128,384]{1,0:T(8,128)(2,1)S(1)}, bf16[128,384]{1,0:T(8,128)(2,1)S(1)}, bf16[128,384]{1,0:T(8,128)(2,1)S(1)}, bf16[128,384]{1,0:T(8,128)(2,1...) custom-call(s32[3]{0:T(128)S(1)} %pad_add_fusion.idx, s32[8]{0:T(128)S(1)} %bitcast.19, s32[8]{0:T(128)S(1)} %bitcast.24, ...), custom_call_target="tpu_custom_call" | custom-call | flops 23000000 | tf_op jit(solution)/shard_map/key_grads/pallas_call | solution.py:556
  76.0 1.0 weights.2
  77.1 0.4 collective-permute-start.28
  77.5 1.0 weights.3.keep
  78.5 1.1 parts.1.early
  79.6 1.3 merge.1
  80.9 7.8 %all-to-all-start = ((bf16[32,80,256]{2,1,0:T(8,128)(2,1)}), bf16[32,80,256]{2,1,0:T(8,128)(2,1)S(1)}, u32[]{:S(2)}, u32[]{:S(2)}) async-start(bf16[32,80,256]{2,1,0:T(8,128)(2,1)} %merge.1), calls=%async_computation | async-start | bytes 2621440 | tf_op jit(solution)/shard_map/all_to_all | solution.py:886
  88.7 2.7 %collective-permute-start.30 = (bf16[128,384]{1,0:T(8,128)(2,1)S(1)}, bf16[128,384]{1,0:T(8,128)(2,1)S(1)}, u32[]{:S(2)}, u32[]{:S(2)}) collective-permute-start(bf16[128,384]{1,0:T(8,128)(2,1)S(1)} %get-tuple-element.132), channel_id=1, source_target_pairs={{0,24},{8,0},{16,8},{24,16},{1,25},{9,1},{17,9},{25,17},{2,26},{10... | collective-permute-start | bytes 294920 | tf_op jit(solution)/shard_map/ppermute | solution.py:821
  91.4 0.5 collective-permute-start.31
  91.9 0.6 collective-permute-start.32
  92.5 18.1 %all-to-all-done.ref = bf16[32,80,256]{2,1,0:T(8,128)(2,1)S(1)} async-done(((bf16[32,80,256]{2,1,0:T(8,128)(2,1)}), bf16[32,80,256]{2,1,0:T(8,128)(2,1)S(1)}, u32[]{:S(2)}, u32[]{:S(2)}) %all-to-all-start) | async-done | bytes 1310752 | tf_op jit(solution)/shard_map/all_to_all | solution.py:886
  110.6 0.9 pack.1
  111.5 7.7 %all-to-all-start.1 = ((bf16[8,96,128]{2,1,0:T(8,128)(2,1)}), bf16[8,96,128]{2,1,0:T(8,128)(2,1)S(1)}, u32[]{:S(2)}, u32[]{:S(2)}) async-start(bf16[8,96,128]{2,1,0:T(8,128)(2,1)} %pack.1), calls=%async_computation.1 | async-start | bytes 393216 | tf_op jit(solution)/shard_map/all_to_all | solution.py:889
  119.2 2.2 %copy-done.1 = bf16[1024,2048]{1,0:T(8,128)(2,1)S(1)} copy-done((bf16[1024,2048]{1,0:T(8,128)(2,1)S(1)}, bf16[1024,2048]{1,0:T(8,128)(2,1)}, u32[]{:S(2)}) %copy-start.1) | copy-done | bytes 4194328
  121.4 3.8 %input_grads.1 = bf16[128,1024]{1,0:T(8,128)(2,1)} custom-call(s32[3]{0:T(128)S(1)} %pad_add_fusion.idx, bf16[128,384]{1,0:T(8,128)(2,1)S(1)} %get-tuple-element.131.b0, bf16[128,384]{1,0:T(8,128)(2,1)S(1)} %collective-permute-done.30.b1, bf16[128,384]{1,0:T(8,128)(2,1)S(1)} %collective-permute-done.31.b2, bf16[128,384]{1,0:T(8,128)(2,1)S(1)} %collective-permute-done.32.b3, ...), custom_call_target="tpu_custom_call" | custom-call | flops 4600000000 | tf_op jit(solution)/shard_map/input_grads/pallas_call | solution.py:742
  125.2 4.3 %all-to-all-done.1.ref = bf16[8,96,128]{2,1,0:T(8,128)(2,1)S(1)} async-done(((bf16[8,96,128]{2,1,0:T(8,128)(2,1)}), bf16[8,96,128]{2,1,0:T(8,128)(2,1)S(1)}, u32[]{:S(2)}, u32[]{:S(2)}) %all-to-all-start.1) | async-done | bytes 196640 | tf_op jit(solution)/shard_map/all_to_all | solution.py:889
  129.4 0.7 last_sum.1
  (49 shorter events, 0.3 us)
Async XLA Ops:
  0.6 32.2 %copy-start.8 = (s32[1,8]{1,0:T(1,128)S(1)}, s32[1,8]{1,0:T(1,128)}, u32[]{:S(2)}) copy-start(s32[1,8]{1,0:T(1,128)} %param.10) | copy-start | bytes 100
  0.6 32.2 %copy-start.9 = (s32[1,8]{1,0:T(1,128)S(1)}, s32[1,8]{1,0:T(1,128)}, u32[]{:S(2)}) copy-start(s32[1,8]{1,0:T(1,128)} %param.11) | copy-start | bytes 100
  4.0 26.4 %copy-start.2 = (bf16[128,1024]{1,0:T(8,128)(2,1)S(1)}, bf16[128,1024]{1,0:T(8,128)(2,1)}, u32[]{:S(2)}) copy-start(bf16[128,1024]{1,0:T(8,128)(2,1)} %get-tuple-element.105.n0.normed_ref) | copy-start | bytes 786436
  4.0 5.7 %collective-permute-start = (bf16[128,384]{1,0:T(8,128)(2,1)}, bf16[128,384]{1,0:T(8,128)(2,1)S(1)}, u32[]{:S(2)}, u32[]{:S(2)}) collective-permute-start(bf16[128,384]{1,0:T(8,128)(2,1)} %get-tuple-element.75), channel_id=1, source_target_pairs={{0,8},{8,16},{16,24},{24,0},{1,9},{9,17},{17,25},{25,1},{2,10},{10... | collective-permute-start | bytes 294920 | tf_op jit(solution)/shard_map/ppermute | solution.py:821
  6.1 6.7 %collective-permute-start.1 = (bf16[128,384]{1,0:T(8,128)(2,1)}, bf16[128,384]{1,0:T(8,128)(2,1)S(1)}, u32[]{:S(2)}, u32[]{:S(2)}) collective-permute-start(bf16[128,384]{1,0:T(8,128)(2,1)} %get-tuple-element.76), channel_id=1, source_target_pairs={{0,16},{8,24},{16,0},{24,8},{1,17},{9,25},{17,1},{25,9},{2,18},{10... | collective-permute-start | bytes 294920 | tf_op jit(solution)/shard_map/ppermute | solution.py:821
  8.6 4.2 %collective-permute-start.2 = (bf16[128,384]{1,0:T(8,128)(2,1)}, bf16[128,384]{1,0:T(8,128)(2,1)S(1)}, u32[]{:S(2)}, u32[]{:S(2)}) collective-permute-start(bf16[128,384]{1,0:T(8,128)(2,1)} %get-tuple-element.77), channel_id=1, source_target_pairs={{0,24},{8,0},{16,8},{24,16},{1,25},{9,1},{17,9},{25,17},{2,26},{10... | collective-permute-start | bytes 294920 | tf_op jit(solution)/shard_map/ppermute | solution.py:821
  12.8 0.9 copy-start.7
  13.8 9.6 %collective-permute-start.3 = (bf16[4,128,384]{2,1,0:T(8,128)(2,1)S(1)}, bf16[4,128,384]{2,1,0:T(8,128)(2,1)S(1)}, u32[]{:S(2)}, u32[]{:S(2)}) collective-permute-start(bf16[4,128,384]{2,1,0:T(8,128)(2,1)S(1)} %join.1.refs_0_), channel_id=1, source_target_pairs={{0,2},{2,4},{4,6},{6,0},{1,3},{3,5},{5,7},{7,1},{8,10},{10,12},{12... | collective-permute-start | bytes 1179656 | tf_op jit(solution)/shard_map/ppermute | solution.py:821
  15.2 11.5 %collective-permute-start.4 = (bf16[4,128,384]{2,1,0:T(8,128)(2,1)S(1)}, bf16[4,128,384]{2,1,0:T(8,128)(2,1)S(1)}, u32[]{:S(2)}, u32[]{:S(2)}) collective-permute-start(bf16[4,128,384]{2,1,0:T(8,128)(2,1)S(1)} %join.1.refs_0_), channel_id=1, source_target_pairs={{0,6},{2,0},{4,2},{6,4},{1,7},{3,1},{5,3},{7,5},{8,14},{10,8},{12,... | collective-permute-start | bytes 1179656 | tf_op jit(solution)/shard_map/ppermute | solution.py:821
  16.7 10.8 %collective-permute-start.7 = (bf16[128,1024]{1,0:T(8,128)(2,1)}, bf16[128,1024]{1,0:T(8,128)(2,1)S(1)}, u32[]{:S(2)}, u32[]{:S(2)}) collective-permute-start(bf16[128,1024]{1,0:T(8,128)(2,1)} %get-tuple-element.105.n0.normed_ref), channel_id=1, source_target_pairs={{0,8},{8,16},{16,24},{24,0},{1,9},{9,17},{17,25},{25,1},{2,10},{10... | collective-permute-start | bytes 786440 | tf_op jit(solution)/shard_map/ppermute | solution.py:821
  17.5 11.3 %collective-permute-start.8 = (bf16[128,1024]{1,0:T(8,128)(2,1)}, bf16[128,1024]{1,0:T(8,128)(2,1)S(1)}, u32[]{:S(2)}, u32[]{:S(2)}) collective-permute-start(bf16[128,1024]{1,0:T(8,128)(2,1)} %get-tuple-element.105.n0.normed_ref), channel_id=1, source_target_pairs={{0,24},{8,0},{16,8},{24,16},{1,25},{9,1},{17,9},{25,17},{2,26},{10... | collective-permute-start | bytes 786440 | tf_op jit(solution)/shard_map/ppermute | solution.py:821
  19.4 11.0 %collective-permute-start.9 = (bf16[4,128,384]{2,1,0:T(8,128)(2,1)S(1)}, bf16[4,128,384]{2,1,0:T(8,128)(2,1)S(1)}, u32[]{:S(2)}, u32[]{:S(2)}) collective-permute-start(bf16[4,128,384]{2,1,0:T(8,128)(2,1)S(1)} %join.1.refs_0_), channel_id=1, source_target_pairs={{0,1},{1,0},{2,3},{3,2},{4,5},{5,4},{6,7},{7,6},{8,9},{9,8},{10,11... | collective-permute-start | bytes 1179656 | tf_op jit(solution)/shard_map/ppermute | solution.py:825
  23.4 9.4 %collective-permute-start.10 = (bf16[4,128,384]{2,1,0:T(8,128)(2,1)S(1)}, bf16[4,128,384]{2,1,0:T(8,128)(2,1)S(1)}, u32[]{:S(2)}, u32[]{:S(2)}) collective-permute-start(bf16[4,128,384]{2,1,0:T(8,128)(2,1)S(1)} %collective-permute-done.3.back.refs_1_), channel_id=1, source_target_pairs={{0,1},{1,0},{2,3},{3,2},{4,5},{5,4},{6,7},{7,6},{8,9},{9,8},{10,11... | collective-permute-start | bytes 1179656 | tf_op jit(solution)/shard_map/ppermute | solution.py:825
  26.7 6.1 %collective-permute-start.11 = (bf16[4,128,384]{2,1,0:T(8,128)(2,1)S(1)}, bf16[4,128,384]{2,1,0:T(8,128)(2,1)S(1)}, u32[]{:S(2)}, u32[]{:S(2)}) collective-permute-start(bf16[4,128,384]{2,1,0:T(8,128)(2,1)S(1)} %collective-permute-done.4.ahead.refs_2_), channel_id=1, source_target_pairs={{0,1},{1,0},{2,3},{3,2},{4,5},{5,4},{6,7},{7,6},{8,9},{9,8},{10,11... | collective-permute-start | bytes 1179656 | tf_op jit(solution)/shard_map/ppermute | solution.py:825
  27.5 8.8 %collective-permute-start.5 = (bf16[2,128,384]{2,1,0:T(8,128)(2,1)}, bf16[2,128,384]{2,1,0:T(8,128)(2,1)S(1)}, u32[]{:S(2)}, u32[]{:S(2)}) collective-permute-start(bf16[2,128,384]{2,1,0:T(8,128)(2,1)} %get-tuple-element.78), channel_id=1, source_target_pairs={{0,2},{2,4},{4,6},{6,0},{1,3},{3,5},{5,7},{7,1},{8,10},{10,12},{12... | collective-permute-start | bytes 589832 | tf_op jit(solution)/shard_map/ppermute | solution.py:821
  28.8 7.5 %collective-permute-start.6 = (bf16[2,128,384]{2,1,0:T(8,128)(2,1)}, bf16[2,128,384]{2,1,0:T(8,128)(2,1)S(1)}, u32[]{:S(2)}, u32[]{:S(2)}) collective-permute-start(bf16[2,128,384]{2,1,0:T(8,128)(2,1)} %get-tuple-element.79), channel_id=1, source_target_pairs={{0,6},{2,0},{4,2},{6,4},{1,7},{3,1},{5,3},{7,5},{8,14},{10,8},{12,... | collective-permute-start | bytes 589832 | tf_op jit(solution)/shard_map/ppermute | solution.py:821
  30.4 14.1 %collective-permute-start.17 = (bf16[128,1024]{1,0:T(8,128)(2,1)S(1)}, bf16[128,1024]{1,0:T(8,128)(2,1)S(1)}, u32[]{:S(2)}, u32[]{:S(2)}) collective-permute-start(bf16[128,1024]{1,0:T(8,128)(2,1)S(1)} %copy-done.2), channel_id=1, source_target_pairs={{0,16},{8,24},{16,0},{24,8},{1,17},{9,25},{17,1},{25,9},{2,18},{10... | collective-permute-start | bytes 786440 | tf_op jit(solution)/shard_map/ppermute | solution.py:821
  36.4 8.2 %copy-start = (bf16[1024,2048]{1,0:T(8,128)(2,1)S(1)}, bf16[1024,2048]{1,0:T(8,128)(2,1)}, u32[]{:S(2)}) copy-start(bf16[1024,2048]{1,0:T(8,128)(2,1)} %w_ref.1) | copy-start | bytes 12582916
  36.4 2.5 %collective-permute-start.12 = (bf16[2,128,384]{2,1,0:T(8,128)(2,1)S(1)}, bf16[2,128,384]{2,1,0:T(8,128)(2,1)S(1)}, u32[]{:S(2)}, u32[]{:S(2)}) collective-permute-start(bf16[2,128,384]{2,1,0:T(8,128)(2,1)S(1)} %collective-permute-done.5.refs_1_), channel_id=1, source_target_pairs={{0,1},{1,0},{2,3},{3,2},{4,5},{5,4},{6,7},{7,6},{8,9},{9,8},{10,11... | collective-permute-start | bytes 589832 | tf_op jit(solution)/shard_map/ppermute | solution.py:825
  37.8 1.4 %collective-permute-start.13 = (bf16[2,128,384]{2,1,0:T(8,128)(2,1)S(1)}, bf16[2,128,384]{2,1,0:T(8,128)(2,1)S(1)}, u32[]{:S(2)}, u32[]{:S(2)}) collective-permute-start(bf16[2,128,384]{2,1,0:T(8,128)(2,1)S(1)} %collective-permute-done.6.refs_2_), channel_id=1, source_target_pairs={{0,1},{1,0},{2,3},{3,2},{4,5},{5,4},{6,7},{7,6},{8,9},{9,8},{10,11... | collective-permute-start | bytes 589832 | tf_op jit(solution)/shard_map/ppermute | solution.py:825
  42.1 5.2 %collective-permute-start.14 = (f32[128,128]{1,0:T(8,128)S(1)}, f32[128,128]{1,0:T(8,128)S(1)}, u32[]{:S(2)}, u32[]{:S(2)}) collective-permute-start(f32[128,128]{1,0:T(8,128)S(1)} %get-tuple-element.93), channel_id=1, source_target_pairs={{0,24},{8,0},{16,8},{24,16},{1,25},{9,1},{17,9},{25,17},{2,26},{10... | collective-permute-start | bytes 196616 | tf_op jit(solution)/shard_map/ppermute | solution.py:821
  43.0 4.6 %collective-permute-start.15 = (f32[128,128]{1,0:T(8,128)S(1)}, f32[128,128]{1,0:T(8,128)S(1)}, u32[]{:S(2)}, u32[]{:S(2)}) collective-permute-start(f32[128,128]{1,0:T(8,128)S(1)} %get-tuple-element.94), channel_id=1, source_target_pairs={{0,16},{8,24},{16,0},{24,8},{1,17},{9,25},{17,1},{25,9},{2,18},{10... | collective-permute-start | bytes 196616 | tf_op jit(solution)/shard_map/ppermute | solution.py:821
  44.5 5.0 %collective-permute-start.16 = (f32[128,128]{1,0:T(8,128)S(1)}, f32[128,128]{1,0:T(8,128)S(1)}, u32[]{:S(2)}, u32[]{:S(2)}) collective-permute-start(f32[128,128]{1,0:T(8,128)S(1)} %get-tuple-element.95), channel_id=1, source_target_pairs={{0,8},{8,16},{16,24},{24,0},{1,9},{9,17},{17,25},{25,1},{2,10},{10... | collective-permute-start | bytes 196616 | tf_op jit(solution)/shard_map/ppermute | solution.py:821
  45.1 4.4 %copy-start.3 = (bf16[512,1024]{1,0:T(8,128)(2,1)S(1)}, bf16[512,1024]{1,0:T(8,128)(2,1)}, u32[]{:S(2)}) copy-start(bf16[512,1024]{1,0:T(8,128)(2,1)} %w_out.1) | copy-start | bytes 3145732
  45.1 4.4 %copy-start.4 = (bf16[1024,256]{1,0:T(8,128)(2,1)S(1)}, bf16[1024,256]{1,0:T(8,128)(2,1)}, u32[]{:S(2)}) copy-start(bf16[1024,256]{1,0:T(8,128)(2,1)} %w_score.3) | copy-start | bytes 1572868
  45.1 4.4 %copy-start.5 = (bf16[1,128,1024]{2,1,0:T(8,128)(2,1)S(1)}, bf16[1,128,1024]{2,1,0:T(8,128)(2,1)}, u32[]{:S(2)}) copy-start(bf16[1,128,1024]{2,1,0:T(8,128)(2,1)} %param.9) | copy-start | bytes 786436
  45.1 4.4 %copy-start.6 = (bf16[1,128,1024]{2,1,0:T(8,128)(2,1)S(1)}, bf16[1,128,1024]{2,1,0:T(8,128)(2,1)}, u32[]{:S(2)}) copy-start(bf16[1,128,1024]{2,1,0:T(8,128)(2,1)} %param.16) | copy-start | bytes 786436
  45.1 4.4 %copy-start.10 = (f32[256]{0:T(256)S(1)}, f32[256]{0:T(256)}, u32[]{:S(2)}) copy-start(f32[256]{0:T(256)} %param.15) | copy-start | bytes 3076
  45.2 4.4 %copy-start.11 = (f32[1,128]{1,0:T(1,128)S(1)}, f32[1,128]{1,0:T(1,128)}, u32[]{:S(2)}) copy-start(f32[1,128]{1,0:T(1,128)} %score.1) | copy-start | bytes 1540
  51.6 5.1 %collective-permute-start.18 = (bf16[144,256]{1,0:T(8,128)(2,1)S(1)}, bf16[144,256]{1,0:T(8,128)(2,1)S(1)}, u32[]{:S(2)}, u32[]{:S(2)}) collective-permute-start(bf16[144,256]{1,0:T(8,128)(2,1)S(1)} %get-tuple-element.109), channel_id=1, source_target_pairs={{0,8},{8,16},{16,24},{24,0},{1,9},{9,17},{17,25},{25,1},{2,10},{10... | collective-permute-start | bytes 221192 | tf_op jit(solution)/shard_map/ppermute | solution.py:821
  51.6 5.4 %collective-permute-start.19 = (bf16[144,256]{1,0:T(8,128)(2,1)S(1)}, bf16[144,256]{1,0:T(8,128)(2,1)S(1)}, u32[]{:S(2)}, u32[]{:S(2)}) collective-permute-start(bf16[144,256]{1,0:T(8,128)(2,1)S(1)} %get-tuple-element.110), channel_id=1, source_target_pairs={{0,16},{8,24},{16,0},{24,8},{1,17},{9,25},{17,1},{25,9},{2,18},{10... | collective-permute-start | bytes 221192 | tf_op jit(solution)/shard_map/ppermute | solution.py:821
  53.3 4.4 %collective-permute-start.20 = (bf16[144,256]{1,0:T(8,128)(2,1)S(1)}, bf16[144,256]{1,0:T(8,128)(2,1)S(1)}, u32[]{:S(2)}, u32[]{:S(2)}) collective-permute-start(bf16[144,256]{1,0:T(8,128)(2,1)S(1)} %get-tuple-element.111), channel_id=1, source_target_pairs={{0,24},{8,0},{16,8},{24,16},{1,25},{9,1},{17,9},{25,17},{2,26},{10... | collective-permute-start | bytes 221192 | tf_op jit(solution)/shard_map/ppermute | solution.py:821
  57.7 11.7 %collective-permute-start.21 = (bf16[544,128]{1,0:T(8,128)(2,1)S(1)}, bf16[544,128]{1,0:T(8,128)(2,1)S(1)}, u32[]{:S(2)}, u32[]{:S(2)}) collective-permute-start(bf16[544,128]{1,0:T(8,128)(2,1)S(1)} %own_rows.1.refs_0_), channel_id=1, source_target_pairs={{0,2},{2,4},{4,6},{6,0},{1,3},{3,5},{5,7},{7,1},{8,10},{10,12},{12... | collective-permute-start | bytes 417800 | tf_op jit(solution)/shard_map/ppermute | solution.py:821
  58.3 11.2 %collective-permute-start.22 = (bf16[544,128]{1,0:T(8,128)(2,1)S(1)}, bf16[544,128]{1,0:T(8,128)(2,1)S(1)}, u32[]{:S(2)}, u32[]{:S(2)}) collective-permute-start(bf16[544,128]{1,0:T(8,128)(2,1)S(1)} %own_rows.1.refs_0_), channel_id=1, source_target_pairs={{0,4},{2,6},{4,0},{6,2},{1,5},{3,7},{5,1},{7,3},{8,12},{10,14},{12... | collective-permute-start | bytes 417800 | tf_op jit(solution)/shard_map/ppermute | solution.py:821
  60.2 9.3 %collective-permute-start.23 = (bf16[544,128]{1,0:T(8,128)(2,1)S(1)}, bf16[544,128]{1,0:T(8,128)(2,1)S(1)}, u32[]{:S(2)}, u32[]{:S(2)}) collective-permute-start(bf16[544,128]{1,0:T(8,128)(2,1)S(1)} %own_rows.1.refs_0_), channel_id=1, source_target_pairs={{0,6},{2,0},{4,2},{6,4},{1,7},{3,1},{5,3},{7,5},{8,14},{10,8},{12,... | collective-permute-start | bytes 417800 | tf_op jit(solution)/shard_map/ppermute | solution.py:821
  62.1 8.5 %collective-permute-start.24 = (bf16[544,128]{1,0:T(8,128)(2,1)S(1)}, bf16[544,128]{1,0:T(8,128)(2,1)S(1)}, u32[]{:S(2)}, u32[]{:S(2)}) collective-permute-start(bf16[544,128]{1,0:T(8,128)(2,1)S(1)} %own_rows.1.refs_0_), channel_id=1, source_target_pairs={{0,1},{1,0},{2,3},{3,2},{4,5},{5,4},{6,7},{7,6},{8,9},{9,8},{10,11... | collective-permute-start | bytes 417800 | tf_op jit(solution)/shard_map/ppermute | solution.py:825
  65.3 13.2 %collective-permute-start.29 = (bf16[128,2816]{1,0:T(8,128)(2,1)S(1)}, bf16[128,2816]{1,0:T(8,128)(2,1)S(1)}, u32[]{:S(2)}, u32[]{:S(2)}) collective-permute-start(bf16[128,2816]{1,0:T(8,128)(2,1)S(1)} %get-tuple-element.130.own), channel_id=1, source_target_pairs={{0,1},{1,0},{2,3},{3,2},{4,5},{5,4},{6,7},{7,6},{8,9},{9,8},{10,11... | collective-permute-start | bytes 2162696 | tf_op jit(solution)/shard_map/ppermute | solution.py:825
  69.5 1.6 %collective-permute-start.25 = (bf16[544,128]{1,0:T(8,128)(2,1)S(1)}, bf16[544,128]{1,0:T(8,128)(2,1)S(1)}, u32[]{:S(2)}, u32[]{:S(2)}) collective-permute-start(bf16[544,128]{1,0:T(8,128)(2,1)S(1)} %collective-permute-done.21.refs_1_), channel_id=1, source_target_pairs={{0,1},{1,0},{2,3},{3,2},{4,5},{5,4},{6,7},{7,6},{8,9},{9,8},{10,11... | collective-permute-start | bytes 417800 | tf_op jit(solution)/shard_map/ppermute | solution.py:825
  70.1 1.4 %collective-permute-start.26 = (bf16[544,128]{1,0:T(8,128)(2,1)S(1)}, bf16[544,128]{1,0:T(8,128)(2,1)S(1)}, u32[]{:S(2)}, u32[]{:S(2)}) collective-permute-start(bf16[544,128]{1,0:T(8,128)(2,1)S(1)} %collective-permute-done.22.refs_2_), channel_id=1, source_target_pairs={{0,1},{1,0},{2,3},{3,2},{4,5},{5,4},{6,7},{7,6},{8,9},{9,8},{10,11... | collective-permute-start | bytes 417800 | tf_op jit(solution)/shard_map/ppermute | solution.py:825
  70.2 1.5 %collective-permute-start.27 = (bf16[544,128]{1,0:T(8,128)(2,1)S(1)}, bf16[544,128]{1,0:T(8,128)(2,1)S(1)}, u32[]{:S(2)}, u32[]{:S(2)}) collective-permute-start(bf16[544,128]{1,0:T(8,128)(2,1)S(1)} %collective-permute-done.23.refs_3_), channel_id=1, source_target_pairs={{0,1},{1,0},{2,3},{3,2},{4,5},{5,4},{6,7},{7,6},{8,9},{9,8},{10,11... | collective-permute-start | bytes 417800 | tf_op jit(solution)/shard_map/ppermute | solution.py:825
  77.1 2.5 %collective-permute-start.28 = (bf16[32,32,256]{2,1,0:T(8,128)(2,1)S(1)}, bf16[32,32,256]{2,1,0:T(8,128)(2,1)S(1)}, u32[]{:S(2)}, u32[]{:S(2)}) collective-permute-start(bf16[32,32,256]{2,1,0:T(8,128)(2,1)S(1)} %weights.2), channel_id=1, source_target_pairs={{0,1},{1,0},{2,3},{3,2},{4,5},{5,4},{6,7},{7,6},{8,9},{9,8},{10,11... | collective-permute-start | bytes 1572872 | tf_op jit(solution)/shard_map/ppermute | solution.py:825
  80.9 29.7 %all-to-all-start = ((bf16[32,80,256]{2,1,0:T(8,128)(2,1)}), bf16[32,80,256]{2,1,0:T(8,128)(2,1)S(1)}, u32[]{:S(2)}, u32[]{:S(2)}) async-start(bf16[32,80,256]{2,1,0:T(8,128)(2,1)} %merge.1), calls=%async_computation | async-start | bytes 2621440 | tf_op jit(solution)/shard_map/all_to_all | solution.py:886
  88.7 30.5 %collective-permute-start.30 = (bf16[128,384]{1,0:T(8,128)(2,1)S(1)}, bf16[128,384]{1,0:T(8,128)(2,1)S(1)}, u32[]{:S(2)}, u32[]{:S(2)}) collective-permute-start(bf16[128,384]{1,0:T(8,128)(2,1)S(1)} %get-tuple-element.132), channel_id=1, source_target_pairs={{0,24},{8,0},{16,8},{24,16},{1,25},{9,1},{17,9},{25,17},{2,26},{10... | collective-permute-start | bytes 294920 | tf_op jit(solution)/shard_map/ppermute | solution.py:821
  91.4 27.8 %collective-permute-start.31 = (bf16[128,384]{1,0:T(8,128)(2,1)S(1)}, bf16[128,384]{1,0:T(8,128)(2,1)S(1)}, u32[]{:S(2)}, u32[]{:S(2)}) collective-permute-start(bf16[128,384]{1,0:T(8,128)(2,1)S(1)} %get-tuple-element.133), channel_id=1, source_target_pairs={{0,16},{8,24},{16,0},{24,8},{1,17},{9,25},{17,1},{25,9},{2,18},{10... | collective-permute-start | bytes 294920 | tf_op jit(solution)/shard_map/ppermute | solution.py:821
  91.9 27.2 %collective-permute-start.32 = (bf16[128,384]{1,0:T(8,128)(2,1)S(1)}, bf16[128,384]{1,0:T(8,128)(2,1)S(1)}, u32[]{:S(2)}, u32[]{:S(2)}) collective-permute-start(bf16[128,384]{1,0:T(8,128)(2,1)S(1)} %get-tuple-element.134), channel_id=1, source_target_pairs={{0,8},{8,16},{16,24},{24,0},{1,9},{9,17},{17,25},{25,1},{2,10},{10... | collective-permute-start | bytes 294920 | tf_op jit(solution)/shard_map/ppermute | solution.py:821
  111.5 17.9 %all-to-all-start.1 = ((bf16[8,96,128]{2,1,0:T(8,128)(2,1)}), bf16[8,96,128]{2,1,0:T(8,128)(2,1)S(1)}, u32[]{:S(2)}, u32[]{:S(2)}) async-start(bf16[8,96,128]{2,1,0:T(8,128)(2,1)} %pack.1), calls=%async_computation.1 | async-start | bytes 393216 | tf_op jit(solution)/shard_map/all_to_all | solution.py:889
  119.2 2.2 %copy-start.1 = (bf16[1024,2048]{1,0:T(8,128)(2,1)S(1)}, bf16[1024,2048]{1,0:T(8,128)(2,1)}, u32[]{:S(2)}) copy-start(bf16[1024,2048]{1,0:T(8,128)(2,1)} %w_ref.1) | copy-start | bytes 12582916
